TPU v7x, 128 devices: a whole 4x4x4 slice. The times are simulated.
128 devices in a mesh: seq: 64 (over x_lo, z, y, core), rep: 2 (over x_hi).
Axes of the slice: x: 4 (x_hi: 2, x_lo: 2; x = x_hi * 2 + x_lo), y: 4, z: 4, core: 2. Of those that a mesh axis runs over, the one named last changes fastest.
Arguments:
- clip_tokens: bfloat16 [2, 64, 256, 1152], P('rep', 'seq'), may hold values from -6 to 6
- modulation: float32 [2, 6, 1152], P('rep'), may hold values from -1 to 1
- spatial_weights: bfloat16 [4608, 1152], replicated, may hold values from -2 to 2, as said below
- temporal_weights: bfloat16 [4608, 1152], replicated, may hold values from -2 to 2, as said below
- out_cotangent: bfloat16 [2, 64, 256, 1152], P('rep', 'seq'), may hold values from -4 to 4
Outputs:
- input_grad: bfloat16 [2, 64, 256, 1152], P('rep', 'seq')
- qkv_weight_grad: float32 [3456, 1152], P(('seq', 'rep'))
- proj_weight_grad: float32 [1152, 1152], P(('seq', 'rep'))
Inputs may be any that keep to these rules, and one draw needn't show every extreme that they name: `spatial_weights`: rows are the q, k, v and output projections (1152 rows each); each row multiplies a vector of 1152 features. `temporal_weights`: rows are the q, k, v and output projections (1152 rows each); each row multiplies a vector of 1152 features.
All inputs are finite; a program needn't handle non-finite values.
Results may differ from a plain program's by a relative error of at most 0.04.
Values may be sent and summed in bfloat16 or wider, within the bound.
No kernel may reach another device: no remote copies, remote signals or barrier semaphores. Data moves between devices by JAX's collectives and lax.ppermute only.
A program may use at most 128 MiB of HBM per device.

v0:
```python
import jax
import jax.numpy as jnp
from jax import lax
from jax.sharding import PartitionSpec as P

HEADS = 16


def normalize(tokens):
    values = tokens.astype(jnp.float32)
    center = values - jnp.mean(values, axis=-1, keepdims=True)
    spread = lax.rsqrt(jnp.mean(center * center, axis=-1, keepdims=True) + 1e-06)
    return (center * spread, spread)


def norm_back(grad_hidden, normed, spread, gain_term):
    grad_norm = grad_hidden * (1.0 + gain_term)
    centered = grad_norm - jnp.mean(grad_norm, axis=-1, keepdims=True)
    return spread * (centered - normed * jnp.mean(grad_norm * normed, axis=-1, keepdims=True))


def project(tokens, weight):
    flat_rows = tokens.reshape(-1, tokens.shape[-1])
    result = lax.dot_general(
        flat_rows, weight, (((1,), (1,)), ((), ())), preferred_element_type=jnp.float32
    )
    return result.reshape(tokens.shape[:-1] + (weight.shape[0],))


def project_back(gradient, weight):
    flat_rows = gradient.reshape(-1, gradient.shape[-1])
    result = jnp.dot(flat_rows, weight, preferred_element_type=jnp.float32)
    return result.reshape(gradient.shape[:-1] + (weight.shape[1],))


def split_heads(qkv, head_count):
    dim_one, dim_two, dim_three, triple = qkv.shape
    features = triple // 3
    pieces = qkv.reshape(dim_one, dim_two, dim_three, 3, head_count, features // head_count)
    return (pieces[:, :, :, 0], pieces[:, :, :, 1], pieces[:, :, :, 2])


def attend(qkv, head_count):
    query_rows, key_rows, value_rows = split_heads(qkv, head_count)
    factor = query_rows.shape[-1] ** (-0.5)
    scores = (
        jnp.einsum("albhe,ambhe->abhlm", query_rows, key_rows, preferred_element_type=jnp.float32)
        * factor
    )
    top_score = jnp.max(scores, axis=-1, keepdims=True)
    raw_weight = jnp.exp(scores - top_score)
    prob_rows = raw_weight / jnp.sum(raw_weight, axis=-1, keepdims=True)
    mixture = jnp.einsum(
        "abhlm,ambhe->albhe",
        prob_rows.astype(jnp.bfloat16),
        value_rows,
        preferred_element_type=jnp.float32,
    )
    shape_out = qkv.shape[:3] + (qkv.shape[3] // 3,)
    return (mixture.astype(jnp.bfloat16).reshape(shape_out), prob_rows)


def attend_back(qkv, prob_rows, grad_attn, head_count):
    query_rows, key_rows, value_rows = split_heads(qkv, head_count)
    factor = query_rows.shape[-1] ** (-0.5)
    grad_heads = grad_attn.reshape(query_rows.shape)
    grad_prob = jnp.einsum(
        "albhe,ambhe->abhlm", grad_heads, value_rows, preferred_element_type=jnp.float32
    )
    inner = jnp.sum(prob_rows * grad_prob, axis=-1, keepdims=True)
    grad_score = (prob_rows * (grad_prob - inner)).astype(jnp.bfloat16)
    grad_query = (
        jnp.einsum("abhlm,ambhe->albhe", grad_score, key_rows, preferred_element_type=jnp.float32)
        * factor
    ).astype(jnp.bfloat16)
    grad_key = (
        jnp.einsum("abhlm,albhe->ambhe", grad_score, query_rows, preferred_element_type=jnp.float32)
        * factor
    ).astype(jnp.bfloat16)
    prob_low = prob_rows.astype(jnp.bfloat16)
    grad_value = jnp.einsum(
        "abhlm,albhe->ambhe", prob_low, grad_heads, preferred_element_type=jnp.float32
    ).astype(jnp.bfloat16)
    stacked = jnp.stack([grad_query, grad_key, grad_value], axis=3)
    return stacked.reshape(qkv.shape)


def on_device(clip_tokens, modulation, spatial_weights, temporal_weights, out_cotangent):
    clip_count, frame_count, span, features = clip_tokens.shape
    seq_count = lax.axis_size("seq")
    place = span // seq_count
    all_frames = frame_count * seq_count
    modes = modulation[:, :, None, None, :]
    shift_s, scale_s, gate_s = (modes[:, 0], modes[:, 1], modes[:, 2])
    shift_t, scale_t, gate_t = (modes[:, 3], modes[:, 4], modes[:, 5])
    qkv_spatial = spatial_weights[: 3 * features]
    out_spatial = spatial_weights[3 * features :]
    qkv_temporal = temporal_weights[: 3 * features]
    out_temporal = temporal_weights[3 * features :]

    def position_rows(tokens, depth):
        return tokens.reshape(clip_count, frame_count, seq_count, place, depth)

    def frame_rows(tokens, depth):
        return tokens.reshape(clip_count, all_frames, 1, place, depth)

    normed_s, spread_s = normalize(clip_tokens)
    hidden_s = (normed_s * (1.0 + scale_s) + shift_s).astype(jnp.bfloat16)
    qkv_s = (
        project(hidden_s, qkv_spatial)
        .astype(jnp.bfloat16)
        .reshape(clip_count * frame_count, span, 1, 3 * features)
    )
    attn_s, prob_s = attend(qkv_s, HEADS)
    attn_s = attn_s.reshape(clip_count, frame_count, span, features)
    middle = (clip_tokens.astype(jnp.float32) + gate_s * project(attn_s, out_spatial)).astype(
        jnp.bfloat16
    )
    normed_t, spread_t = normalize(middle)
    hidden_t = (normed_t * (1.0 + scale_t) + shift_t).astype(jnp.bfloat16)
    qkv_frames = project(hidden_t, qkv_temporal).astype(jnp.bfloat16)
    qkv_pos = lax.all_to_all(
        position_rows(qkv_frames, 3 * features), "seq", split_axis=2, concat_axis=1, tiled=True
    )
    qkv_pos = qkv_pos.reshape(clip_count, all_frames, place, 3 * features)
    attn_pos, prob_t = attend(qkv_pos, HEADS)
    attn_t = lax.all_to_all(
        frame_rows(attn_pos, features), "seq", split_axis=1, concat_axis=2, tiled=True
    )
    attn_t = attn_t.reshape(clip_count, frame_count, span, features)
    grad_out_t = (out_cotangent.astype(jnp.float32) * gate_t).astype(jnp.bfloat16)
    grad_attn_t = project_back(grad_out_t, out_temporal).astype(jnp.bfloat16)
    grad_attn_pos = lax.all_to_all(
        position_rows(grad_attn_t, features), "seq", split_axis=2, concat_axis=1, tiled=True
    )
    grad_attn_pos = grad_attn_pos.reshape(clip_count, all_frames, place, features)
    grad_qkv_pos = attend_back(qkv_pos, prob_t, grad_attn_pos, HEADS)
    grad_qkv_t = lax.all_to_all(
        frame_rows(grad_qkv_pos, 3 * features), "seq", split_axis=1, concat_axis=2, tiled=True
    )
    grad_qkv_t = grad_qkv_t.reshape(clip_count, frame_count, span, 3 * features)
    grad_hidden_t = project_back(grad_qkv_t, qkv_temporal)
    grad_middle = (
        out_cotangent.astype(jnp.float32) + norm_back(grad_hidden_t, normed_t, spread_t, scale_t)
    ).astype(jnp.bfloat16)
    qkv_left = grad_qkv_t.reshape(-1, 3 * features)
    hidden_flat = hidden_t.reshape(-1, features)
    out_left = grad_out_t.reshape(-1, features)
    attn_flat = attn_t.reshape(-1, features)
    left_block = qkv_left
    qkv_weight_grad = lax.psum_scatter(
        lax.dot_general(
            left_block, hidden_flat, (((0,), (0,)), ((), ())), preferred_element_type=jnp.float32
        ),
        ("seq", "rep"),
        scatter_dimension=0,
        tiled=True,
    )
    left_block = out_left
    proj_weight_grad = lax.psum_scatter(
        lax.dot_general(
            left_block, attn_flat, (((0,), (0,)), ((), ())), preferred_element_type=jnp.float32
        ),
        ("seq", "rep"),
        scatter_dimension=0,
        tiled=True,
    )
    grad_out_s = (grad_middle.astype(jnp.float32) * gate_s).astype(jnp.bfloat16)
    grad_attn_s = project_back(grad_out_s, out_spatial).astype(jnp.bfloat16)
    grad_attn_s = grad_attn_s.reshape(clip_count * frame_count, span, 1, features)
    grad_qkv_s = attend_back(qkv_s, prob_s, grad_attn_s, HEADS)
    grad_qkv_s = grad_qkv_s.reshape(clip_count, frame_count, span, 3 * features)
    grad_hidden_s = project_back(grad_qkv_s, qkv_spatial)
    input_grad = grad_middle.astype(jnp.float32) + norm_back(
        grad_hidden_s, normed_s, spread_s, scale_s
    )
    return (input_grad.astype(jnp.bfloat16), qkv_weight_grad, proj_weight_grad)


def solution(mesh):
    placed = (
        P("rep", "seq", None, None),
        P("rep", None, None),
        P(),
        P(),
        P("rep", "seq", None, None),
    )
    return jax.shard_map(
        on_device,
        mesh=mesh,
        in_specs=placed,
        out_specs=(P("rep", "seq", None, None), P(("seq", "rep"), None), P(("seq", "rep"), None)),
        check_vma=False,
    )
```

profile of v0, /device:TPU:0, one launch (start us, length us, event | category | flops | bytes accessed | tf_op | source)
XLA Modules:
  0.0 819.0 jit_solution(5575943876230745834)
XLA Ops:
  8.0 2.9 fusion.30
  11.0 1.0 reshape.326
  12.0 10.0 %all-to-all-start.1 = ((bf16[1,1,64,4,1152]{4,3,1,0,2:T(4,128)(2,1)}), bf16[1,1,64,4,1152]{4,3,1,0,2:T(4,128)(2,1)S(1)}, u32[]{:S(2)}, u32[]{:S(2)}) async-start(bf16[1,1,64,4,1152]{4,3,1,0,2:T(4,128)(2,1)} %bitcast.15), calls=%async_computation.1 | async-start | bytes 1179648 | tf_op jit(solution)/shard_map/all_to_all | solution.py:133
  22.4 7.2 fusion.11
  29.6 2.6 copy.55
  33.0 3.1 fusion.98
  36.7 1.6 copy-done
  38.3 3.8 fusion.99
  43.1 2.6 fusion.14
  45.8 1.4 reshape.322
  47.2 9.5 %all-to-all-start = ((bf16[1,1,64,4,3456]{4,3,1,0,2:T(4,128)(2,1)}), bf16[1,1,64,4,3456]{4,3,1,0,2:T(4,128)(2,1)}, u32[]{:S(2)}, u32[]{:S(2)}) async-start(bf16[1,1,64,4,3456]{4,3,1,0,2:T(4,128)(2,1)} %bitcast.11), calls=%async_computation | async-start | bytes 3538944 | tf_op jit(solution)/shard_map/all_to_all | solution.py:122
  56.7 2.9 reshape.334
  59.6 21.2 %all-to-all-done = bf16[1,1,64,4,3456]{4,3,1,0,2:T(4,128)(2,1)} async-done(((bf16[1,1,64,4,3456]{4,3,1,0,2:T(4,128)(2,1)}), bf16[1,1,64,4,3456]{4,3,1,0,2:T(4,128)(2,1)}, u32[]{:S(2)}, u32[]{:S(2)}) %all-to-all-start) | async-done | bytes 1769504 | tf_op jit(solution)/shard_map/all_to_all | solution.py:122
  80.9 7.2 reshape.333
  88.0 2.2 fusion.97
  90.2 3.6 fusion.100
  93.9 1.3 fusion.45
  95.8 1.7 multiply_reduce_fusion.2
  98.8 1.1 fusion.47
  100.0 1.3 fusion.46
  102.0 2.5 reshape.332
  104.5 18.9 %all-to-all-start.3 = ((bf16[1,64,1,4,1152]{4,3,2,0,1:T(4,128)(2,1)}), bf16[1,64,1,4,1152]{4,3,2,0,1:T(4,128)(2,1)}, u32[]{:S(2)}, u32[]{:S(2)}) async-start(bf16[1,64,1,4,1152]{4,3,2,0,1:T(4,128)(2,1)} %reshape.332), calls=%async_computation.3 | async-start | bytes 1179648 | tf_op jit(solution)/shard_map/all_to_all | solution.py:127
  123.4 3.0 fusion.44
  127.2 2.0 copy.82
  129.2 6.3 reshape.331
  135.5 9.1 %all-to-all-start.2 = ((bf16[1,64,1,4,3456]{4,3,2,0,1:T(4,128)(2,1)}), bf16[1,64,1,4,3456]{4,3,2,0,1:T(4,128)(2,1)}, u32[]{:S(2)}, u32[]{:S(2)}) async-start(bf16[1,64,1,4,3456]{4,3,2,0,1:T(4,128)(2,1)} %reshape.331), calls=%async_computation.2 | async-start | bytes 3538944 | tf_op jit(solution)/shard_map/all_to_all | solution.py:138
  144.7 1.5 reshape_reshape.28
  146.2 3.4 fusion.87
  149.6 20.1 %all-to-all-done.2 = bf16[1,64,1,4,3456]{4,3,2,0,1:T(4,128)(2,1)} async-done(((bf16[1,64,1,4,3456]{4,3,2,0,1:T(4,128)(2,1)}), bf16[1,64,1,4,3456]{4,3,2,0,1:T(4,128)(2,1)}, u32[]{:S(2)}, u32[]{:S(2)}) %all-to-all-start.2) | async-done | bytes 1769504 | tf_op jit(solution)/shard_map/all_to_all | solution.py:138
  169.7 2.9 reshape_reshape.26
  172.7 7.0 fusion.63
  179.7 8.3 %fusion.94 = f32[3456,1152]{1,0:T(8,128)} fusion(bf16[256,3456]{1,0:T(8,128)(2,1)S(1)} %reshape_reshape.26, f32[1,1,256,1152]{3,2,1,0:T(8,128)S(1)} %copy-done.3, f32[1152]{0:T(1024)S(1)} %copy-done.35, f32[1152]{0:T(1024)S(1)} %get-tuple-element.3, f32[256]{0:T(256)S(1)} %copy-done.41, f32[256]{0:T(256)S(1)} %copy-done.37), kind=kOutput, calls=%fused_computation.132 | convolution fusion | flops 2039906304 | bytes 18885632 | tf_op jit(solution)/shard_map/dot_general | solution.py:152
  188.0 1.5 reduce_sum.115
  189.6 1.1 fusion.60
  190.7 3.1 convolution_convert_fusion
  194.1 3.4 multiply_reduce_fusion
  198.8 1.8 fusion.50
  200.6 506.4 %fusion = f32[32,1152]{1,0:T(8,128)S(1)} fusion(f32[3456,1152]{1,0:T(8,128)} %fusion.94), kind=kCustom, calls=%all-reduce-scatter | all-reduce-scatter fusion | flops 4718593 | bytes 16072704
  707.1 1.7 fusion.51
  708.9 1.6 collective-permute-start.18
  710.4 1.4 collective-permute-start.17
  711.9 1.3 collective-permute-start.16
  713.2 1.3 collective-permute-start.15
  714.5 1.5 collective-permute-start.19
  716.0 3.0 fusion.52
  720.1 1.3 collective-permute-start.14
  721.4 4.6 collective-permute-start.13
  726.0 2.0 collective-permute-start.12
  728.0 18.9 %collective-permute-start.11 = (f32[32,1152]{1,0:T(8,128)S(1)}, f32[32,1152]{1,0:T(8,128)}, u32[]{:S(2)}, u32[]{:S(2)}) collective-permute-start(f32[32,1152]{1,0:T(8,128)S(1)} %fusion), channel_id=1, source_target_pairs={{0,12},{1,13},{2,14},{3,15},{4,16},{5,17},{6,18},{7,19},{8,20},{9,... | collective-permute-start | bytes 442376
  746.9 2.0 collective-permute-start.10
  748.9 2.7 fusion.55
  751.8 6.1 collective-permute-start.9
  758.0 4.0 collective-permute-start.8
  762.0 2.6 collective-permute-start.7
  764.7 2.7 collective-permute-start.6
  767.3 2.8 collective-permute-start.5
  770.2 3.8 collective-permute-start.4
  774.0 3.8 collective-permute-start.3
  777.9 3.8 collective-permute-start.2
  781.7 2.0 collective-permute-start.1
  783.7 3.9 collective-permute-start
  787.6 1.3 fusion.62
  790.9 18.8 %concatenate = f32[667,1152]{1,0:T(8,128)S(1)} concatenate(f32[27,1152]{1,0:T(8,128)} %copy-done.20, f32[32,1152]{1,0:T(8,128)S(1)} %collective-permute-done.18, f32[32,1152]{1,0:T(8,128)S(1)} %collective-permute-done.17, f32[32,1152]{1,0:T(8,128)} %copy-done.18, f32[32,1152]{1,0:T(8,128)} %copy-done.19, f32[32,1152]{1,0:T(8,128)} %copy-done.21, f32[32,1152]{1,0:T(8,128)} %copy-done.22, ...), dimensions={0} | concatenate | bytes 6147072
  810.4 1.5 constant_dynamic-slice_fusion.1
  (156 shorter events, 12.7 us)
Async XLA Ops:
  8.0 14.4 %copy-start.42 = (f32[1152]{0:T(1024)}, f32[1152]{0:T(1024)S(1)}, u32[]{:S(2)}) copy-start(f32[1152]{0:T(1024)S(1)} %get-tuple-element.7) | copy-start | bytes 13828
  8.0 30.3 %copy-start.44 = (f32[1152]{0:T(1024)}, f32[1152]{0:T(1024)S(1)}, u32[]{:S(2)}) copy-start(f32[1152]{0:T(1024)S(1)} %get-tuple-element.8) | copy-start | bytes 13828
  8.0 34.4 %copy-start.34 = (f32[1152]{0:T(1024)}, f32[1152]{0:T(1024)S(1)}, u32[]{:S(2)}) copy-start(f32[1152]{0:T(1024)S(1)} %get-tuple-element.5) | copy-start | bytes 13828
  11.0 10.9 %copy-start.5 = (bf16[1,1,256,1152]{3,2,1,0:T(8,128)(2,1)S(1)}, bf16[1,1,256,1152]{3,2,1,0:T(8,128)(2,1)}, u32[]{:S(2)}) copy-start(bf16[1,1,256,1152]{3,2,1,0:T(8,128)(2,1)} %param.5) | copy-start | bytes 1769476
  12.0 35.2 %all-to-all-start.1 = ((bf16[1,1,64,4,1152]{4,3,1,0,2:T(4,128)(2,1)}), bf16[1,1,64,4,1152]{4,3,1,0,2:T(4,128)(2,1)S(1)}, u32[]{:S(2)}, u32[]{:S(2)}) async-start(bf16[1,1,64,4,1152]{4,3,1,0,2:T(4,128)(2,1)} %bitcast.15), calls=%async_computation.1 | async-start | bytes 1179648 | tf_op jit(solution)/shard_map/all_to_all | solution.py:133
  22.1 7.5 copy-start.38
  22.4 7.2 copy-start.46
  32.2 3.9 copy-start.4
  33.0 10.1 %slice-start = ((s8[10616832]{0:T(1024)(128)(4,1)}), s8[4194304]{0:T(1024)(128)(4,1)S(1)}, s32[]{:S(2)}) async-start(s8[10616832]{0:T(1024)(128)(4,1)} %bitcast.163), calls=%async_computation.5 | async-start | bytes 8388608
  36.2 6.9 slice-start.1
  36.2 6.9 slice-start.2
  42.1 3.6 copy-start.36
  42.4 3.4 copy-start.40
  47.2 33.7 %all-to-all-start = ((bf16[1,1,64,4,3456]{4,3,1,0,2:T(4,128)(2,1)}), bf16[1,1,64,4,3456]{4,3,1,0,2:T(4,128)(2,1)}, u32[]{:S(2)}, u32[]{:S(2)}) async-start(bf16[1,1,64,4,3456]{4,3,1,0,2:T(4,128)(2,1)} %bitcast.11), calls=%async_computation | async-start | bytes 3538944 | tf_op jit(solution)/shard_map/all_to_all | solution.py:122
  90.2 3.6 copy-start.15
  93.8 3.7 copy-start.13
  104.5 31.0 %all-to-all-start.3 = ((bf16[1,64,1,4,1152]{4,3,2,0,1:T(4,128)(2,1)}), bf16[1,64,1,4,1152]{4,3,2,0,1:T(4,128)(2,1)}, u32[]{:S(2)}, u32[]{:S(2)}) async-start(bf16[1,64,1,4,1152]{4,3,2,0,1:T(4,128)(2,1)} %reshape.332), calls=%async_computation.3 | async-start | bytes 1179648 | tf_op jit(solution)/shard_map/all_to_all | solution.py:127
  135.5 10.7 %copy-start.10 = (bf16[1,1,256,1152]{3,2,1,0:T(8,128)(2,1)S(1)}, bf16[1,1,256,1152]{3,2,1,0:T(8,128)(2,1)}, u32[]{:S(2)}) copy-start(bf16[1,1,256,1152]{3,2,1,0:T(8,128)(2,1)} %param.9) | copy-start | bytes 1769476
  135.5 34.2 %all-to-all-start.2 = ((bf16[1,64,1,4,3456]{4,3,2,0,1:T(4,128)(2,1)}), bf16[1,64,1,4,3456]{4,3,2,0,1:T(4,128)(2,1)}, u32[]{:S(2)}, u32[]{:S(2)}) async-start(bf16[1,64,1,4,3456]{4,3,2,0,1:T(4,128)(2,1)} %reshape.331), calls=%async_computation.2 | async-start | bytes 3538944 | tf_op jit(solution)/shard_map/all_to_all | solution.py:138
  144.7 665.8 %all-reduce.5.cloned.1.call-start = ((), (), s32[]{:S(2)}) async-start(), calls=%async_computation.4 | async-start | bytes 10616832
  149.6 23.0 %copy-start.3 = (f32[1,1,256,1152]{3,2,1,0:T(8,128)S(1)}, f32[1,1,256,1152]{3,2,1,0:T(8,128)}, u32[]{:S(2)}) copy-start(f32[1,1,256,1152]{3,2,1,0:T(8,128)} %copy-done.2) | copy-start | bytes 3538948
  172.6 7.0 copy-start.35
  172.6 7.0 copy-start.37
  172.6 7.0 copy-start.41
  194.1 3.5 copy-start.16
  194.1 3.8 copy-start.1
  707.1 8.9 %copy-start.17 = (bf16[256,1152]{0,1:T(8,128)(2,1)S(1)}, bf16[256,1152]{0,1:T(8,128)(2,1)}, u32[]{:S(2)}) copy-start(bf16[256,1152]{0,1:T(8,128)(2,1)} %copy-done.16) | copy-start | bytes 1769476
  707.1 41.8 %slice-start.3 = ((s8[10616832]{0:T(1024)(128)(4,1)}), s8[4194304]{0:T(1024)(128)(4,1)S(1)}, s32[]{:S(2)}) async-start(s8[10616832]{0:T(1024)(128)(4,1)} %bitcast.165), calls=%async_computation.8 | async-start | bytes 8388608
  708.8 40.0 %slice-start.4 = ((s8[10616832]{0:T(1024)(128)(4,1)}), s8[4194304]{0:T(1024)(128)(4,1)S(1)}, s32[]{:S(2)}) async-start(s8[10616832]{0:T(1024)(128)(4,1)} %bitcast.165), calls=%async_computation.9 | async-start | bytes 8388608
  708.8 40.0 %slice-start.5 = ((s8[10616832]{0:T(1024)(128)(4,1)}), s8[2228224]{0:T(1024)(128)(4,1)S(1)}, s32[]{:S(2)}) async-start(s8[10616832]{0:T(1024)(128)(4,1)} %bitcast.165), calls=%async_computation.10 | async-start | bytes 4456448
  708.9 12.5 %collective-permute-start.18 = (f32[32,1152]{1,0:T(8,128)S(1)}, f32[32,1152]{1,0:T(8,128)S(1)}, u32[]{:S(2)}, u32[]{:S(2)}) collective-permute-start(f32[32,1152]{1,0:T(8,128)S(1)} %fusion), channel_id=1, source_target_pairs={{0,19},{1,20},{2,21},{3,22},{4,23},{5,24},{6,25},{7,26},{8,27},{9,... | collective-permute-start | bytes 442376
  710.4 15.6 %collective-permute-start.17 = (f32[32,1152]{1,0:T(8,128)S(1)}, f32[32,1152]{1,0:T(8,128)S(1)}, u32[]{:S(2)}, u32[]{:S(2)}) collective-permute-start(f32[32,1152]{1,0:T(8,128)S(1)} %fusion), channel_id=1, source_target_pairs={{0,18},{1,19},{2,20},{3,21},{4,22},{5,23},{6,24},{7,25},{8,26},{9,... | collective-permute-start | bytes 442376
  711.9 16.1 %collective-permute-start.16 = (f32[32,1152]{1,0:T(8,128)S(1)}, f32[32,1152]{1,0:T(8,128)S(1)}, u32[]{:S(2)}, u32[]{:S(2)}) collective-permute-start(f32[32,1152]{1,0:T(8,128)S(1)} %fusion), channel_id=1, source_target_pairs={{0,17},{1,18},{2,19},{3,20},{4,21},{5,22},{6,23},{7,24},{8,25},{9,... | collective-permute-start | bytes 442376
  713.2 33.7 %collective-permute-start.15 = (f32[32,1152]{1,0:T(8,128)S(1)}, f32[32,1152]{1,0:T(8,128)S(1)}, u32[]{:S(2)}, u32[]{:S(2)}) collective-permute-start(f32[32,1152]{1,0:T(8,128)S(1)} %fusion), channel_id=1, source_target_pairs={{0,16},{1,17},{2,18},{3,19},{4,20},{5,21},{6,22},{7,23},{8,24},{9,... | collective-permute-start | bytes 442376
  714.5 5.6 collective-permute-start.19
  718.9 29.9 %copy-start.6 = (bf16[1,1,256,1152]{3,2,1,0:T(8,128)(2,1)S(1)}, bf16[1,1,256,1152]{3,2,1,0:T(8,128)(2,1)}, u32[]{:S(2)}) copy-start(bf16[1,1,256,1152]{3,2,1,0:T(8,128)(2,1)} %param.5) | copy-start | bytes 1769476
  719.0 29.9 %copy-start.39 = (f32[256]{0:T(256)S(1)}, f32[256]{0:T(256)}, u32[]{:S(2)}) copy-start(f32[256]{0:T(256)} %copy-done.38) | copy-start | bytes 3076
  719.0 29.9 %copy-start.43 = (f32[1152]{0:T(1024)S(1)}, f32[1152]{0:T(1024)}, u32[]{:S(2)}) copy-start(f32[1152]{0:T(1024)} %copy-done.42) | copy-start | bytes 13828
  719.0 29.9 %copy-start.47 = (f32[256]{0:T(256)S(1)}, f32[256]{0:T(256)}, u32[]{:S(2)}) copy-start(f32[256]{0:T(256)} %copy-done.46) | copy-start | bytes 3076
  720.1 28.8 %copy-start.20 = (f32[27,1152]{1,0:T(8,128)}, f32[27,1152]{1,0:T(8,128)S(1)}, u32[]{:S(2)}) copy-start(f32[27,1152]{1,0:T(8,128)S(1)} %collective-permute-done.19) | copy-start | bytes 373252
  720.1 31.7 %collective-permute-start.14 = (f32[32,1152]{1,0:T(8,128)S(1)}, f32[32,1152]{1,0:T(8,128)S(1)}, u32[]{:S(2)}, u32[]{:S(2)}) collective-permute-start(f32[32,1152]{1,0:T(8,128)S(1)} %fusion), channel_id=1, source_target_pairs={{0,15},{1,16},{2,17},{3,18},{4,19},{5,20},{6,21},{7,22},{8,23},{9,... | collective-permute-start | bytes 442376
  721.4 36.6 %collective-permute-start.13 = (f32[32,1152]{1,0:T(8,128)S(1)}, f32[32,1152]{1,0:T(8,128)S(1)}, u32[]{:S(2)}, u32[]{:S(2)}) collective-permute-start(f32[32,1152]{1,0:T(8,128)S(1)} %fusion), channel_id=1, source_target_pairs={{0,14},{1,15},{2,16},{3,17},{4,18},{5,19},{6,20},{7,21},{8,22},{9,... | collective-permute-start | bytes 442376
  726.0 36.0 %collective-permute-start.12 = (f32[32,1152]{1,0:T(8,128)S(1)}, f32[32,1152]{1,0:T(8,128)}, u32[]{:S(2)}, u32[]{:S(2)}) collective-permute-start(f32[32,1152]{1,0:T(8,128)S(1)} %fusion), channel_id=1, source_target_pairs={{0,13},{1,14},{2,15},{3,16},{4,17},{5,18},{6,19},{7,20},{8,21},{9,... | collective-permute-start | bytes 442376
  728.0 23.7 %copy-start.18 = (f32[32,1152]{1,0:T(8,128)}, f32[32,1152]{1,0:T(8,128)S(1)}, u32[]{:S(2)}) copy-start(f32[32,1152]{1,0:T(8,128)S(1)} %collective-permute-done.16) | copy-start | bytes 442372
  728.0 36.7 %collective-permute-start.11 = (f32[32,1152]{1,0:T(8,128)S(1)}, f32[32,1152]{1,0:T(8,128)}, u32[]{:S(2)}, u32[]{:S(2)}) collective-permute-start(f32[32,1152]{1,0:T(8,128)S(1)} %fusion), channel_id=1, source_target_pairs={{0,12},{1,13},{2,14},{3,15},{4,16},{5,17},{6,18},{7,19},{8,20},{9,... | collective-permute-start | bytes 442376
  746.9 4.7 copy-start.19
  746.9 20.4 %collective-permute-start.10 = (f32[32,1152]{1,0:T(8,128)S(1)}, f32[32,1152]{1,0:T(8,128)}, u32[]{:S(2)}, u32[]{:S(2)}) collective-permute-start(f32[32,1152]{1,0:T(8,128)S(1)} %fusion), channel_id=1, source_target_pairs={{0,11},{1,12},{2,13},{3,14},{4,15},{5,16},{6,17},{7,18},{8,19},{9,... | collective-permute-start | bytes 442376
  748.9 38.7 %copy-start.12 = (bf16[1,1,256,1152]{3,2,1,0:T(8,128)(2,1)S(1)}, bf16[1,1,256,1152]{3,2,1,0:T(8,128)(2,1)}, u32[]{:S(2)}) copy-start(bf16[1,1,256,1152]{3,2,1,0:T(8,128)(2,1)} %copy-done.11) | copy-start | bytes 1769476
  751.8 37.2 %copy-start.21 = (f32[32,1152]{1,0:T(8,128)}, f32[32,1152]{1,0:T(8,128)S(1)}, u32[]{:S(2)}) copy-start(f32[32,1152]{1,0:T(8,128)S(1)} %collective-permute-done.14) | copy-start | bytes 442372
  751.8 18.4 %collective-permute-start.9 = (f32[32,1152]{1,0:T(8,128)S(1)}, f32[32,1152]{1,0:T(8,128)S(1)}, u32[]{:S(2)}, u32[]{:S(2)}) collective-permute-start(f32[32,1152]{1,0:T(8,128)S(1)} %fusion), channel_id=1, source_target_pairs={{0,10},{1,11},{2,12},{3,13},{4,14},{5,15},{6,16},{7,17},{8,18},{9,... | collective-permute-start | bytes 442376
  758.0 31.0 %copy-start.22 = (f32[32,1152]{1,0:T(8,128)}, f32[32,1152]{1,0:T(8,128)S(1)}, u32[]{:S(2)}) copy-start(f32[32,1152]{1,0:T(8,128)S(1)} %collective-permute-done.13) | copy-start | bytes 442372
  758.0 16.0 %collective-permute-start.8 = (f32[32,1152]{1,0:T(8,128)S(1)}, f32[32,1152]{1,0:T(8,128)S(1)}, u32[]{:S(2)}, u32[]{:S(2)}) collective-permute-start(f32[32,1152]{1,0:T(8,128)S(1)} %fusion), channel_id=1, source_target_pairs={{0,9},{1,10},{2,11},{3,12},{4,13},{5,14},{6,15},{7,16},{8,17},{9,1... | collective-permute-start | bytes 442376
  762.0 15.9 %collective-permute-start.7 = (f32[32,1152]{1,0:T(8,128)S(1)}, f32[32,1152]{1,0:T(8,128)S(1)}, u32[]{:S(2)}, u32[]{:S(2)}) collective-permute-start(f32[32,1152]{1,0:T(8,128)S(1)} %fusion), channel_id=1, source_target_pairs={{0,8},{1,9},{2,10},{3,11},{4,12},{5,13},{6,14},{7,15},{8,16},{9,17... | collective-permute-start | bytes 442376
  764.7 17.0 %collective-permute-start.6 = (f32[32,1152]{1,0:T(8,128)S(1)}, f32[32,1152]{1,0:T(8,128)S(1)}, u32[]{:S(2)}, u32[]{:S(2)}) collective-permute-start(f32[32,1152]{1,0:T(8,128)S(1)} %fusion), channel_id=1, source_target_pairs={{0,7},{1,8},{2,9},{3,10},{4,11},{5,12},{6,13},{7,14},{8,15},{9,16}... | collective-permute-start | bytes 442376
  767.3 16.3 %collective-permute-start.5 = (f32[32,1152]{1,0:T(8,128)S(1)}, f32[32,1152]{1,0:T(8,128)S(1)}, u32[]{:S(2)}, u32[]{:S(2)}) collective-permute-start(f32[32,1152]{1,0:T(8,128)S(1)} %fusion), channel_id=1, source_target_pairs={{0,6},{1,7},{2,8},{3,9},{4,10},{5,11},{6,12},{7,13},{8,14},{9,15},... | collective-permute-start | bytes 442376
  770.2 18.8 %copy-start.23 = (f32[32,1152]{1,0:T(8,128)}, f32[32,1152]{1,0:T(8,128)S(1)}, u32[]{:S(2)}) copy-start(f32[32,1152]{1,0:T(8,128)S(1)} %collective-permute-done.9) | copy-start | bytes 442372
  770.2 18.7 %collective-permute-start.4 = (f32[32,1152]{1,0:T(8,128)S(1)}, f32[32,1152]{1,0:T(8,128)S(1)}, u32[]{:S(2)}, u32[]{:S(2)}) collective-permute-start(f32[32,1152]{1,0:T(8,128)S(1)} %fusion), channel_id=1, source_target_pairs={{0,5},{1,6},{2,7},{3,8},{4,9},{5,10},{6,11},{7,12},{8,13},{9,14},{... | collective-permute-start | bytes 442376
  774.0 15.0 %copy-start.24 = (f32[32,1152]{1,0:T(8,128)}, f32[32,1152]{1,0:T(8,128)S(1)}, u32[]{:S(2)}) copy-start(f32[32,1152]{1,0:T(8,128)S(1)} %collective-permute-done.8) | copy-start | bytes 442372
  774.0 14.9 %collective-permute-start.3 = (f32[32,1152]{1,0:T(8,128)S(1)}, f32[32,1152]{1,0:T(8,128)S(1)}, u32[]{:S(2)}, u32[]{:S(2)}) collective-permute-start(f32[32,1152]{1,0:T(8,128)S(1)} %fusion), channel_id=1, source_target_pairs={{0,4},{1,5},{2,6},{3,7},{4,8},{5,9},{6,10},{7,11},{8,12},{9,13},{1... | collective-permute-start | bytes 442376
  777.9 11.2 %copy-start.25 = (f32[32,1152]{1,0:T(8,128)}, f32[32,1152]{1,0:T(8,128)S(1)}, u32[]{:S(2)}) copy-start(f32[32,1152]{1,0:T(8,128)S(1)} %collective-permute-done.7) | copy-start | bytes 442372
  777.9 11.1 %collective-permute-start.2 = (f32[32,1152]{1,0:T(8,128)S(1)}, f32[32,1152]{1,0:T(8,128)S(1)}, u32[]{:S(2)}, u32[]{:S(2)}) collective-permute-start(f32[32,1152]{1,0:T(8,128)S(1)} %fusion), channel_id=1, source_target_pairs={{0,3},{1,4},{2,5},{3,6},{4,7},{5,8},{6,9},{7,10},{8,11},{9,12},{10... | collective-permute-start | bytes 442376
  781.7 7.3 collective-permute-start.1
  783.7 3.9 copy-start.27
  783.7 7.2 collective-permute-start
  (15 other events, 23.7 us)
Sparse Core Ops, SparseCore 0:
  150.5 555.1 all-reduce.4
where the time goes:
time: 826 us; the launch traced here: 819 us
  blocking collectives  506 us (61%)
  starting transfers between devices  119 us (14%)
  matrix products  64.2 us (8%)
  local copies, waits for them, and re-layouts  60 us (7%)
  waiting for transfers between devices  42.9 us (5%)
  between operations  15.3 us (2%)
  other arithmetic  11.2 us (1%)
    unnamed x1, blocking collectives  506 us
    unnamed x21, starting transfers between devices  71.4 us
    unnamed x112, local copies, waits for them, and re-layouts  26.7 us
    all_to_all x1, waiting for transfers between devices, on_device(): lax.all_to_all(position_rows(qkv_frames, 3 * features), 'seq', split_axis...  21.2 us
    all_to_all x1, waiting for transfers between devices, on_device(): lax.all_to_all(frame_rows(grad_qkv_pos, 3 * features), 'seq', split_axis=...  20.1 us
    all_to_all x1, starting transfers between devices, on_device(): lax.all_to_all(frame_rows(attn_pos, features), 'seq', split_axis=1, conca...  18.9 us
  transfers between devices with their start and end apart: 25, of which 4 were waited for; matrix products, arithmetic and copies ran while one was open for 74% of the time, Pallas kernels for 0%

commit v1 on v0

v1 whole, which is shorter than its diff:
```python
import functools

import jax
import jax.numpy as jnp
import numpy as np
from jax import lax
from jax.experimental import pallas as pl
from jax.experimental.pallas import tpu as pltpu
from jax.sharding import PartitionSpec as P

HEADS = 16
HEAD = 72
D = HEADS * HEAD
T = 256
PLACE = 4
FACTOR = HEAD**-0.5
LOG2E = 1.4426950408889634
BOTH = ("seq", "rep")
Q_ROWS = 27
P_ROWS = 9
SUBS = 8
Q_CHUNK = SUBS * Q_ROWS
P_CHUNK = SUBS * P_ROWS
CHUNK = Q_CHUNK + P_CHUNK
PART = 384
bf16 = jnp.bfloat16
f32 = jnp.float32

NN = (((1,), (0,)), ((), ()))
NT = (((1,), (1,)), ((), ()))
TN = (((0,), (0,)), ((), ()))


def dot(a, b, dims=NN):
    return lax.dot_general(a, b, dims, preferred_element_type=f32)


GRAY = (0, 1, 3, 2)


def device_index(x, y, z, core):
    return ((((x % 2) * 4 + z) * 4 + y) * 2 + core) * 2 + x // 2


def all_coords():
    return [
        (x, y, z, core)
        for x in range(4)
        for y in range(4)
        for z in range(4)
        for core in range(2)
    ]


def flip_pairs(axis, bits):
    pairs = []
    for coord in all_coords():
        other = list(coord)
        other[axis] = GRAY.index(GRAY[coord[axis]] ^ (1 << bits[coord[3]]))
        pairs.append((device_index(*coord), device_index(*other)))
    return pairs


def core_pairs():
    return [(device_index(x, y, z, c), device_index(x, y, z, 1 - c)) for x, y, z, c in all_coords()]


def owner_of(core, chunk, sub):
    coord = []
    for axis in range(3):
        high, low = (chunk >> (2 - axis)) & 1, (sub >> (2 - axis)) & 1
        code = (low << 1) | high if core == 0 else (high << 1) | low
        coord.append(GRAY.index(code))
    return device_index(*coord, core)


def normalize(tokens):
    values = tokens.astype(f32)
    center = values - jnp.mean(values, axis=-1, keepdims=True)
    spread = lax.rsqrt(jnp.mean(center * center, axis=-1, keepdims=True) + 1e-06)
    return center * spread, spread


ROWS = 64


def modulated(src_ref, mod_ref, shift, scale, out_ref):
    for r in range(0, T, ROWS):
        normed, _ = normalize(src_ref[r : r + ROWS, :])
        out_ref[r : r + ROWS, :] = (
            normed * (1.0 + mod_ref[scale : scale + 1, :]) + mod_ref[shift : shift + 1, :]
        ).astype(bf16)


def norm_back_rows(src_ref, direct_ref, grad_ref, mod_ref, scale, out_ref):
    for r in range(0, T, ROWS):
        normed, spread = normalize(src_ref[r : r + ROWS, :])
        g = grad_ref[r : r + ROWS, :] * (1.0 + mod_ref[scale : scale + 1, :])
        centered = g - jnp.mean(g, axis=-1, keepdims=True)
        back = spread * (centered - normed * jnp.mean(g * normed, axis=-1, keepdims=True))
        out_ref[r : r + ROWS, :] = (direct_ref[r : r + ROWS, :].astype(f32) + back).astype(bf16)


W_ROWS = 576
W_CHUNKS = 4 * D // W_ROWS
QKV_CHUNKS = 3 * D // W_ROWS


def weight_copies(w_hbm, w_ref, sems, chunks):
    return [
        pltpu.make_async_copy(
            w_hbm.at[pl.ds(i * W_ROWS, W_ROWS), :], w_ref.at[pl.ds(i * W_ROWS, W_ROWS), :], sems.at[i]
        )
        for i in chunks
    ]


def qkv_heads(copies, w_ref, hid_ref, qkv_ref):
    per = W_ROWS // HEAD
    for i in range(QKV_CHUNKS):
        copies[i].wait()
        block = dot(w_ref[i * W_ROWS : (i + 1) * W_ROWS, :], hid_ref[...], NT)
        for j in range(per):
            qkv_ref[i * per + j] = block[j * HEAD : (j + 1) * HEAD, :].astype(bf16)


def softmax_keys(q, k, mask):
    scores = dot(k, q, TN)
    if mask is not None:
        scores = jnp.where(mask, scores, -1e30)
    top = jnp.max(scores, axis=0, keepdims=True)
    raw = jnp.exp2((scores - top) * (FACTOR * LOG2E))
    return raw * (1.0 / jnp.sum(raw, axis=0, keepdims=True))


def head_back(q, k, v, g, prob, prob_low):
    grad_prob = dot(v, g, TN)
    inner = jnp.sum(prob * grad_prob, axis=0, keepdims=True)
    grad_score = (prob * (grad_prob - inner)).astype(bf16)
    dq = dot(k, grad_score) * FACTOR
    dk = dot(q, grad_score, NT) * FACTOR
    dv = dot(g, prob_low, NT)
    return dq, dk, dv


def grad_heads(w_ref, go_ref, out_ref):
    for j in range(0, D, PART):
        block = dot(go_ref[...], w_ref[3 * D : 4 * D, j : j + PART])
        flipped = block.T
        if j == 0:
            whole = [flipped]
        else:
            whole.append(flipped)
    full = jnp.concatenate(whole, axis=0)
    for h in range(HEADS):
        out_ref[h] = full[h * HEAD : (h + 1) * HEAD, :].astype(bf16)


def spatial_forward_kernel(
    x_ref, mod_ref, w_hbm, middle_ref, qkv_ref, prob_ref, w_ref, hid_ref, attn_ref, sems
):
    copies = weight_copies(w_hbm, w_ref, sems, range(W_CHUNKS))
    for c in copies:
        c.start()
    modulated(x_ref, mod_ref, 0, 1, hid_ref)
    qkv_heads(copies, w_ref, hid_ref, qkv_ref)

    def pair(i, _):
        outs = []
        for s in range(2):
            h = 2 * i + s
            prob = softmax_keys(qkv_ref[h], qkv_ref[HEADS + h], None).astype(bf16)
            prob_ref[h] = prob
            outs.append(dot(qkv_ref[2 * HEADS + h], prob))
        rows = pl.ds(pl.multiple_of(i * 2 * HEAD, 16), 2 * HEAD)
        attn_ref[rows, :] = jnp.concatenate(outs, axis=0).astype(bf16)
        return _

    lax.fori_loop(0, HEADS // 2, pair, 0)
    for c in copies[QKV_CHUNKS:]:
        c.wait()
    for j in range(0, D, PART):
        block = dot(w_ref[3 * D + j : 3 * D + j + PART, :], attn_ref[...]).T
        cols = slice(j, j + PART)
        middle_ref[:, cols] = (
            x_ref[:, cols].astype(f32) + mod_ref[2:3, cols] * block
        ).astype(bf16)


def cotangent_kernel(cot_ref, mod_ref, w_hbm, heads_ref, lp_ref, w_ref, go_ref, gof_ref, tmp_ref, sems):
    copies = weight_copies(w_hbm, w_ref, sems, range(QKV_CHUNKS, W_CHUNKS))
    for c in copies:
        c.start()
    for r in range(0, T, ROWS):
        go_ref[r : r + ROWS, :] = (
            cot_ref[r : r + ROWS, :].astype(f32) * mod_ref[5:6, :]
        ).astype(bf16)
    for j in range(0, D, PART):
        gof_ref[j : j + PART, :] = go_ref[:, j : j + PART].astype(f32).T
    gather_rows(gof_ref, tmp_ref, lp_ref, P_ROWS)
    for c in copies:
        c.wait()
    grad_heads(w_ref, go_ref, heads_ref)


def gather_rows(src_ref, tmp_ref, out_ref, rows):
    for core in range(2):
        for chunk in range(SUBS):
            slot = (core * SUBS + chunk) % 2
            for sub in range(SUBS):
                start = rows * owner_of(core, chunk, sub)
                tmp_ref[slot, rows * sub : rows * (sub + 1), :] = src_ref[start : start + rows, :]
            out_ref[core * SUBS + chunk] = tmp_ref[slot].astype(bf16)


def temporal_kernel(
    m_ref, cot_ref, g_ref, mod_ref, w_hbm,
    gm_ref, hid_ref, attn_out_ref, lq_ref,
    w_ref, qkv_ref, attn_ref, grad_ref, gh_ref, tmp_ref, sems,
):
    copies = weight_copies(w_hbm, w_ref, sems, range(QKV_CHUNKS))
    for c in copies:
        c.start()
    modulated(m_ref, mod_ref, 3, 4, hid_ref)
    qkv_heads(copies, w_ref, hid_ref, qkv_ref)
    one = lax.broadcasted_iota(jnp.int32, (T, T), 0)
    two = lax.broadcasted_iota(jnp.int32, (T, T), 1)
    mask = (one & (PLACE - 1)) == (two & (PLACE - 1))

    def pair(i, _):
        outs, grads = [], []
        for s in range(2):
            h = 2 * i + s
            q, k, v, g = qkv_ref[h], qkv_ref[HEADS + h], qkv_ref[2 * HEADS + h], g_ref[h]
            prob = softmax_keys(q, k, mask)
            low = prob.astype(bf16)
            outs.append(dot(v, low))
            grads.append(head_back(q, k, v, g, prob, low))
        rows = pl.ds(pl.multiple_of(i * 2 * HEAD, 16), 2 * HEAD)
        attn_ref[rows, :] = jnp.concatenate(outs, axis=0)
        for n in range(3):
            rows = pl.ds(pl.multiple_of(n * D + i * 2 * HEAD, 16), 2 * HEAD)
            grad_ref[rows, :] = jnp.concatenate([grads[0][n], grads[1][n]], axis=0)
        return _

    lax.fori_loop(0, HEADS // 2, pair, 0)
    for n in range(3):
        rows = slice(n * D, (n + 1) * D)
        part = dot(grad_ref[rows, :].astype(bf16).T, w_ref[rows, :])
        gh_ref[...] = part if n == 0 else gh_ref[...] + part
    norm_back_rows(m_ref, cot_ref, gh_ref, mod_ref, 4, gm_ref)
    attn_out_ref[...] = attn_ref[...].astype(bf16).T
    gather_rows(grad_ref, tmp_ref, lq_ref, Q_ROWS)


def weight_grad_kernel(tbl_ref, lq_ref, lq2_ref, lp_ref, lp2_ref, hid_ref, hid2_ref, attn_ref, attn2_ref, out_ref):
    core = tbl_ref[12]
    for p in range(3):
        cols = slice(p * PART, (p + 1) * PART)

        def chunk(i, _, p=p, cols=cols):
            j = tbl_ref[p * 4 + i]
            mine = core * SUBS + j
            q = dot(lq_ref[mine], hid_ref[:, cols]) + dot(lq2_ref[j], hid2_ref[:, cols])
            o = dot(lp_ref[mine], attn_ref[:, cols]) + dot(lp2_ref[j], attn2_ref[:, cols])
            out_ref[p * 4 + i] = jnp.concatenate([q, o], axis=0).astype(bf16)
            return _

        lax.fori_loop(0, 4, chunk, 0)


def spatial_back_kernel(
    gm_ref, x_ref, mod_ref, qkv_ref, prob_ref, w_hbm, out_ref,
    w_ref, go_ref, g_ref, grad_ref, gh_ref, sems,
):
    copies = weight_copies(w_hbm, w_ref, sems, range(W_CHUNKS))
    for c in copies[QKV_CHUNKS:] + copies[:QKV_CHUNKS]:
        c.start()
    for r in range(0, T, ROWS):
        go_ref[r : r + ROWS, :] = (
            gm_ref[r : r + ROWS, :].astype(f32) * mod_ref[2:3, :]
        ).astype(bf16)
    for c in copies[QKV_CHUNKS:]:
        c.wait()
    grad_heads(w_ref, go_ref, g_ref)

    def pair(i, _):
        grads = []
        for s in range(2):
            h = 2 * i + s
            low = prob_ref[h]
            grads.append(
                head_back(
                    qkv_ref[h], qkv_ref[HEADS + h], qkv_ref[2 * HEADS + h], g_ref[h], low.astype(f32), low
                )
            )
        for n in range(3):
            rows = pl.ds(pl.multiple_of(n * D + i * 2 * HEAD, 16), 2 * HEAD)
            grad_ref[rows, :] = jnp.concatenate([grads[0][n], grads[1][n]], axis=0).astype(bf16)
        return _

    lax.fori_loop(0, HEADS // 2, pair, 0)
    for c in copies[:QKV_CHUNKS]:
        c.wait()
    for n in range(3):
        rows = slice(n * D, (n + 1) * D)
        part = dot(grad_ref[rows, :].T, w_ref[rows, :])
        gh_ref[...] = part if n == 0 else gh_ref[...] + part
    norm_back_rows(x_ref, gm_ref, gh_ref, mod_ref, 1, out_ref)


VMEM = pl.BlockSpec(memory_space=pltpu.VMEM)
ANY = pl.BlockSpec(memory_space=pl.ANY)
SMEM = pl.BlockSpec(memory_space=pltpu.SMEM)


def call(kernel, outs, scratch, specs, flops, name):
    return pl.pallas_call(
        kernel,
        out_shape=[jax.ShapeDtypeStruct(s, d) for s, d in outs],
        in_specs=specs,
        out_specs=[VMEM] * len(outs),
        scratch_shapes=scratch,
        compiler_params=pltpu.CompilerParams(vmem_limit_bytes=56 * 1024 * 1024),
        cost_estimate=pl.CostEstimate(flops=flops, bytes_accessed=12_000_000, transcendentals=0),
        name=name,
    )


WEIGHT = pltpu.VMEM((4 * D, D), bf16)
SEMS = pltpu.SemaphoreType.DMA((W_CHUNKS,))


def spatial_forward(x, mod, w):
    return call(
        spatial_forward_kernel,
        [((T, D), bf16), ((3 * HEADS, HEAD, T), bf16), ((HEADS, T, T), bf16)],
        [WEIGHT, pltpu.VMEM((T, D), bf16), pltpu.VMEM((D, T), bf16), SEMS],
        [VMEM, VMEM, ANY],
        6_000_000_000,
        "spatial_forward",
    )(x, mod, w)


def cotangent(cot, mod, w):
    return call(
        cotangent_kernel,
        [((HEADS, HEAD, T), bf16), ((2 * SUBS, P_CHUNK, T), bf16)],
        [WEIGHT, pltpu.VMEM((T, D), bf16), pltpu.VMEM((D, T), f32), pltpu.VMEM((2, P_CHUNK, T), f32), SEMS],
        [VMEM, VMEM, ANY],
        2_000_000_000,
        "cotangent_heads",
    )(cot, mod, w)


def temporal(m, cot, g, mod, w):
    return call(
        temporal_kernel,
        [((T, D), bf16), ((T, D), bf16), ((T, D), bf16), ((2 * SUBS, Q_CHUNK, T), bf16)],
        [
            WEIGHT,
            pltpu.VMEM((3 * HEADS, HEAD, T), bf16),
            pltpu.VMEM((D, T), f32),
            pltpu.VMEM((3 * D, T), f32),
            pltpu.VMEM((T, D), f32),
            pltpu.VMEM((2, Q_CHUNK, T), f32),
            SEMS,
        ],
        [VMEM, VMEM, VMEM, VMEM, ANY],
        12_000_000_000,
        "temporal_sublayer",
    )(m, cot, g, mod, w)


def weight_grad(tbl, *operands):
    return call(
        weight_grad_kernel,
        [((12, CHUNK, PART), bf16)],
        [],
        [SMEM] + [VMEM] * 8,
        2_000_000_000,
        "weight_grad",
    )(tbl, *operands)[0]


def spatial_back(gm, x, mod, qkv, prob, w):
    return call(
        spatial_back_kernel,
        [((T, D), bf16)],
        [
            WEIGHT,
            pltpu.VMEM((T, D), bf16),
            pltpu.VMEM((HEADS, HEAD, T), bf16),
            pltpu.VMEM((3 * D, T), bf16),
            pltpu.VMEM((T, D), f32),
            SEMS,
        ],
        [VMEM] * 5 + [ANY],
        8_000_000_000,
        "spatial_back",
    )(gm, x, mod, qkv, prob, w)[0]


def swap_positions(tokens):
    return lax.all_to_all(tokens.reshape(64, PLACE, D), "seq", 0, 0, tiled=True).reshape(T, D)


def pick(array, index):
    return lax.dynamic_index_in_dim(array, index, 0, keepdims=False)


def summed(a, b):
    return (a.astype(f32) + b.astype(f32)).astype(bf16)


def reduce_rows(send, keep, bits, low_bits):
    parts = []
    for p in range(3):
        got = lax.ppermute(send[4 * p : 4 * p + 4], BOTH, flip_pairs(p, (0, 1)))
        parts.append((keep[4 * p : 4 * p + 4], got))
    for step in (1, 2):
        shape = (2, 4 >> step, CHUNK, PART)
        nexts = []
        for p in range(3):
            axis = (p + step) % 3
            own, got = (v.reshape(shape) for v in parts[p])
            out = summed(pick(own, 1 - bits[axis]), pick(got, 1 - bits[axis]))
            moved = lax.ppermute(out, BOTH, flip_pairs(axis, (0, 1)))
            nexts.append((summed(pick(own, bits[axis]), pick(got, bits[axis])), moved))
        parts = nexts
    rows = jnp.concatenate([summed(a, b).reshape(CHUNK, PART) for a, b in parts], axis=1)
    rows = jnp.concatenate(
        [rows[:Q_CHUNK].reshape(SUBS, Q_ROWS, D), rows[Q_CHUNK:].reshape(SUBS, P_ROWS, D)], axis=1
    )
    for axis in range(3):
        rows = rows.reshape(2, SUBS >> (axis + 1), Q_ROWS + P_ROWS, D)
        moved = lax.ppermute(pick(rows, 1 - low_bits[axis]), BOTH, flip_pairs(axis, (1, 0)))
        rows = pick(rows, low_bits[axis]).astype(f32) + moved.astype(f32)
        if axis < 2:
            rows = rows.astype(bf16)
    rows = rows.reshape(Q_ROWS + P_ROWS, D)
    return rows[:Q_ROWS], rows[Q_ROWS:]


def on_device(clip_tokens, modulation, spatial_weights, temporal_weights, out_cotangent):
    x = clip_tokens.reshape(T, D)
    cot = out_cotangent.reshape(T, D)
    mod = modulation.reshape(6, D)
    seq = lax.axis_index("seq")
    core = seq % 2
    ring = (lax.axis_index("rep") * 2 + seq // 32, (seq // 2) % 4, (seq // 8) % 4)
    codes = [v ^ (v >> 1) for v in ring]
    first = [jnp.where(core == 0, v & 1, v >> 1) for v in codes]
    last = [jnp.where(core == 0, v >> 1, v & 1) for v in codes]

    cot_pos = swap_positions(cot)
    middle, qkv_s, prob_s = spatial_forward(x, mod, spatial_weights)
    middle_pos = swap_positions(middle)
    grad_attn, left_p = cotangent(cot_pos, mod, temporal_weights)
    gm_pos, hidden, attn, left_q = temporal(middle_pos, cot_pos, grad_attn, mod, temporal_weights)
    gm = swap_positions(gm_pos)

    def other(v):
        return lax.ppermute(v, BOTH, core_pairs())

    def theirs(v):
        return other(pick(v.reshape((2, SUBS) + v.shape[1:]), 1 - core))

    operands = (left_q, theirs(left_q), left_p, theirs(left_p), hidden, other(hidden), attn, other(attn))
    tables = []
    for send in (1, 0):
        entries = []
        for p in range(3):
            for i in range(4):
                b = [None] * 3
                b[p] = first[p] ^ send
                b[(p + 1) % 3] = i >> 1
                b[(p + 2) % 3] = i & 1
                entries.append(4 * b[0] + 2 * b[1] + b[2])
        tables.append(jnp.stack(entries + [core]).astype(jnp.int32))
    send = weight_grad(tables[0], *operands)
    keep = weight_grad(tables[1], *operands)
    qkv_rows, proj_rows = reduce_rows(send, keep, first, last)
    input_grad = spatial_back(gm, x, mod, qkv_s, prob_s, spatial_weights)
    return input_grad.reshape(clip_tokens.shape), qkv_rows, proj_rows


def solution(mesh):
    placed = (
        P("rep", "seq", None, None),
        P("rep", None, None),
        P(),
        P(),
        P("rep", "seq", None, None),
    )
    return jax.shard_map(
        on_device,
        mesh=mesh,
        in_specs=placed,
        out_specs=(P("rep", "seq", None, None), P(BOTH, None), P(BOTH, None)),
        check_vma=False,
    )
```

time: 826 us -> 177 us (0.21)
  blocking collectives: 506 us -> 0 us
  Pallas kernels: 0 us -> 79.2 us
  starting transfers between devices: 119 us -> 43.5 us
  matrix products: 64.2 us -> 0 us
  local copies, waits for them, and re-layouts: 60 us -> 21.3 us
  waiting for transfers between devices: 42.9 us -> 27.9 us
  between operations: 15.3 us -> 0.94 us
    unnamed x1 -> x0, blocking collectives: 506 us -> none
    pallas_call x0 -> x6, Pallas kernels: none -> 79.2 us  [the longest x1 25.1 us: temporal(): call(temporal_kernel, [((T, D), bf16), ((T, D), bf16), ((T, D), bf16), ((...]
    unnamed x21 -> x0, starting transfers between devices: 71.4 us -> none
    dot_general x20 -> x0, matrix products: 60.6 us -> none  [the longest x4 15.7 us: project_back(): result = jnp.dot(flat_rows, weight, preferred_element_type=jnp.float32)]
    all_to_all x4 -> x3, waiting for transfers between devices: 41.4 us -> 15.8 us  [swap_positions(): lax.all_to_all(tokens.reshape(64, PLACE, D), 'seq', 0, 0, tiled=True)]
    unnamed x112 -> x17, local copies, waits for them, and re-layouts: 26.7 us -> 2.46 us
    all_to_all x4 -> x3, starting transfers between devices: 47.5 us -> 24.8 us  [swap_positions(): lax.all_to_all(tokens.reshape(64, PLACE, D), 'seq', 0, 0, tiled=True)]
    another operation x8 -> x3, local copies, waits for them, and re-layouts: 26 us -> 3.56 us  [the longest x1 2.28 us: swap_positions(): tokens.reshape(64, PLACE, D)]
  transfers between devices with their start and end apart: 25 -> 19, of which waited for: 4 -> 9; matrix products, arithmetic and copies ran while one was open for 74% -> 7% of each run, Pallas kernels for 0% -> 26%
where the time goes in v1:
time: 177 us
  Pallas kernels  79.2 us (45%)
  starting transfers between devices  43.5 us (25%)
  waiting for transfers between devices  27.9 us (16%)
  local copies, waits for them, and re-layouts  21.3 us (12%)
  other arithmetic  3.75 us (2%)
    pallas_call x1, Pallas kernels, temporal(): call(temporal_kernel, [((T, D), bf16), ((T, D), bf16), ((T, D), bf16), ((...  25.1 us
    all_to_all x3, starting transfers between devices, swap_positions(): lax.all_to_all(tokens.reshape(64, PLACE, D), 'seq', 0, 0, tiled=True)  24.8 us
    pallas_call x1, Pallas kernels, spatial_forward(): call(spatial_forward_kernel, [((T, D), bf16), ((3 * HEADS, HEAD, T), bf16...  16.6 us
    pallas_call x1, Pallas kernels, spatial_back(): call(spatial_back_kernel, [((T, D), bf16)], [WEIGHT, pltpu.VMEM((T, D), b...  16.4 us
    pallas_call x2, Pallas kernels, weight_grad(): call(weight_grad_kernel, [((12, CHUNK, PART), bf16)], [], [SMEM] + [VMEM]...  16.2 us
    all_to_all x3, waiting for transfers between devices, swap_positions(): lax.all_to_all(tokens.reshape(64, PLACE, D), 'seq', 0, 0, tiled=True)  15.8 us
    ppermute x6, waiting for transfers between devices, reduce_rows(): moved = lax.ppermute(out, BOTH, flip_pairs(axis, (0, 1)))  9.33 us
    ppermute x3, starting transfers between devices, reduce_rows(): lax.ppermute(pick(rows, 1 - low_bits[axis]), BOTH, flip_pairs(axis, (1, 0)))  7.95 us
  transfers between devices with their start and end apart: 19, of which 9 were waited for; matrix products, arithmetic and copies ran while one was open for 7% of the time, Pallas kernels for 26%

profile of v1, /device:TPU:0, one launch (start us, length us, event | category | flops | bytes accessed | tf_op | source)
XLA Modules:
  0.0 176.6 jit_solution(4834281432230199188)
XLA Ops:
  0.6 2.3 %reshape_reshape.3 = bf16[64,4,1152]{2,1,0:T(4,128)(2,1)} reshape(bf16[1,1,256,1152]{3,2,1,0:T(8,128)(2,1)} %param.9) | data formatting | bytes 1179648 | tf_op jit(solution)/shard_map/reshape;reshape | solution.py:405
  2.9 10.0 %all-to-all-start.1 = ((bf16[64,4,1152]{2,1,0:T(4,128)(2,1)}), bf16[64,4,1152]{2,1,0:T(4,128)(2,1)S(1)}, u32[]{:S(2)}, u32[]{:S(2)}) async-start(bf16[64,4,1152]{2,1,0:T(4,128)(2,1)} %reshape_reshape.3), calls=%async_computation.1 | async-start | bytes 1179648 | tf_op jit(solution)/shard_map/all_to_all | solution.py:405
  12.9 0.6 copy.10
  13.5 16.6 %spatial_forward.1 = (bf16[256,1152]{1,0:T(8,128)(2,1)}, bf16[48,72,256]{2,1,0:T(8,128)(2,1)}, bf16[16,256,256]{2,1,0:T(8,128)(2,1)}) custom-call(bf16[256,1152]{1,0:T(8,128)(2,1)} %bitcast.105, f32[6,1152]{1,0:T(8,128)} %bitcast.101, bf16[4608,1152]{1,0:T(8,128)(2,1)} %w_hbm.7), custom_call_target="tpu_custom_call" | custom-call | flops 6000000000 | bytes 12000000 | tf_op jit(solution)/shard_map/spatial_forward/pallas_call | solution.py:335
  30.2 2.3 %reshape.200 = bf16[64,4,1152]{2,1,0:T(4,128)(2,1)} reshape(bf16[256,1152]{1,0:T(8,128)(2,1)} %get-tuple-element.12) | data formatting | bytes 1179648 | tf_op jit(solution)/shard_map/reshape | solution.py:405
  32.5 9.1 %all-to-all-start = ((bf16[64,4,1152]{2,1,0:T(4,128)(2,1)}), bf16[64,4,1152]{2,1,0:T(4,128)(2,1)S(1)}, u32[]{:S(2)}, u32[]{:S(2)}) async-start(bf16[64,4,1152]{2,1,0:T(4,128)(2,1)} %reshape.200), calls=%async_computation | async-start | bytes 1179648 | tf_op jit(solution)/shard_map/all_to_all | solution.py:405
  41.6 0.9 reshape.202.cot_ref
  42.5 4.9 %cotangent_heads.1 = (bf16[16,72,256]{2,1,0:T(8,128)(2,1)}, bf16[16,72,256]{2,1,0:T(8,128)(2,1)}) custom-call(bf16[256,1152]{1,0:T(8,128)(2,1)} %reshape.202.cot_ref, f32[6,1152]{1,0:T(8,128)} %bitcast.102, bf16[4608,1152]{1,0:T(8,128)(2,1)} %w_hbm.6), custom_call_target="tpu_custom_call" | custom-call | flops 2000000000 | bytes 12000000 | tf_op jit(solution)/shard_map/cotangent_heads/pallas_call | solution.py:346
  47.5 6.3 %all-to-all-done = bf16[64,4,1152]{2,1,0:T(4,128)(2,1)S(1)} async-done(((bf16[64,4,1152]{2,1,0:T(4,128)(2,1)}), bf16[64,4,1152]{2,1,0:T(4,128)(2,1)S(1)}, u32[]{:S(2)}, u32[]{:S(2)}) %all-to-all-start) | async-done | bytes 589856 | tf_op jit(solution)/shard_map/all_to_all | solution.py:405
  53.8 0.9 reshape.201.m_ref
  54.7 25.1 %temporal_sublayer.1 = (bf16[256,1152]{1,0:T(8,128)(2,1)}, bf16[256,1152]{1,0:T(8,128)(2,1)}, bf16[256,1152]{1,0:T(8,128)(2,1)}, bf16[16,216,256]{2,1,0:T(8,128)(2,1)}) custom-call(bf16[256,1152]{1,0:T(8,128)(2,1)} %reshape.201.m_ref, bf16[256,1152]{1,0:T(8,128)(2,1)} %reshape.202.cot_ref, bf16[16,72,256]{2,1,0:T(8,128)(2,1)} %get-tuple-element.13.g_ref, ...), custom_call_target="tpu_custom_call" | custom-call | flops 12000000000 | bytes 12000000 | tf_op jit(solution)/shard_map/temporal_sublayer/pallas_call | solution.py:357
  79.9 2.3 %dynamic-slice_bitcast_fusion = bf16[8,216,256]{2,1,0:T(8,128)(2,1)} fusion(bf16[2,8,216,256]{3,2,1,0:T(8,128)(2,1)} %bitcast.91, s32[]{:T(128)S(6)} %select_n.117), kind=kLoop, calls=%fused_computation.6 | loop fusion | bytes 1769476 | tf_op jit(solution)/shard_map/jit(dynamic_index_in_dim)/squeeze | solution.py:409
  82.2 0.4 collective-permute-start
  82.6 0.1 collective-permute-start.2
  82.7 0.4 collective-permute-start.3
  83.1 0.2 collective-permute-start.1
  83.3 0.6 stack.108.tbl_ref
  83.9 2.8 %collective-permute-done.1.lp2_ref = bf16[8,72,256]{2,1,0:T(8,128)(2,1)S(1)} collective-permute-done((bf16[8,72,256]{2,1,0:T(8,128)(2,1)S(1)}, bf16[8,72,256]{2,1,0:T(8,128)(2,1)S(1)}, u32[]{:S(2)}, u32[]{:S(2)}) %collective-permute-start.1) | collective-permute-done | bytes 294944 | tf_op jit(solution)/shard_map/ppermute | solution.py:464
  86.8 0.7 copy-done.5
  87.5 0.2 copy-done.4
  87.6 0.9 copy-done.1
  88.6 8.1 %weight_grad.3 = bf16[12,288,384]{2,1,0:T(8,128)(2,1)} custom-call(s32[13]{0:T(128)} %stack.108.tbl_ref, bf16[16,216,256]{2,1,0:T(8,128)(2,1)} %get-tuple-element.17.lq_ref, bf16[8,216,256]{2,1,0:T(8,128)(2,1)} %copy-done.1, bf16[16,72,256]{2,1,0:T(8,128)(2,1)} %get-tuple-element.18.lp_ref, bf16[8,72,256]{2,1,0:T(8,128)(2,1)} %copy-done.5, ...), custom_call_target="tpu_custom_call" | custom-call | flops 2000000000 | bytes 12000000 | tf_op jit(solution)/shard_map/weight_grad/pallas_call | solution.py:376
  96.7 3.3 %fusion.19 = (bf16[4,288,384]{2,1,0:T(8,128)(2,1)}, bf16[4,288,384]{2,1,0:T(8,128)(2,1)}, bf16[4,288,384]{2,1,0:T(8,128)(2,1)}) fusion(bf16[12,288,384]{2,1,0:T(8,128)(2,1)} %weight_grad.3), kind=kLoop, calls=%fused_computation.50 | loop fusion | bytes 5308416 | tf_op jit(solution)/shard_map/slice | solution.py:419
  99.9 1.3 collective-permute-start.4
  101.2 0.7 collective-permute-start.10
  101.9 0.6 collective-permute-start.7
  102.5 0.6 stack.95.tbl_ref
  103.2 8.1 %weight_grad.2 = bf16[12,288,384]{2,1,0:T(8,128)(2,1)} custom-call(s32[13]{0:T(128)} %stack.95.tbl_ref, bf16[16,216,256]{2,1,0:T(8,128)(2,1)} %get-tuple-element.17.lq_ref, bf16[8,216,256]{2,1,0:T(8,128)(2,1)} %copy-done.1, bf16[16,72,256]{2,1,0:T(8,128)(2,1)} %get-tuple-element.18.lp_ref, bf16[8,72,256]{2,1,0:T(8,128)(2,1)} %copy-done.5, ...), custom_call_target="tpu_custom_call" | custom-call | flops 2000000000 | bytes 12000000 | tf_op jit(solution)/shard_map/weight_grad/pallas_call | solution.py:376
  111.2 2.0 %fusion.18 = (bf16[4,288,384]{2,1,0:T(8,128)(2,1)S(1)}, bf16[4,288,384]{2,1,0:T(8,128)(2,1)S(1)}, bf16[4,288,384]{2,1,0:T(8,128)(2,1)S(1)}) fusion(bf16[12,288,384]{2,1,0:T(8,128)(2,1)} %weight_grad.2), kind=kLoop, calls=%fused_computation.49 | loop fusion | bytes 5308416 | tf_op jit(solution)/shard_map/slice | solution.py:420
  113.2 1.0 add_convert_fusion.5
  114.2 1.4 collective-permute-start.5
  115.6 1.0 add_convert_fusion.1
  116.6 0.7 collective-permute-start.11
  117.4 1.0 add_convert_fusion.3
  118.3 1.4 collective-permute-start.8
  119.7 3.0 %collective-permute-done.5 = bf16[2,288,384]{2,1,0:T(8,128)(2,1)S(1)} collective-permute-done((bf16[2,288,384]{2,1,0:T(8,128)(2,1)}, bf16[2,288,384]{2,1,0:T(8,128)(2,1)S(1)}, u32[]{:S(2)}, u32[]{:S(2)}) %collective-permute-start.5) | collective-permute-done | bytes 442400 | tf_op jit(solution)/shard_map/ppermute | solution.py:428
  122.7 0.1 fusion.8
  122.8 1.5 collective-permute-start.6
  124.3 0.9 collective-permute-done.11
  125.1 0.1 fusion.4
  125.2 0.7 collective-permute-start.12
  125.9 1.0 collective-permute-done.8
  126.9 1.4 collective-permute-start.9
  128.3 0.9 collective-permute-done.6
  129.2 0.1 fusion.15
  129.3 1.9 %collective-permute-done.12 = bf16[1,288,384]{2,1,0:T(8,128)(2,1)S(1)} collective-permute-done((bf16[1,288,384]{2,1,0:T(8,128)(2,1)S(1)}, bf16[1,288,384]{2,1,0:T(8,128)(2,1)S(1)}, u32[]{:S(2)}, u32[]{:S(2)}) %collective-permute-start.12) | collective-permute-done | bytes 221216 | tf_op jit(solution)/shard_map/ppermute | solution.py:428
  131.2 0.1 fusion.17
  131.3 1.6 collective-permute-done.9
  132.9 0.1 fusion.16
  133.0 0.1 pad_maximum_fusion
  133.2 0.2 concatenate.12
  133.3 0.1 concatenate.13
  133.4 0.1 fusion.11
  133.5 2.7 %collective-permute-start.13 = (bf16[4,36,1152]{2,1,0:T(8,128)(2,1)S(1)}, bf16[4,36,1152]{2,1,0:T(8,128)(2,1)S(1)}, u32[]{:S(2)}, u32[]{:S(2)}) collective-permute-start(bf16[4,36,1152]{2,1,0:T(8,128)(2,1)S(1)} %fusion.11), channel_id=1, source_target_pairs={{0,65},{2,66},{16,81},{18,82},{32,97},{34,98},{48,113},{50,114},{4... | collective-permute-start | bytes 995336 | tf_op jit(solution)/shard_map/ppermute | solution.py:437
  136.2 1.0 reshape.203
  137.1 5.8 %all-to-all-start.2 = ((bf16[64,4,1152]{2,1,0:T(4,128)(2,1)}), bf16[64,4,1152]{2,1,0:T(4,128)(2,1)S(1)}, u32[]{:S(2)}, u32[]{:S(2)}) async-start(bf16[64,4,1152]{2,1,0:T(4,128)(2,1)} %reshape.203), calls=%async_computation.2 | async-start | bytes 1179648 | tf_op jit(solution)/shard_map/all_to_all | solution.py:405
  142.9 0.1 fusion
  143.1 2.9 %collective-permute-start.14 = (bf16[2,36,1152]{2,1,0:T(8,128)(2,1)S(1)}, bf16[2,36,1152]{2,1,0:T(8,128)(2,1)S(1)}, u32[]{:S(2)}, u32[]{:S(2)}) collective-permute-start(bf16[2,36,1152]{2,1,0:T(8,128)(2,1)S(1)} %dynamic-slice_bitcast_fusion.2), channel_id=1, source_target_pairs={{0,12},{2,6},{16,28},{18,22},{32,44},{34,38},{48,60},{50,54},{4,8}... | collective-permute-start | bytes 497672 | tf_op jit(solution)/shard_map/ppermute | solution.py:437
  145.9 9.4 %all-to-all-done.2 = bf16[64,4,1152]{2,1,0:T(4,128)(2,1)S(1)} async-done(((bf16[64,4,1152]{2,1,0:T(4,128)(2,1)}), bf16[64,4,1152]{2,1,0:T(4,128)(2,1)S(1)}, u32[]{:S(2)}, u32[]{:S(2)}) %all-to-all-start.2) | async-done | bytes 589856 | tf_op jit(solution)/shard_map/all_to_all | solution.py:405
  155.3 0.9 reshape.204.gm_ref
  156.3 2.4 %collective-permute-start.15 = (bf16[1,36,1152]{2,1,0:T(8,128)(2,1)S(1)}, bf16[1,36,1152]{2,1,0:T(8,128)(2,1)S(1)}, u32[]{:S(2)}, u32[]{:S(2)}) collective-permute-start(bf16[1,36,1152]{2,1,0:T(8,128)(2,1)S(1)} %constant_dynamic-slice_fusion), channel_id=1, source_target_pairs={{0,48},{2,18},{16,32},{18,2},{32,16},{34,50},{48,0},{50,34},{4,52}... | collective-permute-start | bytes 248840 | tf_op jit(solution)/shard_map/ppermute | solution.py:437
  158.8 16.4 %spatial_back.1 = bf16[256,1152]{1,0:T(8,128)(2,1)} custom-call(bf16[256,1152]{1,0:T(8,128)(2,1)} %reshape.204.gm_ref, bf16[256,1152]{1,0:T(8,128)(2,1)} %bitcast.106, f32[6,1152]{1,0:T(8,128)} %bitcast.104, bf16[48,72,256]{2,1,0:T(8,128)(2,1)} %get-tuple-element.15.qkv_ref, bf16[16,256,256]{2,1,0:T(8,128)(2,1)} %get-tuple-element.16.prob_ref, ...), custom_call_target="tpu_custom_call" | custom-call | flops 8000000000 | bytes 12000000 | tf_op jit(solution)/shard_map/spatial_back/pallas_call | solution.py:387
  175.3 0.6 slice_bitcast_fusion.1
  175.9 0.7 slice_bitcast_fusion
  (31 shorter events, 0.3 us)
Async XLA Ops:
  0.6 12.3 %copy-start.7 = (f32[1,6,1152]{2,0,1:T(1,128)S(1)}, f32[1,6,1152]{2,0,1:T(1,128)}, u32[]{:S(2)}) copy-start(f32[1,6,1152]{2,0,1:T(1,128)} %param.6) | copy-start | bytes 82948
  2.9 29.5 %all-to-all-start.1 = ((bf16[64,4,1152]{2,1,0:T(4,128)(2,1)}), bf16[64,4,1152]{2,1,0:T(4,128)(2,1)S(1)}, u32[]{:S(2)}, u32[]{:S(2)}) async-start(bf16[64,4,1152]{2,1,0:T(4,128)(2,1)} %reshape_reshape.3), calls=%async_computation.1 | async-start | bytes 1179648 | tf_op jit(solution)/shard_map/all_to_all | solution.py:405
  32.5 21.3 %all-to-all-start = ((bf16[64,4,1152]{2,1,0:T(4,128)(2,1)}), bf16[64,4,1152]{2,1,0:T(4,128)(2,1)S(1)}, u32[]{:S(2)}, u32[]{:S(2)}) async-start(bf16[64,4,1152]{2,1,0:T(4,128)(2,1)} %reshape.200), calls=%async_computation | async-start | bytes 1179648 | tf_op jit(solution)/shard_map/all_to_all | solution.py:405
  79.8 2.7 %copy-start.2 = (bf16[256,1152]{1,0:T(8,128)(2,1)S(1)}, bf16[256,1152]{1,0:T(8,128)(2,1)}, u32[]{:S(2)}) copy-start(bf16[256,1152]{1,0:T(8,128)(2,1)} %get-tuple-element.19.hid_ref) | copy-start | bytes 1769476
  79.8 2.8 %copy-start.3 = (bf16[256,1152]{1,0:T(8,128)(2,1)S(1)}, bf16[256,1152]{1,0:T(8,128)(2,1)}, u32[]{:S(2)}) copy-start(bf16[256,1152]{1,0:T(8,128)(2,1)} %get-tuple-element.20.attn_ref) | copy-start | bytes 1769476
  79.9 3.2 %copy-start = (bf16[16,72,256]{2,1,0:T(8,128)(2,1)S(1)}, bf16[16,72,256]{2,1,0:T(8,128)(2,1)}, u32[]{:S(2)}) copy-start(bf16[16,72,256]{2,1,0:T(8,128)(2,1)} %get-tuple-element.18.lp_ref) | copy-start | bytes 1769476
  82.2 4.6 %collective-permute-start = (bf16[8,216,256]{2,1,0:T(8,128)(2,1)}, bf16[8,216,256]{2,1,0:T(8,128)(2,1)S(1)}, u32[]{:S(2)}, u32[]{:S(2)}) collective-permute-start(bf16[8,216,256]{2,1,0:T(8,128)(2,1)} %dynamic-slice_bitcast_fusion), channel_id=1, source_target_pairs={{0,2},{2,0},{16,18},{18,16},{32,34},{34,32},{48,50},{50,48},{4,6},... | collective-permute-start | bytes 2654216 | tf_op jit(solution)/shard_map/ppermute | solution.py:464
  82.6 4.2 %collective-permute-start.2 = (bf16[256,1152]{1,0:T(8,128)(2,1)S(1)}, bf16[256,1152]{1,0:T(8,128)(2,1)S(1)}, u32[]{:S(2)}, u32[]{:S(2)}) collective-permute-start(bf16[256,1152]{1,0:T(8,128)(2,1)S(1)} %copy-done.2), channel_id=1, source_target_pairs={{0,2},{2,0},{16,18},{18,16},{32,34},{34,32},{48,50},{50,48},{4,6},... | collective-permute-start | bytes 1769480 | tf_op jit(solution)/shard_map/ppermute | solution.py:464
  82.7 4.1 %collective-permute-start.3 = (bf16[256,1152]{1,0:T(8,128)(2,1)S(1)}, bf16[256,1152]{1,0:T(8,128)(2,1)}, u32[]{:S(2)}, u32[]{:S(2)}) collective-permute-start(bf16[256,1152]{1,0:T(8,128)(2,1)S(1)} %copy-done.3), channel_id=1, source_target_pairs={{0,2},{2,0},{16,18},{18,16},{32,34},{34,32},{48,50},{50,48},{4,6},... | collective-permute-start | bytes 1769480 | tf_op jit(solution)/shard_map/ppermute | solution.py:464
  83.1 3.6 %collective-permute-start.1 = (bf16[8,72,256]{2,1,0:T(8,128)(2,1)S(1)}, bf16[8,72,256]{2,1,0:T(8,128)(2,1)S(1)}, u32[]{:S(2)}, u32[]{:S(2)}) collective-permute-start(bf16[8,72,256]{2,1,0:T(8,128)(2,1)S(1)} %dynamic-slice_bitcast_fusion.1), channel_id=1, source_target_pairs={{0,2},{2,0},{16,18},{18,16},{32,34},{34,32},{48,50},{50,48},{4,6},... | collective-permute-start | bytes 884744 | tf_op jit(solution)/shard_map/ppermute | solution.py:464
  86.7 0.7 copy-start.5
  86.7 0.9 copy-start.4
  87.6 0.9 copy-start.1
  99.9 13.3 %collective-permute-start.4 = (bf16[4,288,384]{2,1,0:T(8,128)(2,1)}, bf16[4,288,384]{2,1,0:T(8,128)(2,1)S(1)}, u32[]{:S(2)}, u32[]{:S(2)}) collective-permute-start(bf16[4,288,384]{2,1,0:T(8,128)(2,1)} %get-tuple-element.24), channel_id=1, source_target_pairs={{0,64},{2,67},{16,80},{18,83},{32,96},{34,99},{48,112},{50,115},{4... | collective-permute-start | bytes 2654216 | tf_op jit(solution)/shard_map/ppermute | solution.py:419
  101.2 14.4 %collective-permute-start.10 = (bf16[4,288,384]{2,1,0:T(8,128)(2,1)}, bf16[4,288,384]{2,1,0:T(8,128)(2,1)S(1)}, u32[]{:S(2)}, u32[]{:S(2)}) collective-permute-start(bf16[4,288,384]{2,1,0:T(8,128)(2,1)} %get-tuple-element.25), channel_id=1, source_target_pairs={{0,16},{2,50},{16,0},{18,34},{32,48},{34,18},{48,32},{50,2},{4,20}... | collective-permute-start | bytes 2654216 | tf_op jit(solution)/shard_map/ppermute | solution.py:419
  101.9 15.4 %collective-permute-start.7 = (bf16[4,288,384]{2,1,0:T(8,128)(2,1)}, bf16[4,288,384]{2,1,0:T(8,128)(2,1)S(1)}, u32[]{:S(2)}, u32[]{:S(2)}) collective-permute-start(bf16[4,288,384]{2,1,0:T(8,128)(2,1)} %get-tuple-element.26), channel_id=1, source_target_pairs={{0,4},{2,14},{16,20},{18,30},{32,36},{34,46},{48,52},{50,62},{4,0}... | collective-permute-start | bytes 2654216 | tf_op jit(solution)/shard_map/ppermute | solution.py:419
  114.2 8.5 %collective-permute-start.5 = (bf16[2,288,384]{2,1,0:T(8,128)(2,1)}, bf16[2,288,384]{2,1,0:T(8,128)(2,1)S(1)}, u32[]{:S(2)}, u32[]{:S(2)}) collective-permute-start(bf16[2,288,384]{2,1,0:T(8,128)(2,1)} %get-tuple-element.28), channel_id=1, source_target_pairs={{0,4},{2,14},{16,20},{18,30},{32,36},{34,46},{48,52},{50,62},{4,0}... | collective-permute-start | bytes 1327112 | tf_op jit(solution)/shard_map/ppermute | solution.py:428
  116.6 8.5 %collective-permute-start.11 = (bf16[2,288,384]{2,1,0:T(8,128)(2,1)}, bf16[2,288,384]{2,1,0:T(8,128)(2,1)S(1)}, u32[]{:S(2)}, u32[]{:S(2)}) collective-permute-start(bf16[2,288,384]{2,1,0:T(8,128)(2,1)} %get-tuple-element.32), channel_id=1, source_target_pairs={{0,64},{2,67},{16,80},{18,83},{32,96},{34,99},{48,112},{50,115},{4... | collective-permute-start | bytes 1327112 | tf_op jit(solution)/shard_map/ppermute | solution.py:428
  118.3 8.5 %collective-permute-start.8 = (bf16[2,288,384]{2,1,0:T(8,128)(2,1)}, bf16[2,288,384]{2,1,0:T(8,128)(2,1)S(1)}, u32[]{:S(2)}, u32[]{:S(2)}) collective-permute-start(bf16[2,288,384]{2,1,0:T(8,128)(2,1)} %get-tuple-element.30), channel_id=1, source_target_pairs={{0,16},{2,50},{16,0},{18,34},{32,48},{34,18},{48,32},{50,2},{4,20}... | collective-permute-start | bytes 1327112 | tf_op jit(solution)/shard_map/ppermute | solution.py:428
  122.8 6.4 %collective-permute-start.6 = (bf16[1,288,384]{2,1,0:T(8,128)(2,1)S(1)}, bf16[1,288,384]{2,1,0:T(8,128)(2,1)S(1)}, u32[]{:S(2)}, u32[]{:S(2)}) collective-permute-start(bf16[1,288,384]{2,1,0:T(8,128)(2,1)S(1)} %fusion.8), channel_id=1, source_target_pairs={{0,16},{2,50},{16,0},{18,34},{32,48},{34,18},{48,32},{50,2},{4,20}... | collective-permute-start | bytes 663560 | tf_op jit(solution)/shard_map/ppermute | solution.py:428
  125.2 6.0 %collective-permute-start.12 = (bf16[1,288,384]{2,1,0:T(8,128)(2,1)S(1)}, bf16[1,288,384]{2,1,0:T(8,128)(2,1)S(1)}, u32[]{:S(2)}, u32[]{:S(2)}) collective-permute-start(bf16[1,288,384]{2,1,0:T(8,128)(2,1)S(1)} %fusion.4), channel_id=1, source_target_pairs={{0,4},{2,14},{16,20},{18,30},{32,36},{34,46},{48,52},{50,62},{4,0}... | collective-permute-start | bytes 663560 | tf_op jit(solution)/shard_map/ppermute | solution.py:428
  126.9 6.0 %collective-permute-start.9 = (bf16[1,288,384]{2,1,0:T(8,128)(2,1)S(1)}, bf16[1,288,384]{2,1,0:T(8,128)(2,1)S(1)}, u32[]{:S(2)}, u32[]{:S(2)}) collective-permute-start(bf16[1,288,384]{2,1,0:T(8,128)(2,1)S(1)} %fusion.6), channel_id=1, source_target_pairs={{0,64},{2,67},{16,80},{18,83},{32,96},{34,99},{48,112},{50,115},{4... | collective-permute-start | bytes 663560 | tf_op jit(solution)/shard_map/ppermute | solution.py:428
  133.1 3.0 %copy-start.6 = (bf16[256,1152]{1,0:T(8,128)(2,1)S(1)}, bf16[256,1152]{1,0:T(8,128)(2,1)}, u32[]{:S(2)}) copy-start(bf16[256,1152]{1,0:T(8,128)(2,1)} %get-tuple-element.14) | copy-start | bytes 1769476
  133.5 9.4 %collective-permute-start.13 = (bf16[4,36,1152]{2,1,0:T(8,128)(2,1)S(1)}, bf16[4,36,1152]{2,1,0:T(8,128)(2,1)S(1)}, u32[]{:S(2)}, u32[]{:S(2)}) collective-permute-start(bf16[4,36,1152]{2,1,0:T(8,128)(2,1)S(1)} %fusion.11), channel_id=1, source_target_pairs={{0,65},{2,66},{16,81},{18,82},{32,97},{34,98},{48,113},{50,114},{4... | collective-permute-start | bytes 995336 | tf_op jit(solution)/shard_map/ppermute | solution.py:437
  137.1 18.2 %all-to-all-start.2 = ((bf16[64,4,1152]{2,1,0:T(4,128)(2,1)}), bf16[64,4,1152]{2,1,0:T(4,128)(2,1)S(1)}, u32[]{:S(2)}, u32[]{:S(2)}) async-start(bf16[64,4,1152]{2,1,0:T(4,128)(2,1)} %reshape.203), calls=%async_computation.2 | async-start | bytes 1179648 | tf_op jit(solution)/shard_map/all_to_all | solution.py:405
  143.1 13.2 %collective-permute-start.14 = (bf16[2,36,1152]{2,1,0:T(8,128)(2,1)S(1)}, bf16[2,36,1152]{2,1,0:T(8,128)(2,1)S(1)}, u32[]{:S(2)}, u32[]{:S(2)}) collective-permute-start(bf16[2,36,1152]{2,1,0:T(8,128)(2,1)S(1)} %dynamic-slice_bitcast_fusion.2), channel_id=1, source_target_pairs={{0,12},{2,6},{16,28},{18,22},{32,44},{34,38},{48,60},{50,54},{4,8}... | collective-permute-start | bytes 497672 | tf_op jit(solution)/shard_map/ppermute | solution.py:437
  156.3 18.9 %collective-permute-start.15 = (bf16[1,36,1152]{2,1,0:T(8,128)(2,1)S(1)}, bf16[1,36,1152]{2,1,0:T(8,128)(2,1)S(1)}, u32[]{:S(2)}, u32[]{:S(2)}) collective-permute-start(bf16[1,36,1152]{2,1,0:T(8,128)(2,1)S(1)} %constant_dynamic-slice_fusion), channel_id=1, source_target_pairs={{0,48},{2,18},{16,32},{18,2},{32,16},{34,50},{48,0},{50,34},{4,52}... | collective-permute-start | bytes 248840 | tf_op jit(solution)/shard_map/ppermute | solution.py:437

commit v2 on v1

v2 whole, which is shorter than its diff:
```python
import functools

import jax
import jax.numpy as jnp
import numpy as np
from jax import lax
from jax.experimental import pallas as pl
from jax.experimental.pallas import tpu as pltpu
from jax.sharding import PartitionSpec as P

HEADS = 16
HEAD = 72
D = HEADS * HEAD
T = 256
PLACE = 4
FACTOR = HEAD**-0.5
LOG2E = 1.4426950408889634
BOTH = ("seq", "rep")
Q_ROWS = 27
P_ROWS = 9
SUBS = 8
Q_CHUNK = SUBS * Q_ROWS
P_CHUNK = SUBS * P_ROWS
CHUNK = Q_CHUNK + P_CHUNK
Q_PAD = 224
P_PAD = 80
KEPT = ((280, 80, 256), jnp.bfloat16)
KEPT_RAW = ((88, 256, 256), jnp.bfloat16)
GROUP = 4
V_ROWS = 80
FRAMES = 64
PART = 384
bf16 = jnp.bfloat16
f32 = jnp.float32

NN = (((1,), (0,)), ((), ()))
NT = (((1,), (1,)), ((), ()))
TN = (((0,), (0,)), ((), ()))


def dot(a, b, dims=NN):
    return lax.dot_general(a, b, dims, preferred_element_type=f32)


GRAY = (0, 1, 3, 2)


def device_index(x, y, z, core):
    return ((((x % 2) * 4 + z) * 4 + y) * 2 + core) * 2 + x // 2


def all_coords():
    return [
        (x, y, z, core)
        for x in range(4)
        for y in range(4)
        for z in range(4)
        for core in range(2)
    ]


def flip_pairs(axis, bits):
    pairs = []
    for coord in all_coords():
        other = list(coord)
        other[axis] = GRAY.index(GRAY[coord[axis]] ^ (1 << bits[coord[3]]))
        pairs.append((device_index(*coord), device_index(*other)))
    return pairs


def core_pairs():
    return [(device_index(x, y, z, c), device_index(x, y, z, 1 - c)) for x, y, z, c in all_coords()]


def owner_of(core, chunk, sub):
    coord = []
    for axis in range(3):
        high, low = (chunk >> (2 - axis)) & 1, (sub >> (2 - axis)) & 1
        code = (low << 1) | high if core == 0 else (high << 1) | low
        coord.append(GRAY.index(code))
    return device_index(*coord, core)


def normalize(tokens):
    values = tokens.astype(f32)
    center = values - jnp.mean(values, axis=-1, keepdims=True)
    spread = lax.rsqrt(jnp.mean(center * center, axis=-1, keepdims=True) + 1e-06)
    return center * spread, spread


ROWS = 64


def modulated(src_ref, mod_ref, shift, scale, out_ref):
    for r in range(0, T, ROWS):
        normed, _ = normalize(src_ref[r : r + ROWS, :])
        out_ref[r : r + ROWS, :] = (
            normed * (1.0 + mod_ref[scale : scale + 1, :]) + mod_ref[shift : shift + 1, :]
        ).astype(bf16)


def norm_back_rows(src_ref, direct_ref, grad_ref, mod_ref, scale, out_ref):
    for r in range(0, T, ROWS):
        normed, spread = normalize(src_ref[r : r + ROWS, :])
        g = grad_ref[r : r + ROWS, :] * (1.0 + mod_ref[scale : scale + 1, :])
        centered = g - jnp.mean(g, axis=-1, keepdims=True)
        back = spread * (centered - normed * jnp.mean(g * normed, axis=-1, keepdims=True))
        out_ref[r : r + ROWS, :] = (direct_ref[r : r + ROWS, :].astype(f32) + back).astype(bf16)


W_ROWS = 576
W_CHUNKS = 4 * D // W_ROWS
QKV_CHUNKS = 3 * D // W_ROWS


def weight_copies(w_hbm, w_ref, sems, chunks):
    return [
        pltpu.make_async_copy(
            w_hbm.at[pl.ds(i * W_ROWS, W_ROWS), :],
            w_ref.at[pl.ds((i - chunks[0]) * W_ROWS, W_ROWS), :],
            sems.at[i],
        )
        for i in chunks
    ]


def qkv_heads(copies, w_ref, hid_ref, qk_ref, v_ref):
    per = W_ROWS // HEAD
    for i in range(QKV_CHUNKS):
        copies[i].wait()
        block = dot(w_ref[i * W_ROWS : (i + 1) * W_ROWS, :], hid_ref[...], NT)
        for j in range(per):
            h = i * per + j
            rows = block[j * HEAD : (j + 1) * HEAD, :]
            if h < HEADS:
                qk_ref[h, :HEAD] = (rows * (FACTOR * LOG2E)).astype(bf16)
            elif h < 2 * HEADS:
                qk_ref[h, :HEAD] = rows.astype(bf16)
            else:
                v_ref[h - 2 * HEADS, :HEAD] = rows.astype(bf16)


def score_grads(q, k, grad_score):
    return dot(k, grad_score) * FACTOR, dot(q, grad_score, NT) * (1.0 / LOG2E)


def grad_heads(w_ref, go_ref, out_ref):
    block = dot(go_ref[...], w_ref[...]).T
    for h in range(HEADS):
        out_ref[h] = block[h * HEAD : (h + 1) * HEAD, :].astype(bf16)


def spatial_forward_kernel(
    x_ref, mod_ref, w_hbm,
    middle_ref, kept_out, raw_out, inv_ref,
    w_ref, hid_ref, attn_ref, qk_ref, v_ref, o_ref, raw_ref, sems, out_sems,
):
    copies = weight_copies(w_hbm, w_ref, sems, range(W_CHUNKS))
    for c in copies:
        c.start()
    v_ref[:, HEAD:V_ROWS, :] = jnp.ones((HEADS, V_ROWS - HEAD, T), bf16)
    modulated(x_ref, mod_ref, 0, 1, hid_ref)
    qkv_heads(copies, w_ref, hid_ref, qk_ref, v_ref)
    kept = [
        pltpu.make_async_copy(qk_ref, kept_out.at[pl.ds(0, 2 * HEADS)], out_sems.at[0]),
        pltpu.make_async_copy(v_ref, kept_out.at[pl.ds(2 * HEADS, HEADS)], out_sems.at[1]),
    ]
    for c in kept:
        c.start()

    def raw_copy(i):
        part = pl.ds(i * GROUP, GROUP)
        return pltpu.make_async_copy(raw_ref.at[part], raw_out.at[part], out_sems.at[3 + i])

    def group(i, _):
        heads = [i * GROUP + s for s in range(GROUP)]
        scores = [dot(qk_ref[HEADS + h, :HEAD], qk_ref[h, :HEAD], TN) for h in heads]
        raws = []
        for h, sc in zip(heads, scores):
            raws.append(jnp.exp2(sc - jnp.max(sc, axis=0, keepdims=True)).astype(bf16))
            raw_ref[h] = raws[-1]
        raw_copy(i).start()
        for h, raw in zip(heads, raws):
            mixed = dot(v_ref[h], raw)
            inv = 1.0 / mixed[HEAD : HEAD + 1]
            inv_ref[h] = inv
            out = mixed[:HEAD] * inv
            o_ref[h, :HEAD] = out.astype(bf16)
            attn_ref[pl.ds(pl.multiple_of(h * HEAD, 8), HEAD), :] = out
        return _

    lax.fori_loop(0, HEADS // GROUP, group, 0)
    kept.append(pltpu.make_async_copy(o_ref, kept_out.at[pl.ds(3 * HEADS, HEADS)], out_sems.at[2]))
    kept[-1].start()
    for c in copies[QKV_CHUNKS:]:
        c.wait()
    block = dot(w_ref[3 * D :, :], attn_ref[...].astype(bf16)).T
    middle_ref[...] = (x_ref[...].astype(f32) + mod_ref[2:3, :] * block).astype(bf16)
    for c in kept + [raw_copy(i) for i in range(HEADS // GROUP)]:
        c.wait()


def cotangent_kernel(
    cot_ref, mod_ref, w_hbm, heads_ref, mine_ref, theirs_ref, w_ref, go_ref, gof_ref, tmp_ref, sems
):
    copies = weight_copies(w_hbm, w_ref, sems, range(QKV_CHUNKS, W_CHUNKS))
    for c in copies:
        c.start()
    for r in range(0, T, ROWS):
        go_ref[r : r + ROWS, :] = (
            cot_ref[r : r + ROWS, :].astype(f32) * mod_ref[5:6, :]
        ).astype(bf16)
    for j in range(0, D, PART):
        gof_ref[j : j + PART, :] = go_ref[:, j : j + PART].astype(f32).T
    gather_rows(gof_ref, tmp_ref, mine_ref, theirs_ref, P_ROWS)
    for c in copies:
        c.wait()
    grad_heads(w_ref, go_ref, heads_ref)


def gather_rows(src_ref, tmp_ref, mine_ref, theirs_ref, rows):
    me = lax.axis_index("seq") % 2
    tmp_ref[...] = jnp.zeros_like(tmp_ref)
    for core in range(2):
        for chunk in range(SUBS):
            slot = (core * SUBS + chunk) % 2
            for sub in range(SUBS):
                start = rows * owner_of(core, chunk, sub)
                tmp_ref[slot, rows * sub : rows * (sub + 1), :] = src_ref[start : start + rows, :]
            low = tmp_ref[slot].astype(bf16)

            @pl.when(me == core)
            def _(chunk=chunk, low=low):
                mine_ref[chunk] = low

            @pl.when(me != core)
            def _(chunk=chunk, low=low):
                theirs_ref[chunk] = low


def temporal_kernel(
    m_ref, cot_ref, g_ref, mod_ref, w_hbm,
    gm_ref, hid_ref, attn_out_ref, mine_ref, theirs_ref,
    w_ref, qk_ref, v_ref, attn_ref, grad_ref, gh_ref, tmp_ref, sems,
):
    copies = weight_copies(w_hbm, w_ref, sems, range(QKV_CHUNKS))
    for c in copies:
        c.start()
    modulated(m_ref, mod_ref, 3, 4, hid_ref)
    qkv_heads(copies, w_ref, hid_ref, qk_ref, v_ref)

    def group(i, _):
        heads = [i * GROUP + s for s in range(GROUP)]
        scores = [blocks(dot(qk_ref[HEADS + h, :HEAD], qk_ref[h, :HEAD], TN)) for h in heads]
        raws = [jnp.exp2(sc - jnp.max(sc, axis=0, keepdims=True)) for sc in scores]
        probs = [raw * (1.0 / jnp.sum(raw, axis=0, keepdims=True)) for raw in raws]
        lows = [spread(prob) for prob in probs]
        grad_probs = [blocks(dot(v_ref[h], g_ref[h], TN)) for h in heads]
        for h, prob, low, gp in zip(heads, probs, lows, grad_probs):
            inner = jnp.sum(prob * gp, axis=0, keepdims=True)
            grad_score = spread(prob * (gp - inner))
            dq, dk = score_grads(qk_ref[h, :HEAD], qk_ref[HEADS + h, :HEAD], grad_score)
            dv = dot(g_ref[h], low, NT)
            attn_ref[pl.ds(pl.multiple_of(h * HEAD, 8), HEAD), :] = dot(v_ref[h], low)
            for n, value in enumerate((dq, dk, dv)):
                grad_ref[pl.ds(pl.multiple_of(n * D + h * HEAD, 8), HEAD), :] = value
        return _

    lax.fori_loop(0, HEADS // GROUP, group, 0)
    gh_ref[...] = dot(grad_ref[...].astype(bf16).T, w_ref[: 3 * D, :])
    norm_back_rows(m_ref, cot_ref, gh_ref, mod_ref, 4, gm_ref)
    attn_out_ref[...] = attn_ref[...].astype(bf16).T
    gather_rows(grad_ref, tmp_ref, mine_ref, theirs_ref, Q_ROWS)


def first_lanes():
    return lax.broadcasted_iota(jnp.int32, (FRAMES, 2 * FRAMES), 1) < FRAMES


def blocks(full):
    f, lane = FRAMES, first_lanes()
    left = jnp.where(lane, full[:f, : 2 * f], full[f : 2 * f, : 2 * f])
    right = jnp.where(lane, full[2 * f : 3 * f, 2 * f :], full[3 * f :, 2 * f :])
    return jnp.concatenate([left, right], axis=1)


def spread(side):
    lane = first_lanes()
    zero = jnp.zeros((FRAMES, 2 * FRAMES), f32)
    a, b = side[:, : 2 * FRAMES], side[:, 2 * FRAMES :]
    left = jnp.concatenate([jnp.where(lane, a, zero), jnp.where(lane, zero, a), zero, zero], axis=0)
    right = jnp.concatenate([zero, zero, jnp.where(lane, b, zero), jnp.where(lane, zero, b)], axis=0)
    return jnp.concatenate([left, right], axis=1).astype(bf16)


def own_bits():
    seq, rep = lax.axis_index("seq"), lax.axis_index("rep")
    core = seq % 2
    ring = (rep * 2 + seq // 32, (seq // 2) % 4, (seq // 8) % 4)
    codes = [v ^ (v >> 1) for v in ring]
    first = [jnp.where(core == 0, v & 1, v >> 1) for v in codes]
    last = [jnp.where(core == 0, v >> 1, v & 1) for v in codes]
    return first, last


def weight_grad_kernel(
    flip,
    q1_ref, q2_ref, p1_ref, p2_ref, h1_ref, h2_ref, a1_ref, a2_ref,
    out0_ref, out1_ref, out2_ref,
    ql_ref, pl_ref, h_ref, a_ref,
):
    first, _ = own_bits()
    h_ref[:T, :] = h1_ref[...]
    h_ref[T:, :] = h2_ref[...]
    a_ref[:T, :] = a1_ref[...]
    a_ref[T:, :] = a2_ref[...]
    for p, out_ref in enumerate((out0_ref, out1_ref, out2_ref)):
        for i in range(4):
            bits = [None] * 3
            bits[p] = first[p] ^ flip
            bits[(p + 1) % 3] = i >> 1
            bits[(p + 2) % 3] = i & 1
            j = 4 * bits[0] + 2 * bits[1] + bits[2]
            rows = slice(i * Q_PAD, (i + 1) * Q_PAD)
            ql_ref[rows, :T] = q1_ref[j]
            ql_ref[rows, T:] = q2_ref[j]
            rows = slice(i * P_PAD, (i + 1) * P_PAD)
            pl_ref[rows, :T] = p1_ref[j]
            pl_ref[rows, T:] = p2_ref[j]
        cols = slice(p * PART, (p + 1) * PART)
        q = dot(ql_ref[...], h_ref[:, cols])
        o = dot(pl_ref[...], a_ref[:, cols])
        for i in range(4):
            out_ref[i] = jnp.concatenate(
                [q[i * Q_PAD : i * Q_PAD + Q_CHUNK], o[i * P_PAD : i * P_PAD + P_CHUNK]], axis=0
            ).astype(bf16)


def spatial_attention_back_kernel(
    gm_ref, mod_ref, inv_ref, kept_hbm, raw_hbm, w_hbm, grad_ref,
    w_ref, go_ref, g_ref, kept_ref, raw_ref, sems, in_sems,
):
    copies = weight_copies(w_hbm, w_ref, sems, range(QKV_CHUNKS, W_CHUNKS))
    kept = [
        pltpu.make_async_copy(kept_hbm.at[pl.ds(0, 4 * HEADS)], kept_ref, in_sems.at[0]),
        pltpu.make_async_copy(raw_hbm.at[pl.ds(0, HEADS)], raw_ref, in_sems.at[1]),
    ]
    for c in copies + kept:
        c.start()
    for r in range(0, T, ROWS):
        go_ref[r : r + ROWS, :] = (
            gm_ref[r : r + ROWS, :].astype(f32) * mod_ref[2:3, :]
        ).astype(bf16)
    for c in copies:
        c.wait()
    grad_heads(w_ref, go_ref, g_ref)
    for c in kept:
        c.wait()

    def group(i, _):
        heads = [i * GROUP + s for s in range(GROUP)]
        scaled, grad_probs, inners = [], [], []
        for h in heads:
            g = (g_ref[h].astype(f32) * inv_ref[h]).astype(bf16)
            scaled.append(g)
            out = kept_ref[3 * HEADS + h, :HEAD].astype(f32)
            inners.append(jnp.sum(g.astype(f32) * out, axis=0, keepdims=True))
            grad_probs.append(dot(kept_ref[2 * HEADS + h, :HEAD], g, TN))
        for h, g, inner, gp in zip(heads, scaled, inners, grad_probs):
            raw = raw_ref[h]
            grad_score = (raw.astype(f32) * (gp - inner)).astype(bf16)
            dq, dk = score_grads(kept_ref[h, :HEAD], kept_ref[HEADS + h, :HEAD], grad_score)
            for n, value in enumerate((dq, dk, dot(g, raw, NT))):
                grad_ref[n * HEADS + h] = value.astype(bf16)
        return _

    lax.fori_loop(0, HEADS // GROUP, group, 0)


def spatial_norm_back_kernel(grad_ref, gm_ref, x_ref, mod_ref, w_hbm, out_ref, w_ref, cat_ref, gh_ref, sems):
    copies = weight_copies(w_hbm, w_ref, sems, range(QKV_CHUNKS))
    for c in copies:
        c.start()
    for h in range(0, 3 * HEADS, 2):
        pair = jnp.concatenate([grad_ref[h].astype(f32), grad_ref[h + 1].astype(f32)], axis=0)
        cat_ref[h * HEAD : (h + 2) * HEAD, :] = pair.astype(bf16)
    flipped = cat_ref[...].T
    for c in copies:
        c.wait()
    gh_ref[...] = dot(flipped, w_ref[: 3 * D, :])
    norm_back_rows(x_ref, gm_ref, gh_ref, mod_ref, 1, out_ref)


def chunk_bits():
    first, _ = own_bits()
    return [(first[(p + 1) % 3], first[(p + 2) % 3]) for p in range(3)]


def second_send_kernel(*refs):
    keep, got, out = refs[0:3], refs[3:6], refs[7:10]
    for p, (a, _) in enumerate(chunk_bits()):
        for j in range(2):
            i = 2 * (1 - a) + j
            out[p][j] = (keep[p][i].astype(f32) + got[p][i].astype(f32)).astype(bf16)


def third_send_kernel(*refs):
    keep, got, more, out = refs[0:3], refs[3:6], refs[6:9], refs[10:13]
    for p, (a, b) in enumerate(chunk_bits()):
        i = 2 * a + 1 - b
        out[p][...] = (
            keep[p][i].astype(f32) + got[p][i].astype(f32) + more[p][1 - b].astype(f32)
        ).astype(bf16)


Q_HALVES = (Q_CHUNK // 2, Q_CHUNK // 4, Q_CHUNK // 8)
P_HALVES = (P_CHUNK // 2, P_CHUNK // 4, P_CHUNK // 8)


def split_halves(total_ref, bit, q_rows, p_rows, half_ref, keep_ref, send_ref):
    total = 2 * q_rows + 2 * p_rows
    for side in range(2):
        q, p = side * q_rows, 2 * q_rows + side * p_rows
        half_ref[side, :q_rows] = total_ref[q : q + q_rows, :]
        half_ref[side, q_rows : total // 2] = total_ref[p : p + p_rows, :]
    keep_ref[...] = half_ref[bit]
    send_ref[...] = half_ref[1 - bit].astype(bf16)


def fourth_send_kernel(*refs):
    keep, got, more, most = refs[0:3], refs[3:6], refs[6:9], refs[9:12]
    own_ref, send_ref, row_ref, half_ref = refs[12:16]
    for p, (a, b) in enumerate(chunk_bits()):
        i = 2 * a + b
        row_ref[:, p * PART : (p + 1) * PART] = (
            keep[p][i].astype(f32) + got[p][i].astype(f32) + more[p][b].astype(f32)
        ) + most[p][...].astype(f32)
    split_halves(row_ref, own_bits()[1][0], Q_HALVES[0], P_HALVES[0], half_ref, own_ref, send_ref)


def later_send_kernel(step, own_in, got_ref, own_ref, send_ref, row_ref, half_ref):
    row_ref[...] = own_in[...] + got_ref[...].astype(f32)
    split_halves(row_ref, own_bits()[1][step], Q_HALVES[step], P_HALVES[step], half_ref, own_ref, send_ref)


def last_sum_kernel(own_ref, got_ref, q_ref, p_ref):
    total = own_ref[...] + got_ref[...].astype(f32)
    q_ref[...] = total[:Q_ROWS]
    p_ref[...] = total[Q_ROWS:]


VMEM = pl.BlockSpec(memory_space=pltpu.VMEM)
ANY = pl.BlockSpec(memory_space=pl.ANY)


def call(kernel, outs, scratch, specs, flops, name, out_specs=None, limit=54):
    return pl.pallas_call(
        kernel,
        out_shape=[jax.ShapeDtypeStruct(s, d) for s, d in outs],
        in_specs=specs,
        out_specs=out_specs or [VMEM] * len(outs),
        scratch_shapes=scratch,
        compiler_params=pltpu.CompilerParams(vmem_limit_bytes=limit * 1024 * 1024),
        cost_estimate=pl.CostEstimate(flops=flops, bytes_accessed=12_000_000 if flops > 1_000_000_000 else 1_000, transcendentals=0),
        name=name,
    )


WEIGHT = pltpu.VMEM((4 * D, D), bf16)
W_QKV = pltpu.VMEM((3 * D, D), bf16)
W_OUT = pltpu.VMEM((D, D), bf16)
SEMS = pltpu.SemaphoreType.DMA((W_CHUNKS,))
QK = ((2 * HEADS, V_ROWS, T), bf16)
V = ((HEADS, V_ROWS, T), bf16)
HEAD_ROWS = ((HEADS, HEAD, T), bf16)
TOKENS = ((T, D), bf16)


RAW = ((HEADS, T, T), bf16)


def spatial_forward(x, mod, w):
    return call(
        spatial_forward_kernel,
        [TOKENS, KEPT, KEPT_RAW, ((HEADS, 1, T), f32)],
        [
            WEIGHT,
            pltpu.VMEM(*TOKENS),
            pltpu.VMEM((D, T), f32),
            pltpu.VMEM(*QK),
            pltpu.VMEM(*V),
            pltpu.VMEM(*V),
            pltpu.VMEM(*RAW),
            SEMS,
            pltpu.SemaphoreType.DMA((3 + HEADS // GROUP,)),
        ],
        [VMEM, VMEM, ANY],
        6_000_000_000,
        "spatial_forward",
        [VMEM, ANY, ANY, VMEM],
    )(x, mod, w)


def cotangent(cot, mod, w):
    rows = ((SUBS, P_PAD, T), bf16)
    return call(
        cotangent_kernel,
        [HEAD_ROWS, rows, rows],
        [W_OUT, pltpu.VMEM(*TOKENS), pltpu.VMEM((D, T), f32), pltpu.VMEM((2, P_PAD, T), f32), SEMS],
        [VMEM, VMEM, ANY],
        2_000_000_000,
        "cotangent_heads",
    )(cot, mod, w)


def temporal(m, cot, g, mod, w):
    rows = ((SUBS, Q_PAD, T), bf16)
    return call(
        temporal_kernel,
        [TOKENS, TOKENS, TOKENS, rows, rows],
        [
            W_QKV,
            pltpu.VMEM(*QK),
            pltpu.VMEM(*HEAD_ROWS),
            pltpu.VMEM((D, T), f32),
            pltpu.VMEM((3 * D, T), f32),
            pltpu.VMEM((T, D), f32),
            pltpu.VMEM((2, Q_PAD, T), f32),
            SEMS,
        ],
        [VMEM, VMEM, VMEM, VMEM, ANY],
        12_000_000_000,
        "temporal_sublayer",
    )(m, cot, g, mod, w)


def weight_grad(flip, *operands):
    return call(
        functools.partial(weight_grad_kernel, flip),
        [((4, CHUNK, PART), bf16)] * 3,
        [
            pltpu.VMEM((4 * Q_PAD, 2 * T), bf16),
            pltpu.VMEM((4 * P_PAD, 2 * T), bf16),
            pltpu.VMEM((2 * T, D), bf16),
            pltpu.VMEM((2 * T, D), bf16),
        ],
        [VMEM] * 8,
        10_000_000,
        "weight_grad_send" if flip else "weight_grad_keep",
        limit=20,
    )(*operands)


def spatial_attention_back(gm, mod, kept, raw, inv, w):
    return call(
        spatial_attention_back_kernel,
        [((3 * HEADS, HEAD, T), bf16)],
        [
            W_OUT,
            pltpu.VMEM(*TOKENS),
            pltpu.VMEM(*HEAD_ROWS),
            pltpu.VMEM((4 * HEADS, V_ROWS, T), bf16),
            pltpu.VMEM(*RAW),
            SEMS,
            pltpu.SemaphoreType.DMA((2,)),
        ],
        [VMEM] * 3 + [ANY] * 3,
        5_000_000_000,
        "spatial_attention_back",
    )(gm, mod, inv, kept, raw, w)[0]


def spatial_norm_back(grad, gm, x, mod, w):
    return call(
        spatial_norm_back_kernel,
        [TOKENS],
        [W_QKV, pltpu.VMEM((3 * D, T), bf16), pltpu.VMEM((T, D), f32), SEMS],
        [VMEM] * 4 + [ANY],
        5_000_000_000,
        "spatial_norm_back",
    )(grad, gm, x, mod, w)[0]


def to_positions(tokens):
    got = lax.all_to_all(tokens.reshape(FRAMES, PLACE, D), "seq", 0, 0, tiled=True)
    return got.transpose(1, 0, 2).reshape(T, D)


def to_frames(tokens):
    sent = tokens.reshape(PLACE, FRAMES, D).transpose(1, 0, 2)
    return lax.all_to_all(sent, "seq", 0, 0, tiled=True).reshape(T, D)


def reduce_rows(send, keep, before_second, before_third):
    half, one = ((2, CHUNK, PART), bf16), ((CHUNK, PART), bf16)
    got = [lax.ppermute(send[p], BOTH, flip_pairs(p, (0, 1))) for p in range(3)]
    out = call(second_send_kernel, [half] * 3, [], [VMEM] * 6 + [ANY], 1_000_000, "second_send", limit=12)(
        *keep, *got, before_second
    )
    more = [lax.ppermute(out[p], BOTH, flip_pairs((p + 1) % 3, (0, 1))) for p in range(3)]
    out = call(third_send_kernel, [one] * 3, [], [VMEM] * 9 + [ANY], 1_000_000, "third_send", limit=12)(
        *keep, *got, *more, before_third
    )
    most = [lax.ppermute(out[p], BOTH, flip_pairs((p + 2) % 3, (0, 1))) for p in range(3)]
    for step in range(3):
        rows = Q_HALVES[step] + P_HALVES[step]
        kernel = fourth_send_kernel if step == 0 else functools.partial(later_send_kernel, step)
        operands = (*keep, *got, *more, *most) if step == 0 else (own, moved)
        own, sent = call(
            kernel,
            [((rows, D), f32), ((rows, D), bf16)],
            [pltpu.VMEM((2 * rows, D), f32), pltpu.VMEM((2, rows, D), f32)],
            [VMEM] * len(operands),
            1_000_000,
            "later_send",
            limit=16,
        )(*operands)
        moved = lax.ppermute(sent, BOTH, flip_pairs(step, (1, 0)))
    return call(
        last_sum_kernel,
        [((Q_ROWS, D), f32), ((P_ROWS, D), f32)],
        [],
        [VMEM] * 2,
        1_000_000,
        "last_sum",
        limit=8,
    )(own, moved)


def on_device(clip_tokens, modulation, spatial_weights, temporal_weights, out_cotangent):
    x = clip_tokens.reshape(T, D)
    cot = out_cotangent.reshape(T, D)
    mod = modulation.reshape(6, D)
    cot_pos = to_positions(cot)
    middle, kept, raw, inv = spatial_forward(x, mod, spatial_weights)
    middle_pos = to_positions(middle)
    grad_attn, mine_p, theirs_p = cotangent(cot_pos, mod, temporal_weights)
    gm_pos, hidden, attn, mine_q, theirs_q = temporal(
        middle_pos, cot_pos, grad_attn, mod, temporal_weights
    )
    gm = to_frames(gm_pos)

    def other(v):
        return lax.ppermute(v, BOTH, core_pairs())

    operands = (mine_q, other(theirs_q), mine_p, other(theirs_p), hidden, other(hidden), attn, other(attn))
    send = weight_grad(1, *operands)
    keep = weight_grad(0, *operands)
    grad = spatial_attention_back(gm, mod, kept, raw, inv, spatial_weights)
    input_grad = spatial_norm_back(grad, gm, x, mod, spatial_weights)
    qkv_rows, proj_rows = reduce_rows(send, keep, grad, input_grad)
    return input_grad.reshape(clip_tokens.shape), qkv_rows, proj_rows


def solution(mesh):
    placed = (
        P("rep", "seq", None, None),
        P("rep", None, None),
        P(),
        P(),
        P("rep", "seq", None, None),
    )
    return jax.shard_map(
        on_device,
        mesh=mesh,
        in_specs=placed,
        out_specs=(P("rep", "seq", None, None), P(BOTH, None), P(BOTH, None)),
        check_vma=False,
    )
```

time: 177 us -> 156 us (0.88)
  Pallas kernels: 79.2 us -> 60.6 us
  other arithmetic: 3.75 us -> 0 us
  waiting for transfers between devices: 27.9 us -> 30.6 us
    pallas_call x6 -> x13, Pallas kernels: 79.2 us -> 60.6 us  [the longest x1 17.7 us: temporal(): call(temporal_kernel, [TOKENS, TOKENS, TOKENS, rows, rows], [W_QKV, pltpu...]
    ppermute x12, waiting for transfers between devices: 9.34 us -> 18.7 us  [the longest x3 13.9 us: reduce_rows(): moved = lax.ppermute(sent, BOTH, flip_pairs(step, (1, 0)))]
    slice x5 -> x0, local copies, waits for them, and re-layouts: 6.59 us -> none  [the longest x1 3.27 us: reduce_rows(): got = lax.ppermute(send[4 * p:4 * p + 4], BOTH, flip_pairs(p, (0, 1)))]
    unnamed x17 -> x35, local copies, waits for them, and re-layouts: 2.46 us -> 8.81 us
    all_to_all x3, waiting for transfers between devices: 15.8 us -> 11.9 us  [the longest x2 11.5 us: to_positions(): lax.all_to_all(tokens.reshape(FRAMES, PLACE, D), 'seq', 0, 0, tiled=True)]
    convert_element_type x8 -> x0, other arithmetic: 3.32 us -> none  [the longest x6 3.13 us: summed(): return (a.astype(f32) + b.astype(f32)).astype(bf16)]
    ppermute x4, waiting for transfers between devices: 2.81 us -> 0.01 us  [other(): return lax.ppermute(v, BOTH, core_pairs())]
    squeeze x4 -> x0, local copies, waits for them, and re-layouts: 2.34 us -> none  [pick(): return lax.dynamic_index_in_dim(array, index, 0, keepdims=False)]
  transfers between devices with their start and end apart: 19 -> 19, of which waited for: 9 -> 8; matrix products, arithmetic and copies ran while one was open for 7% -> 6% of each run, Pallas kernels for 26% -> 23%
where the time goes in v2:
time: 156 us; the launch traced here: 155 us
  Pallas kernels  60.6 us (39%)
  starting transfers between devices  43.2 us (28%)
  waiting for transfers between devices  30.6 us (20%)
  local copies, waits for them, and re-layouts  19.8 us (13%)
    all_to_all x2, starting transfers between devices, to_positions(): lax.all_to_all(tokens.reshape(FRAMES, PLACE, D), 'seq', 0, 0, tiled=True)  18.9 us
    pallas_call x1, Pallas kernels, temporal(): call(temporal_kernel, [TOKENS, TOKENS, TOKENS, rows, rows], [W_QKV, pltpu...  17.7 us
    ppermute x3, waiting for transfers between devices, reduce_rows(): moved = lax.ppermute(sent, BOTH, flip_pairs(step, (1, 0)))  13.9 us
    pallas_call x1, Pallas kernels, spatial_forward(): call(spatial_forward_kernel, [TOKENS, KEPT, KEPT_RAW, ((HEADS, 1, T), f32...  12.5 us
    all_to_all x2, waiting for transfers between devices, to_positions(): lax.all_to_all(tokens.reshape(FRAMES, PLACE, D), 'seq', 0, 0, tiled=True)  11.5 us
    pallas_call x1, Pallas kernels, spatial_attention_back(): call(spatial_attention_back_kernel, [((3 * HEADS, HEAD, T), bf16)], [W_OU...  9.19 us
    pallas_call x1, Pallas kernels, spatial_norm_back(): call(spatial_norm_back_kernel, [TOKENS], [W_QKV, pltpu.VMEM((3 * D, T), b...  8.92 us
    unnamed x35, local copies, waits for them, and re-layouts  8.81 us
  transfers between devices with their start and end apart: 19, of which 8 were waited for; matrix products, arithmetic and copies ran while one was open for 6% of the time, Pallas kernels for 23%

profile of v2, /device:TPU:0, one launch (start us, length us, event | category | flops | bytes accessed | tf_op | source)
XLA Modules:
  0.0 155.2 jit_solution(10067734097982730943)
XLA Ops:
  0.6 2.3 %reshape_reshape.3 = bf16[64,4,1152]{2,1,0:T(4,128)(2,1)} reshape(bf16[1,1,256,1152]{3,2,1,0:T(8,128)(2,1)} %param.9) | data formatting | bytes 1179648 | tf_op jit(solution)/shard_map/reshape;reshape | solution.py:585
  2.9 10.0 %all-to-all-start.1 = ((bf16[64,4,1152]{2,1,0:T(4,128)(2,1)}), bf16[64,4,1152]{2,1,0:T(4,128)(2,1)S(1)}, u32[]{:S(2)}, u32[]{:S(2)}) async-start(bf16[64,4,1152]{2,1,0:T(4,128)(2,1)} %reshape_reshape.3), calls=%async_computation.1 | async-start | bytes 1179648 | tf_op jit(solution)/shard_map/all_to_all | solution.py:585
  12.9 1.4 copy.18
  14.2 12.5 %spatial_forward.1 = (bf16[256,1152]{1,0:T(8,128)(2,1)}, bf16[280,80,256]{2,1,0:T(8,128)(2,1)}, bf16[88,256,256]{2,1,0:T(8,128)(2,1)}, f32[16,1,256]{2,1,0:T(1,128)}) custom-call(bf16[256,1152]{1,0:T(8,128)(2,1)} %bitcast.28, f32[6,1152]{1,0:T(8,128)} %bitcast.23, bf16[4608,1152]{1,0:T(8,128)(2,1)} %w_hbm.9), custom_call_target="tpu_custom_call" | custom-call | flops 6000000000 | bytes 12000000 | tf_op jit(solution)/shard_map/spatial_forward/pallas_call | solution.py:483
  26.7 2.3 %reshape.32 = bf16[64,4,1152]{2,1,0:T(4,128)(2,1)} reshape(bf16[256,1152]{1,0:T(8,128)(2,1)} %get-tuple-element.35) | data formatting | bytes 1179648 | tf_op jit(solution)/shard_map/reshape | solution.py:585
  29.1 0.0 all-to-all-done.1
  29.1 8.9 %all-to-all-start = ((bf16[64,4,1152]{2,1,0:T(4,128)(2,1)}), bf16[64,4,1152]{2,1,0:T(4,128)(2,1)S(1)}, u32[]{:S(2)}, u32[]{:S(2)}) async-start(bf16[64,4,1152]{2,1,0:T(4,128)(2,1)} %reshape.32), calls=%async_computation | async-start | bytes 1179648 | tf_op jit(solution)/shard_map/all_to_all | solution.py:585
  38.0 0.9 copy.12
  38.9 11.5 %all-to-all-done = bf16[64,4,1152]{2,1,0:T(4,128)(2,1)S(1)} async-done(((bf16[64,4,1152]{2,1,0:T(4,128)(2,1)}), bf16[64,4,1152]{2,1,0:T(4,128)(2,1)S(1)}, u32[]{:S(2)}, u32[]{:S(2)}) %all-to-all-start) | async-done | bytes 589856 | tf_op jit(solution)/shard_map/all_to_all | solution.py:585
  50.4 0.9 copy.11
  51.3 4.8 %cotangent_heads.1 = (bf16[16,72,256]{2,1,0:T(8,128)(2,1)}, bf16[8,80,256]{2,1,0:T(8,128)(2,1)}, bf16[8,80,256]{2,1,0:T(8,128)(2,1)}) custom-call(bf16[256,1152]{1,0:T(8,128)(2,1)} %bitcast.16, f32[6,1152]{1,0:T(8,128)} %bitcast.24, bf16[4608,1152]{1,0:T(8,128)(2,1)} %w_hbm.7), custom_call_target="tpu_custom_call" | custom-call | flops 2000000000 | bytes 12000000 | tf_op jit(solution)/shard_map/cotangent_heads/pallas_call | solution.py:506
  56.1 17.7 %temporal_sublayer.1 = (bf16[256,1152]{1,0:T(8,128)(2,1)}, bf16[256,1152]{1,0:T(8,128)(2,1)}, bf16[256,1152]{1,0:T(8,128)(2,1)}, bf16[8,224,256]{2,1,0:T(8,128)(2,1)}, bf16[8,224,256]{2,1,0:T(8,128)(2,1)}) custom-call(bf16[256,1152]{1,0:T(8,128)(2,1)} %bitcast.22, bf16[256,1152]{1,0:T(8,128)(2,1)} %bitcast.17, bf16[16,72,256]{2,1,0:T(8,128)(2,1)} %get-tuple-element.36.g_ref, ...), custom_call_target="tpu_custom_call" | custom-call | flops 12000000000 | bytes 12000000 | tf_op jit(solution)/shard_map/temporal_sublayer/pallas_call | solution.py:518
  73.7 0.5 collective-permute-start
  74.2 0.1 collective-permute-start.2
  74.3 0.4 collective-permute-start.3
  74.7 0.1 collective-permute-start.1
  74.8 2.3 %copy.17 = bf16[4,64,1152]{2,0,1:T(4,128)(2,1)} copy(bf16[4,64,1152]{2,1,0:T(8,128)(2,1)} %bitcast.21) | data formatting | bytes 1179648 | tf_op jit(solution)/shard_map/reshape | solution.py:590
  77.2 5.7 %all-to-all-start.2 = ((bf16[64,4,1152]{2,1,0:T(4,128)(2,1)}), bf16[64,4,1152]{2,1,0:T(4,128)(2,1)}, u32[]{:S(2)}, u32[]{:S(2)}) async-start(bf16[64,4,1152]{2,1,0:T(4,128)(2,1)} %bitcast.18), calls=%async_computation.2 | async-start | bytes 1179648 | tf_op jit(solution)/shard_map/all_to_all | solution.py:591
  82.8 0.0 collective-permute-done.1.p2_ref
  82.9 0.0 collective-permute-done.2.h2_ref
  82.9 0.0 collective-permute-done.3.a2_ref
  82.9 0.0 collective-permute-done.q2_ref
  82.9 1.8 %copy-done.1 = bf16[8,224,256]{2,1,0:T(8,128)(2,1)S(1)} copy-done((bf16[8,224,256]{2,1,0:T(8,128)(2,1)S(1)}, bf16[8,224,256]{2,1,0:T(8,128)(2,1)}, u32[]{:S(2)}) %copy-start.1) | copy-done | bytes 917528
  84.7 1.1 copy-done.5
  85.8 1.1 copy-done.7
  86.8 3.3 %weight_grad_send.1 = (bf16[4,288,384]{2,1,0:T(8,128)(2,1)}, bf16[4,288,384]{2,1,0:T(8,128)(2,1)}, bf16[4,288,384]{2,1,0:T(8,128)(2,1)}) custom-call(bf16[8,224,256]{2,1,0:T(8,128)(2,1)S(1)} %copy-done.1, bf16[8,224,256]{2,1,0:T(8,128)(2,1)S(1)} %collective-permute-done.q2_ref, bf16[8,80,256]{2,1,0:T(8,128)(2,1)S(1)} %copy-done.11, ...), custom_call_target="tpu_custom_call" | custom-call | flops 10000000 | bytes 1000 | tf_op jit(solution)/shard_map/weight_grad_send/pallas_call | solution.py:538
  90.2 1.4 collective-permute-start.4
  91.6 1.5 collective-permute-start.5
  93.1 1.5 collective-permute-start.6
  94.6 0.4 all-to-all-done.2
  94.9 2.2 %reshape.36.gm_ref = bf16[256,1152]{1,0:T(8,128)(2,1)} reshape(bf16[64,4,1152]{2,1,0:T(4,128)(2,1)} %all-to-all-done.2) | data formatting | bytes 1179648 | tf_op jit(solution)/shard_map/reshape | solution.py:591
  97.2 9.2 %spatial_attention_back.1.grad_ref.refs_6_ = bf16[48,72,256]{2,1,0:T(8,128)(2,1)} custom-call(bf16[256,1152]{1,0:T(8,128)(2,1)} %reshape.36.gm_ref, f32[6,1152]{1,0:T(8,128)} %bitcast.26, f32[16,1,256]{2,1,0:T(1,128)} %get-tuple-element.38.inv_ref, bf16[280,80,256]{2,1,0:T(8,128)(2,1)} %get-tuple-element.39.kept_hbm, ...), custom_call_target="tpu_custom_call" | custom-call | flops 5000000000 | bytes 12000000 | tf_op jit(solution)/shard_map/spatial_attention_back/pallas_call | solution.py:555
  106.4 1.0 copy-done.14
  107.4 2.2 %weight_grad_keep.1 = (bf16[4,288,384]{2,1,0:T(8,128)(2,1)S(1)}, bf16[4,288,384]{2,1,0:T(8,128)(2,1)S(1)}, bf16[4,288,384]{2,1,0:T(8,128)(2,1)S(1)}) custom-call(bf16[8,224,256]{2,1,0:T(8,128)(2,1)S(1)} %copy-done.2, bf16[8,224,256]{2,1,0:T(8,128)(2,1)S(1)} %copy-done.4, bf16[8,80,256]{2,1,0:T(8,128)(2,1)S(1)} %copy-done.12, ...), custom_call_target="tpu_custom_call" | custom-call | flops 10000000 | bytes 1000 | tf_op jit(solution)/shard_map/weight_grad_keep/pallas_call | solution.py:538
  109.6 0.0 collective-permute-done.4.refs_3_
  109.6 0.0 collective-permute-done.5.refs_4_
  109.6 0.0 collective-permute-done.6.refs_5_
  109.6 1.5 copy-done
  111.1 0.3 second_send.1
  111.4 1.0 collective-permute-start.7
  112.4 0.4 collective-permute-start.8
  112.8 1.8 %collective-permute-start.9 = (bf16[2,288,384]{2,1,0:T(8,128)(2,1)S(1)}, bf16[2,288,384]{2,1,0:T(8,128)(2,1)S(1)}, u32[]{:S(2)}, u32[]{:S(2)}) collective-permute-start(bf16[2,288,384]{2,1,0:T(8,128)(2,1)S(1)} %get-tuple-element.55), channel_id=1, source_target_pairs={{0,64},{2,67},{16,80},{18,83},{32,96},{34,99},{48,112},{50,115},{4... | collective-permute-start | bytes 1327112 | tf_op jit(solution)/shard_map/ppermute | solution.py:600
  114.5 8.9 %spatial_norm_back.1.refs_9_ = bf16[256,1152]{1,0:T(8,128)(2,1)} custom-call(bf16[48,72,256]{2,1,0:T(8,128)(2,1)} %spatial_attention_back.1.grad_ref.refs_6_, bf16[256,1152]{1,0:T(8,128)(2,1)} %reshape.36.gm_ref, bf16[256,1152]{1,0:T(8,128)(2,1)} %bitcast.29, f32[6,1152]{1,0:T(8,128)} %bitcast.27, bf16[4608,1152]{1,0:T(8,128)(2,1)} %w_hbm.9), custom_call_target="tpu_custom_call" | custom-call | flops 5000000000 | bytes 12000000 | tf_op jit(solution)/shard_map/spatial_norm_back/pallas_call | solution.py:574
  123.5 0.0 collective-permute-done.7.refs_6_
  123.5 0.0 collective-permute-done.9.refs_8_
  123.5 0.0 copy-start.15
  123.5 1.1 copy-done.15
  124.6 0.2 third_send.1
  124.8 1.5 collective-permute-start.10
  126.3 0.6 collective-permute-start.11
  126.8 1.1 collective-permute-start.12
  127.9 2.9 %collective-permute-done.10.refs_9_ = bf16[288,384]{1,0:T(8,128)(2,1)S(1)} collective-permute-done((bf16[288,384]{1,0:T(8,128)(2,1)S(1)}, bf16[288,384]{1,0:T(8,128)(2,1)S(1)}, u32[]{:S(2)}, u32[]{:S(2)}) %collective-permute-start.10) | collective-permute-done | bytes 221216 | tf_op jit(solution)/shard_map/ppermute | solution.py:604
  130.8 1.4 collective-permute-done.11.refs_10_
  132.2 0.6 collective-permute-done.12.refs_11_
  132.7 0.6 later_send.3
  133.3 2.8 %collective-permute-start.13 = (bf16[144,1152]{1,0:T(8,128)(2,1)S(1)}, bf16[144,1152]{1,0:T(8,128)(2,1)S(1)}, u32[]{:S(2)}, u32[]{:S(2)}) collective-permute-start(bf16[144,1152]{1,0:T(8,128)(2,1)S(1)} %get-tuple-element.60), channel_id=1, source_target_pairs={{0,65},{2,66},{16,81},{18,82},{32,97},{34,98},{48,113},{50,114},{4... | collective-permute-start | bytes 995336 | tf_op jit(solution)/shard_map/ppermute | solution.py:618
  136.2 5.6 %collective-permute-done.13.got_ref = bf16[144,1152]{1,0:T(8,128)(2,1)S(1)} collective-permute-done((bf16[144,1152]{1,0:T(8,128)(2,1)S(1)}, bf16[144,1152]{1,0:T(8,128)(2,1)S(1)}, u32[]{:S(2)}, u32[]{:S(2)}) %collective-permute-start.13) | collective-permute-done | bytes 331808 | tf_op jit(solution)/shard_map/ppermute | solution.py:618
  141.8 0.2 later_send.4
  141.9 2.1 %collective-permute-start.14 = (bf16[72,1152]{1,0:T(8,128)(2,1)S(1)}, bf16[72,1152]{1,0:T(8,128)(2,1)S(1)}, u32[]{:S(2)}, u32[]{:S(2)}) collective-permute-start(bf16[72,1152]{1,0:T(8,128)(2,1)S(1)} %get-tuple-element.62), channel_id=1, source_target_pairs={{0,12},{2,6},{16,28},{18,22},{32,44},{34,38},{48,60},{50,54},{4,8}... | collective-permute-start | bytes 497672 | tf_op jit(solution)/shard_map/ppermute | solution.py:618
  144.0 4.5 %collective-permute-done.14.got_ref = bf16[72,1152]{1,0:T(8,128)(2,1)S(1)} collective-permute-done((bf16[72,1152]{1,0:T(8,128)(2,1)S(1)}, bf16[72,1152]{1,0:T(8,128)(2,1)S(1)}, u32[]{:S(2)}, u32[]{:S(2)}) %collective-permute-start.14) | collective-permute-done | bytes 165920 | tf_op jit(solution)/shard_map/ppermute | solution.py:618
  148.5 0.1 later_send.5
  148.6 2.0 %collective-permute-start.15 = (bf16[36,1152]{1,0:T(8,128)(2,1)S(1)}, bf16[36,1152]{1,0:T(8,128)(2,1)S(1)}, u32[]{:S(2)}, u32[]{:S(2)}) collective-permute-start(bf16[36,1152]{1,0:T(8,128)(2,1)S(1)} %get-tuple-element.64), channel_id=1, source_target_pairs={{0,48},{2,18},{16,32},{18,2},{32,16},{34,50},{48,0},{50,34},{4,52}... | collective-permute-start | bytes 248840 | tf_op jit(solution)/shard_map/ppermute | solution.py:618
  150.7 3.8 %collective-permute-done.15.got_ref = bf16[36,1152]{1,0:T(8,128)(2,1)S(1)} collective-permute-done((bf16[36,1152]{1,0:T(8,128)(2,1)S(1)}, bf16[36,1152]{1,0:T(8,128)(2,1)S(1)}, u32[]{:S(2)}, u32[]{:S(2)}) %collective-permute-start.15) | collective-permute-done | bytes 82976 | tf_op jit(solution)/shard_map/ppermute | solution.py:618
  154.5 0.7 last_sum.1
  (28 shorter events, 0.1 us)
Async XLA Ops:
  2.9 26.2 %all-to-all-start.1 = ((bf16[64,4,1152]{2,1,0:T(4,128)(2,1)}), bf16[64,4,1152]{2,1,0:T(4,128)(2,1)S(1)}, u32[]{:S(2)}, u32[]{:S(2)}) async-start(bf16[64,4,1152]{2,1,0:T(4,128)(2,1)} %reshape_reshape.3), calls=%async_computation.1 | async-start | bytes 1179648 | tf_op jit(solution)/shard_map/all_to_all | solution.py:585
  29.1 21.3 %all-to-all-start = ((bf16[64,4,1152]{2,1,0:T(4,128)(2,1)}), bf16[64,4,1152]{2,1,0:T(4,128)(2,1)S(1)}, u32[]{:S(2)}, u32[]{:S(2)}) async-start(bf16[64,4,1152]{2,1,0:T(4,128)(2,1)} %reshape.32), calls=%async_computation | async-start | bytes 1179648 | tf_op jit(solution)/shard_map/all_to_all | solution.py:585
  56.0 18.7 %copy-start.16 = (bf16[8,80,256]{2,1,0:T(8,128)(2,1)S(1)}, bf16[8,80,256]{2,1,0:T(8,128)(2,1)}, u32[]{:S(2)}) copy-start(bf16[8,80,256]{2,1,0:T(8,128)(2,1)} %get-tuple-element.44) | copy-start | bytes 983044
  56.0 26.9 %copy-start.11 = (bf16[8,80,256]{2,1,0:T(8,128)(2,1)S(1)}, bf16[8,80,256]{2,1,0:T(8,128)(2,1)}, u32[]{:S(2)}) copy-start(bf16[8,80,256]{2,1,0:T(8,128)(2,1)} %get-tuple-element.43.p1_ref) | copy-start | bytes 983044
  73.7 9.2 %collective-permute-start = (bf16[8,224,256]{2,1,0:T(8,128)(2,1)}, bf16[8,224,256]{2,1,0:T(8,128)(2,1)S(1)}, u32[]{:S(2)}, u32[]{:S(2)}) collective-permute-start(bf16[8,224,256]{2,1,0:T(8,128)(2,1)} %get-tuple-element.42), channel_id=1, source_target_pairs={{0,2},{2,0},{16,18},{18,16},{32,34},{34,32},{48,50},{50,48},{4,6},... | collective-permute-start | bytes 2752520 | tf_op jit(solution)/shard_map/ppermute | solution.py:644
  74.2 8.7 %collective-permute-start.2 = (bf16[256,1152]{1,0:T(8,128)(2,1)}, bf16[256,1152]{1,0:T(8,128)(2,1)S(1)}, u32[]{:S(2)}, u32[]{:S(2)}) collective-permute-start(bf16[256,1152]{1,0:T(8,128)(2,1)} %get-tuple-element.45.h1_ref), channel_id=1, source_target_pairs={{0,2},{2,0},{16,18},{18,16},{32,34},{34,32},{48,50},{50,48},{4,6},... | collective-permute-start | bytes 1769480 | tf_op jit(solution)/shard_map/ppermute | solution.py:644
  74.3 8.6 %collective-permute-start.3 = (bf16[256,1152]{1,0:T(8,128)(2,1)}, bf16[256,1152]{1,0:T(8,128)(2,1)S(1)}, u32[]{:S(2)}, u32[]{:S(2)}) collective-permute-start(bf16[256,1152]{1,0:T(8,128)(2,1)} %get-tuple-element.46.a1_ref), channel_id=1, source_target_pairs={{0,2},{2,0},{16,18},{18,16},{32,34},{34,32},{48,50},{50,48},{4,6},... | collective-permute-start | bytes 1769480 | tf_op jit(solution)/shard_map/ppermute | solution.py:644
  74.7 8.1 %collective-permute-start.1 = (bf16[8,80,256]{2,1,0:T(8,128)(2,1)S(1)}, bf16[8,80,256]{2,1,0:T(8,128)(2,1)S(1)}, u32[]{:S(2)}, u32[]{:S(2)}) collective-permute-start(bf16[8,80,256]{2,1,0:T(8,128)(2,1)S(1)} %copy-done.16), channel_id=1, source_target_pairs={{0,2},{2,0},{16,18},{18,16},{32,34},{34,32},{48,50},{50,48},{4,6},... | collective-permute-start | bytes 983048 | tf_op jit(solution)/shard_map/ppermute | solution.py:644
  77.2 17.8 %all-to-all-start.2 = ((bf16[64,4,1152]{2,1,0:T(4,128)(2,1)}), bf16[64,4,1152]{2,1,0:T(4,128)(2,1)}, u32[]{:S(2)}, u32[]{:S(2)}) async-start(bf16[64,4,1152]{2,1,0:T(4,128)(2,1)} %bitcast.18), calls=%async_computation.2 | async-start | bytes 1179648 | tf_op jit(solution)/shard_map/all_to_all | solution.py:591
  82.9 10.2 %copy-start.13 = (bf16[8,80,256]{2,1,0:T(8,128)(2,1)}, bf16[8,80,256]{2,1,0:T(8,128)(2,1)S(1)}, u32[]{:S(2)}) copy-start(bf16[8,80,256]{2,1,0:T(8,128)(2,1)S(1)} %collective-permute-done.1.p2_ref) | copy-start | bytes 983044
  82.9 8.7 %copy-start.9 = (bf16[256,1152]{1,0:T(8,128)(2,1)}, bf16[256,1152]{1,0:T(8,128)(2,1)S(1)}, u32[]{:S(2)}) copy-start(bf16[256,1152]{1,0:T(8,128)(2,1)S(1)} %collective-permute-done.3.a2_ref) | copy-start | bytes 1769476
  82.9 7.3 %copy-start.3 = (bf16[8,224,256]{2,1,0:T(8,128)(2,1)}, bf16[8,224,256]{2,1,0:T(8,128)(2,1)S(1)}, u32[]{:S(2)}) copy-start(bf16[8,224,256]{2,1,0:T(8,128)(2,1)S(1)} %collective-permute-done.q2_ref) | copy-start | bytes 2752516
  82.9 1.8 %copy-start.1 = (bf16[8,224,256]{2,1,0:T(8,128)(2,1)S(1)}, bf16[8,224,256]{2,1,0:T(8,128)(2,1)}, u32[]{:S(2)}) copy-start(bf16[8,224,256]{2,1,0:T(8,128)(2,1)} %get-tuple-element.41.q1_ref) | copy-start | bytes 2752516
  84.7 1.1 copy-start.5
  85.8 1.1 copy-start.7
  90.2 19.4 %collective-permute-start.4 = (bf16[4,288,384]{2,1,0:T(8,128)(2,1)}, bf16[4,288,384]{2,1,0:T(8,128)(2,1)S(1)}, u32[]{:S(2)}, u32[]{:S(2)}) collective-permute-start(bf16[4,288,384]{2,1,0:T(8,128)(2,1)} %get-tuple-element.50), channel_id=1, source_target_pairs={{0,64},{2,67},{16,80},{18,83},{32,96},{34,99},{48,112},{50,115},{4... | collective-permute-start | bytes 2654216 | tf_op jit(solution)/shard_map/ppermute | solution.py:596
  91.6 18.0 %collective-permute-start.5 = (bf16[4,288,384]{2,1,0:T(8,128)(2,1)}, bf16[4,288,384]{2,1,0:T(8,128)(2,1)S(1)}, u32[]{:S(2)}, u32[]{:S(2)}) collective-permute-start(bf16[4,288,384]{2,1,0:T(8,128)(2,1)} %get-tuple-element.51), channel_id=1, source_target_pairs={{0,4},{2,14},{16,20},{18,30},{32,36},{34,46},{48,52},{50,62},{4,0}... | collective-permute-start | bytes 2654216 | tf_op jit(solution)/shard_map/ppermute | solution.py:596
  93.1 16.6 %collective-permute-start.6 = (bf16[4,288,384]{2,1,0:T(8,128)(2,1)}, bf16[4,288,384]{2,1,0:T(8,128)(2,1)S(1)}, u32[]{:S(2)}, u32[]{:S(2)}) collective-permute-start(bf16[4,288,384]{2,1,0:T(8,128)(2,1)} %get-tuple-element.52), channel_id=1, source_target_pairs={{0,16},{2,50},{16,0},{18,34},{32,48},{34,18},{48,32},{50,2},{4,20}... | collective-permute-start | bytes 2654216 | tf_op jit(solution)/shard_map/ppermute | solution.py:596
  97.1 9.2 %copy-start.2 = (bf16[8,224,256]{2,1,0:T(8,128)(2,1)S(1)}, bf16[8,224,256]{2,1,0:T(8,128)(2,1)}, u32[]{:S(2)}) copy-start(bf16[8,224,256]{2,1,0:T(8,128)(2,1)} %get-tuple-element.41.q1_ref) | copy-start | bytes 2752516
  97.1 9.2 %copy-start.4 = (bf16[8,224,256]{2,1,0:T(8,128)(2,1)S(1)}, bf16[8,224,256]{2,1,0:T(8,128)(2,1)}, u32[]{:S(2)}) copy-start(bf16[8,224,256]{2,1,0:T(8,128)(2,1)} %copy-done.3) | copy-start | bytes 2752516
  97.1 9.2 %copy-start.6 = (bf16[256,1152]{1,0:T(8,128)(2,1)S(1)}, bf16[256,1152]{1,0:T(8,128)(2,1)}, u32[]{:S(2)}) copy-start(bf16[256,1152]{1,0:T(8,128)(2,1)} %get-tuple-element.45.h1_ref) | copy-start | bytes 1769476
  97.1 9.3 %copy-start.8 = (bf16[256,1152]{1,0:T(8,128)(2,1)S(1)}, bf16[256,1152]{1,0:T(8,128)(2,1)}, u32[]{:S(2)}) copy-start(bf16[256,1152]{1,0:T(8,128)(2,1)} %get-tuple-element.46.a1_ref) | copy-start | bytes 1769476
  97.1 9.3 %copy-start.10 = (bf16[256,1152]{1,0:T(8,128)(2,1)S(1)}, bf16[256,1152]{1,0:T(8,128)(2,1)}, u32[]{:S(2)}) copy-start(bf16[256,1152]{1,0:T(8,128)(2,1)} %copy-done.9) | copy-start | bytes 1769476
  97.2 9.3 %copy-start.12 = (bf16[8,80,256]{2,1,0:T(8,128)(2,1)S(1)}, bf16[8,80,256]{2,1,0:T(8,128)(2,1)}, u32[]{:S(2)}) copy-start(bf16[8,80,256]{2,1,0:T(8,128)(2,1)} %get-tuple-element.43.p1_ref) | copy-start | bytes 983044
  106.4 1.0 copy-start.14
  109.6 1.5 copy-start
  111.4 12.0 %collective-permute-start.7 = (bf16[2,288,384]{2,1,0:T(8,128)(2,1)S(1)}, bf16[2,288,384]{2,1,0:T(8,128)(2,1)S(1)}, u32[]{:S(2)}, u32[]{:S(2)}) collective-permute-start(bf16[2,288,384]{2,1,0:T(8,128)(2,1)S(1)} %get-tuple-element.53), channel_id=1, source_target_pairs={{0,4},{2,14},{16,20},{18,30},{32,36},{34,46},{48,52},{50,62},{4,0}... | collective-permute-start | bytes 1327112 | tf_op jit(solution)/shard_map/ppermute | solution.py:600
  112.4 11.1 %collective-permute-start.8 = (bf16[2,288,384]{2,1,0:T(8,128)(2,1)S(1)}, bf16[2,288,384]{2,1,0:T(8,128)(2,1)S(1)}, u32[]{:S(2)}, u32[]{:S(2)}) collective-permute-start(bf16[2,288,384]{2,1,0:T(8,128)(2,1)S(1)} %get-tuple-element.54), channel_id=1, source_target_pairs={{0,16},{2,50},{16,0},{18,34},{32,48},{34,18},{48,32},{50,2},{4,20}... | collective-permute-start | bytes 1327112 | tf_op jit(solution)/shard_map/ppermute | solution.py:600
  112.8 10.7 %collective-permute-start.9 = (bf16[2,288,384]{2,1,0:T(8,128)(2,1)S(1)}, bf16[2,288,384]{2,1,0:T(8,128)(2,1)S(1)}, u32[]{:S(2)}, u32[]{:S(2)}) collective-permute-start(bf16[2,288,384]{2,1,0:T(8,128)(2,1)S(1)} %get-tuple-element.55), channel_id=1, source_target_pairs={{0,64},{2,67},{16,80},{18,83},{32,96},{34,99},{48,112},{50,115},{4... | collective-permute-start | bytes 1327112 | tf_op jit(solution)/shard_map/ppermute | solution.py:600
  123.5 1.1 copy-start.15
  124.8 6.0 %collective-permute-start.10 = (bf16[288,384]{1,0:T(8,128)(2,1)S(1)}, bf16[288,384]{1,0:T(8,128)(2,1)S(1)}, u32[]{:S(2)}, u32[]{:S(2)}) collective-permute-start(bf16[288,384]{1,0:T(8,128)(2,1)S(1)} %get-tuple-element.56), channel_id=1, source_target_pairs={{0,16},{2,50},{16,0},{18,34},{32,48},{34,18},{48,32},{50,2},{4,20}... | collective-permute-start | bytes 663560 | tf_op jit(solution)/shard_map/ppermute | solution.py:604
  126.3 5.9 %collective-permute-start.11 = (bf16[288,384]{1,0:T(8,128)(2,1)S(1)}, bf16[288,384]{1,0:T(8,128)(2,1)S(1)}, u32[]{:S(2)}, u32[]{:S(2)}) collective-permute-start(bf16[288,384]{1,0:T(8,128)(2,1)S(1)} %get-tuple-element.57), channel_id=1, source_target_pairs={{0,64},{2,67},{16,80},{18,83},{32,96},{34,99},{48,112},{50,115},{4... | collective-permute-start | bytes 663560 | tf_op jit(solution)/shard_map/ppermute | solution.py:604
  126.8 5.9 %collective-permute-start.12 = (bf16[288,384]{1,0:T(8,128)(2,1)S(1)}, bf16[288,384]{1,0:T(8,128)(2,1)S(1)}, u32[]{:S(2)}, u32[]{:S(2)}) collective-permute-start(bf16[288,384]{1,0:T(8,128)(2,1)S(1)} %get-tuple-element.58), channel_id=1, source_target_pairs={{0,4},{2,14},{16,20},{18,30},{32,36},{34,46},{48,52},{50,62},{4,0}... | collective-permute-start | bytes 663560 | tf_op jit(solution)/shard_map/ppermute | solution.py:604
  133.3 8.4 %collective-permute-start.13 = (bf16[144,1152]{1,0:T(8,128)(2,1)S(1)}, bf16[144,1152]{1,0:T(8,128)(2,1)S(1)}, u32[]{:S(2)}, u32[]{:S(2)}) collective-permute-start(bf16[144,1152]{1,0:T(8,128)(2,1)S(1)} %get-tuple-element.60), channel_id=1, source_target_pairs={{0,65},{2,66},{16,81},{18,82},{32,97},{34,98},{48,113},{50,114},{4... | collective-permute-start | bytes 995336 | tf_op jit(solution)/shard_map/ppermute | solution.py:618
  141.9 6.6 %collective-permute-start.14 = (bf16[72,1152]{1,0:T(8,128)(2,1)S(1)}, bf16[72,1152]{1,0:T(8,128)(2,1)S(1)}, u32[]{:S(2)}, u32[]{:S(2)}) collective-permute-start(bf16[72,1152]{1,0:T(8,128)(2,1)S(1)} %get-tuple-element.62), channel_id=1, source_target_pairs={{0,12},{2,6},{16,28},{18,22},{32,44},{34,38},{48,60},{50,54},{4,8}... | collective-permute-start | bytes 497672 | tf_op jit(solution)/shard_map/ppermute | solution.py:618
  148.6 5.8 %collective-permute-start.15 = (bf16[36,1152]{1,0:T(8,128)(2,1)S(1)}, bf16[36,1152]{1,0:T(8,128)(2,1)S(1)}, u32[]{:S(2)}, u32[]{:S(2)}) collective-permute-start(bf16[36,1152]{1,0:T(8,128)(2,1)S(1)} %get-tuple-element.64), channel_id=1, source_target_pairs={{0,48},{2,18},{16,32},{18,2},{32,16},{34,50},{48,0},{50,34},{4,52}... | collective-permute-start | bytes 248840 | tf_op jit(solution)/shard_map/ppermute | solution.py:618

commit v3 on v2

--- a/solution.py
+++ b/solution.py
@@ -124,10 +124,24 @@
     ]
 
 
+AHEAD = 3
+
+
+def start_weights(copies):
+    for c in copies[:AHEAD]:
+        c.start()
+
+
+def next_weights(copies, i):
+    copies[i].wait()
+    if i + AHEAD < len(copies):
+        copies[i + AHEAD].start()
+
+
 def qkv_heads(copies, w_ref, hid_ref, qk_ref, v_ref):
     per = W_ROWS // HEAD
     for i in range(QKV_CHUNKS):
-        copies[i].wait()
+        next_weights(copies, i)
         block = dot(w_ref[i * W_ROWS : (i + 1) * W_ROWS, :], hid_ref[...], NT)
         for j in range(per):
             h = i * per + j
@@ -144,20 +158,20 @@
     return dot(k, grad_score) * FACTOR, dot(q, grad_score, NT) * (1.0 / LOG2E)
 
 
-def grad_heads(w_ref, go_ref, out_ref):
-    block = dot(go_ref[...], w_ref[...]).T
+def grad_heads(w, go, out_ref):
+    block = dot(go, w).T
     for h in range(HEADS):
         out_ref[h] = block[h * HEAD : (h + 1) * HEAD, :].astype(bf16)
 
 
 def spatial_forward_kernel(
-    x_ref, mod_ref, w_hbm,
-    middle_ref, kept_out, raw_out, inv_ref,
+    x_ref, cot_ref, mod_ref, w_hbm,
+    both_ref, kept_out, raw_out, inv_ref,
     w_ref, hid_ref, attn_ref, qk_ref, v_ref, o_ref, raw_ref, sems, out_sems,
 ):
     copies = weight_copies(w_hbm, w_ref, sems, range(W_CHUNKS))
-    for c in copies:
-        c.start()
+    start_weights(copies)
+    both_ref[:, PLACE:, :] = cot_ref[...].astype(f32).reshape(FRAMES, PLACE, D).astype(bf16)
     v_ref[:, HEAD:V_ROWS, :] = jnp.ones((HEADS, V_ROWS - HEAD, T), bf16)
     modulated(x_ref, mod_ref, 0, 1, hid_ref)
     qkv_heads(copies, w_ref, hid_ref, qk_ref, v_ref)
@@ -192,62 +206,70 @@
     lax.fori_loop(0, HEADS // GROUP, group, 0)
     kept.append(pltpu.make_async_copy(o_ref, kept_out.at[pl.ds(3 * HEADS, HEADS)], out_sems.at[2]))
     kept[-1].start()
-    for c in copies[QKV_CHUNKS:]:
-        c.wait()
+    for i in range(QKV_CHUNKS, W_CHUNKS):
+        next_weights(copies, i)
     block = dot(w_ref[3 * D :, :], attn_ref[...].astype(bf16)).T
-    middle_ref[...] = (x_ref[...].astype(f32) + mod_ref[2:3, :] * block).astype(bf16)
+    middle = x_ref[...].astype(f32) + mod_ref[2:3, :] * block
+    both_ref[:, :PLACE, :] = middle.reshape(FRAMES, PLACE, D).astype(bf16)
     for c in kept + [raw_copy(i) for i in range(HEADS // GROUP)]:
         c.wait()
 
 
-def cotangent_kernel(
-    cot_ref, mod_ref, w_hbm, heads_ref, mine_ref, theirs_ref, w_ref, go_ref, gof_ref, tmp_ref, sems
-):
-    copies = weight_copies(w_hbm, w_ref, sems, range(QKV_CHUNKS, W_CHUNKS))
-    for c in copies:
-        c.start()
-    for r in range(0, T, ROWS):
-        go_ref[r : r + ROWS, :] = (
-            cot_ref[r : r + ROWS, :].astype(f32) * mod_ref[5:6, :]
-        ).astype(bf16)
-    for j in range(0, D, PART):
-        gof_ref[j : j + PART, :] = go_ref[:, j : j + PART].astype(f32).T
-    gather_rows(gof_ref, tmp_ref, mine_ref, theirs_ref, P_ROWS)
-    for c in copies:
-        c.wait()
-    grad_heads(w_ref, go_ref, heads_ref)
-
-
-def gather_rows(src_ref, tmp_ref, mine_ref, theirs_ref, rows):
+def gather_rows(src_ref, tmp_ref, mine_ref, theirs_ref, rows, start):
     me = lax.axis_index("seq") % 2
+    padded = tmp_ref.shape[1]
     tmp_ref[...] = jnp.zeros_like(tmp_ref)
     for core in range(2):
         for chunk in range(SUBS):
             slot = (core * SUBS + chunk) % 2
             for sub in range(SUBS):
-                start = rows * owner_of(core, chunk, sub)
-                tmp_ref[slot, rows * sub : rows * (sub + 1), :] = src_ref[start : start + rows, :]
+                first = rows * owner_of(core, chunk, sub)
+                tmp_ref[slot, rows * sub : rows * (sub + 1), :] = src_ref[first : first + rows, :]
             low = tmp_ref[slot].astype(bf16)
 
             @pl.when(me == core)
             def _(chunk=chunk, low=low):
-                mine_ref[chunk] = low
+                mine_ref[chunk, start : start + padded] = low
 
             @pl.when(me != core)
             def _(chunk=chunk, low=low):
-                theirs_ref[chunk] = low
+                theirs_ref[chunk, start : start + padded] = low
+
+
+def by_position(both, start):
+    row = lax.broadcasted_iota(jnp.int32, (T, 2 * T), 0)
+    col = lax.broadcasted_iota(jnp.int32, (T, 2 * T), 1)
+    source = (row % FRAMES) * (2 * PLACE) + row // FRAMES + start
+    return dot(jnp.where(source == col, 1.0, 0.0).astype(bf16), both).astype(bf16)
+
+
+def by_frame(tokens):
+    row = lax.broadcasted_iota(jnp.int32, (T, T), 0)
+    col = lax.broadcasted_iota(jnp.int32, (T, T), 1)
+    source = (row % PLACE) * FRAMES + row // PLACE
+    return dot(jnp.where(source == col, 1.0, 0.0).astype(bf16), tokens)
 
 
 def temporal_kernel(
-    m_ref, cot_ref, g_ref, mod_ref, w_hbm,
-    gm_ref, hid_ref, attn_out_ref, mine_ref, theirs_ref,
-    w_ref, qk_ref, v_ref, attn_ref, grad_ref, gh_ref, tmp_ref, sems,
+    both_ref, mod_ref, w_hbm,
+    gm_out, right_ref, mine_ref, theirs_ref,
+    w_ref, m_ref, cot_ref, gm_ref, hid_ref, qk_ref, v_ref, g_ref, attn_ref, grad_ref, gh_ref,
+    tmp_ref, tmp_p_ref, sems,
 ):
-    copies = weight_copies(w_hbm, w_ref, sems, range(QKV_CHUNKS))
-    for c in copies:
-        c.start()
+    copies = weight_copies(w_hbm, w_ref, sems, range(W_CHUNKS))
+    start_weights(copies)
+    both = both_ref[...].reshape(2 * T, D)
+    m_ref[...] = by_position(both, 0)
     modulated(m_ref, mod_ref, 3, 4, hid_ref)
+    right_ref[:T, :] = hid_ref[...]
     qkv_heads(copies, w_ref, hid_ref, qk_ref, v_ref)
+    cot_ref[...] = by_position(both, PLACE)
+    go = (cot_ref[...].astype(f32) * mod_ref[5:6, :]).astype(bf16)
+    grad_ref[:D, :] = go.astype(f32).T
+    gather_rows(grad_ref, tmp_p_ref, mine_ref, theirs_ref, P_ROWS, Q_PAD)
+    for i in range(QKV_CHUNKS, W_CHUNKS):
+        next_weights(copies, i)
+    grad_heads(w_ref[3 * D :, :], go, g_ref)
 
     def group(i, _):
         heads = [i * GROUP + s for s in range(GROUP)]
@@ -269,8 +291,9 @@
     lax.fori_loop(0, HEADS // GROUP, group, 0)
     gh_ref[...] = dot(grad_ref[...].astype(bf16).T, w_ref[: 3 * D, :])
     norm_back_rows(m_ref, cot_ref, gh_ref, mod_ref, 4, gm_ref)
-    attn_out_ref[...] = attn_ref[...].astype(bf16).T
-    gather_rows(grad_ref, tmp_ref, mine_ref, theirs_ref, Q_ROWS)
+    gm_out[...] = by_frame(gm_ref[...]).reshape(FRAMES, PLACE, D).astype(bf16)
+    right_ref[T:, :] = attn_ref[...].astype(bf16).T
+    gather_rows(grad_ref, tmp_ref, mine_ref, theirs_ref, Q_ROWS, 0)
 
 
 def first_lanes():
@@ -304,16 +327,13 @@
 
 
 def weight_grad_kernel(
-    flip,
-    q1_ref, q2_ref, p1_ref, p2_ref, h1_ref, h2_ref, a1_ref, a2_ref,
-    out0_ref, out1_ref, out2_ref,
-    ql_ref, pl_ref, h_ref, a_ref,
+    flip, left1_ref, left2_ref, right1_ref, right2_ref, out0_ref, out1_ref, out2_ref, ql_ref, pl_ref, h_ref, a_ref
 ):
     first, _ = own_bits()
-    h_ref[:T, :] = h1_ref[...]
-    h_ref[T:, :] = h2_ref[...]
-    a_ref[:T, :] = a1_ref[...]
-    a_ref[T:, :] = a2_ref[...]
+    h_ref[:T, :] = right1_ref[:T, :]
+    h_ref[T:, :] = right2_ref[:T, :]
+    a_ref[:T, :] = right1_ref[T:, :]
+    a_ref[T:, :] = right2_ref[T:, :]
     for p, out_ref in enumerate((out0_ref, out1_ref, out2_ref)):
         for i in range(4):
             bits = [None] * 3
@@ -322,11 +342,11 @@
             bits[(p + 2) % 3] = i & 1
             j = 4 * bits[0] + 2 * bits[1] + bits[2]
             rows = slice(i * Q_PAD, (i + 1) * Q_PAD)
-            ql_ref[rows, :T] = q1_ref[j]
-            ql_ref[rows, T:] = q2_ref[j]
+            ql_ref[rows, :T] = left1_ref[j, :Q_PAD]
+            ql_ref[rows, T:] = left2_ref[j, :Q_PAD]
             rows = slice(i * P_PAD, (i + 1) * P_PAD)
-            pl_ref[rows, :T] = p1_ref[j]
-            pl_ref[rows, T:] = p2_ref[j]
+            pl_ref[rows, :T] = left1_ref[j, Q_PAD:]
+            pl_ref[rows, T:] = left2_ref[j, Q_PAD:]
         cols = slice(p * PART, (p + 1) * PART)
         q = dot(ql_ref[...], h_ref[:, cols])
         o = dot(pl_ref[...], a_ref[:, cols])
@@ -347,13 +367,11 @@
     ]
     for c in copies + kept:
         c.start()
-    for r in range(0, T, ROWS):
-        go_ref[r : r + ROWS, :] = (
-            gm_ref[r : r + ROWS, :].astype(f32) * mod_ref[2:3, :]
-        ).astype(bf16)
+    gm = gm_ref[...].astype(f32).reshape(T, D)
+    go_ref[...] = (gm * mod_ref[2:3, :]).astype(bf16)
     for c in copies:
         c.wait()
-    grad_heads(w_ref, go_ref, g_ref)
+    grad_heads(w_ref[...], go_ref[...], g_ref)
     for c in kept:
         c.wait()
 
@@ -377,17 +395,22 @@
     lax.fori_loop(0, HEADS // GROUP, group, 0)
 
 
-def spatial_norm_back_kernel(grad_ref, gm_ref, x_ref, mod_ref, w_hbm, out_ref, w_ref, cat_ref, gh_ref, sems):
+def spatial_norm_back_kernel(
+    grad_ref, gm_in, x_ref, mod_ref, w_hbm, out_ref, w_ref, cat_ref, gh_ref, gm_ref, sems
+):
     copies = weight_copies(w_hbm, w_ref, sems, range(QKV_CHUNKS))
-    for c in copies:
-        c.start()
+    start_weights(copies)
+    gm_ref[...] = gm_in[...].astype(f32).reshape(T, D).astype(bf16)
     for h in range(0, 3 * HEADS, 2):
         pair = jnp.concatenate([grad_ref[h].astype(f32), grad_ref[h + 1].astype(f32)], axis=0)
         cat_ref[h * HEAD : (h + 2) * HEAD, :] = pair.astype(bf16)
     flipped = cat_ref[...].T
-    for c in copies:
-        c.wait()
-    gh_ref[...] = dot(flipped, w_ref[: 3 * D, :])
+    for n in range(3):
+        for i in range(QKV_CHUNKS // 3):
+            next_weights(copies, n * (QKV_CHUNKS // 3) + i)
+        cols = slice(n * D, (n + 1) * D)
+        part = dot(flipped[:, cols], w_ref[cols, :])
+        gh_ref[...] = part if n == 0 else gh_ref[...] + part
     norm_back_rows(x_ref, gm_ref, gh_ref, mod_ref, 1, out_ref)
 
 
@@ -413,34 +436,51 @@
         ).astype(bf16)
 
 
-Q_HALVES = (Q_CHUNK // 2, Q_CHUNK // 4, Q_CHUNK // 8)
-P_HALVES = (P_CHUNK // 2, P_CHUNK // 4, P_CHUNK // 8)
-
-
-def split_halves(total_ref, bit, q_rows, p_rows, half_ref, keep_ref, send_ref):
-    total = 2 * q_rows + 2 * p_rows
-    for side in range(2):
-        q, p = side * q_rows, 2 * q_rows + side * p_rows
-        half_ref[side, :q_rows] = total_ref[q : q + q_rows, :]
-        half_ref[side, q_rows : total // 2] = total_ref[p : p + p_rows, :]
-    keep_ref[...] = half_ref[bit]
-    send_ref[...] = half_ref[1 - bit].astype(bf16)
+def xor_pairs(flips):
+    pairs = []
+    for coord in all_coords():
+        other = list(coord)
+        for axis in range(2):
+            if (flips >> (1 - axis)) & 1:
+                other[axis] = GRAY.index(GRAY[coord[axis]] ^ (1 << (1 - coord[3])))
+        pairs.append((device_index(*coord), device_index(*other)))
+    return pairs
+
+
+def split_rows(total_ref, count, part_ref):
+    rows = total_ref.shape[0]
+    q_rows = rows * Q_ROWS // (Q_ROWS + P_ROWS) // count
+    p_rows = rows // count - q_rows
+    for k in range(count):
+        p = count * q_rows + k * p_rows
+        part_ref[k, :q_rows] = total_ref[k * q_rows : (k + 1) * q_rows, :]
+        part_ref[k, q_rows:] = total_ref[p : p + p_rows, :]
 
 
 def fourth_send_kernel(*refs):
     keep, got, more, most = refs[0:3], refs[3:6], refs[6:9], refs[9:12]
-    own_ref, send_ref, row_ref, half_ref = refs[12:16]
+    own_ref, sends, row_ref, part_ref = refs[12], refs[13:16], refs[16], refs[17]
     for p, (a, b) in enumerate(chunk_bits()):
         i = 2 * a + b
         row_ref[:, p * PART : (p + 1) * PART] = (
             keep[p][i].astype(f32) + got[p][i].astype(f32) + more[p][b].astype(f32)
         ) + most[p][...].astype(f32)
-    split_halves(row_ref, own_bits()[1][0], Q_HALVES[0], P_HALVES[0], half_ref, own_ref, send_ref)
-
-
-def later_send_kernel(step, own_in, got_ref, own_ref, send_ref, row_ref, half_ref):
-    row_ref[...] = own_in[...] + got_ref[...].astype(f32)
-    split_halves(row_ref, own_bits()[1][step], Q_HALVES[step], P_HALVES[step], half_ref, own_ref, send_ref)
+    split_rows(row_ref, 4, part_ref)
+    _, last = own_bits()
+    me = 2 * last[0] + last[1]
+    own_ref[...] = part_ref[me]
+    for d in range(1, 4):
+        sends[d - 1][...] = part_ref[me ^ d].astype(bf16)
+
+
+def fifth_send_kernel(own_in, got1_ref, got2_ref, got3_ref, own_ref, send_ref, row_ref, part_ref):
+    row_ref[...] = (own_in[...] + got1_ref[...].astype(f32)) + (
+        got2_ref[...].astype(f32) + got3_ref[...].astype(f32)
+    )
+    split_rows(row_ref, 2, part_ref)
+    _, last = own_bits()
+    own_ref[...] = part_ref[last[2]]
+    send_ref[...] = part_ref[1 - last[2]].astype(bf16)
 
 
 def last_sum_kernel(own_ref, got_ref, q_ref, p_ref):
@@ -479,10 +519,10 @@
 RAW = ((HEADS, T, T), bf16)
 
 
-def spatial_forward(x, mod, w):
+def spatial_forward(x, cot, mod, w):
     return call(
         spatial_forward_kernel,
-        [TOKENS, KEPT, KEPT_RAW, ((HEADS, 1, T), f32)],
+        [((FRAMES, 2 * PLACE, D), bf16), KEPT, KEPT_RAW, ((HEADS, 1, T), f32)],
         [
             WEIGHT,
             pltpu.VMEM(*TOKENS),
@@ -494,44 +534,41 @@
             SEMS,
             pltpu.SemaphoreType.DMA((3 + HEADS // GROUP,)),
         ],
-        [VMEM, VMEM, ANY],
+        [VMEM, VMEM, VMEM, ANY],
         6_000_000_000,
         "spatial_forward",
         [VMEM, ANY, ANY, VMEM],
-    )(x, mod, w)
-
-
-def cotangent(cot, mod, w):
-    rows = ((SUBS, P_PAD, T), bf16)
-    return call(
-        cotangent_kernel,
-        [HEAD_ROWS, rows, rows],
-        [W_OUT, pltpu.VMEM(*TOKENS), pltpu.VMEM((D, T), f32), pltpu.VMEM((2, P_PAD, T), f32), SEMS],
-        [VMEM, VMEM, ANY],
-        2_000_000_000,
-        "cotangent_heads",
-    )(cot, mod, w)
-
-
-def temporal(m, cot, g, mod, w):
-    rows = ((SUBS, Q_PAD, T), bf16)
+    )(x, cot, mod, w)
+
+
+LEFT = ((SUBS, Q_PAD + P_PAD, T), bf16)
+RIGHT = ((2 * T, D), bf16)
+
+
+def temporal(both, mod, w):
     return call(
         temporal_kernel,
-        [TOKENS, TOKENS, TOKENS, rows, rows],
+        [((FRAMES, PLACE, D), bf16), RIGHT, LEFT, LEFT],
         [
-            W_QKV,
+            WEIGHT,
+            pltpu.VMEM(*TOKENS),
+            pltpu.VMEM(*TOKENS),
+            pltpu.VMEM(*TOKENS),
+            pltpu.VMEM(*TOKENS),
             pltpu.VMEM(*QK),
+            pltpu.VMEM(*HEAD_ROWS),
             pltpu.VMEM(*HEAD_ROWS),
             pltpu.VMEM((D, T), f32),
             pltpu.VMEM((3 * D, T), f32),
             pltpu.VMEM((T, D), f32),
             pltpu.VMEM((2, Q_PAD, T), f32),
+            pltpu.VMEM((2, P_PAD, T), f32),
             SEMS,
         ],
-        [VMEM, VMEM, VMEM, VMEM, ANY],
+        [VMEM, VMEM, ANY],
         12_000_000_000,
         "temporal_sublayer",
-    )(m, cot, g, mod, w)
+    )(both, mod, w)
 
 
 def weight_grad(flip, *operands):
@@ -544,7 +581,7 @@
             pltpu.VMEM((2 * T, D), bf16),
             pltpu.VMEM((2 * T, D), bf16),
         ],
-        [VMEM] * 8,
+        [VMEM] * 4,
         10_000_000,
         "weight_grad_send" if flip else "weight_grad_keep",
         limit=20,
@@ -574,21 +611,11 @@
     return call(
         spatial_norm_back_kernel,
         [TOKENS],
-        [W_QKV, pltpu.VMEM((3 * D, T), bf16), pltpu.VMEM((T, D), f32), SEMS],
+        [W_QKV, pltpu.VMEM((3 * D, T), bf16), pltpu.VMEM((T, D), f32), pltpu.VMEM(*TOKENS), SEMS],
         [VMEM] * 4 + [ANY],
         5_000_000_000,
         "spatial_norm_back",
     )(grad, gm, x, mod, w)[0]
-
-
-def to_positions(tokens):
-    got = lax.all_to_all(tokens.reshape(FRAMES, PLACE, D), "seq", 0, 0, tiled=True)
-    return got.transpose(1, 0, 2).reshape(T, D)
-
-
-def to_frames(tokens):
-    sent = tokens.reshape(PLACE, FRAMES, D).transpose(1, 0, 2)
-    return lax.all_to_all(sent, "seq", 0, 0, tiled=True).reshape(T, D)
 
 
 def reduce_rows(send, keep, before_second, before_third):
@@ -602,20 +629,27 @@
         *keep, *got, *more, before_third
     )
     most = [lax.ppermute(out[p], BOTH, flip_pairs((p + 2) % 3, (0, 1))) for p in range(3)]
-    for step in range(3):
-        rows = Q_HALVES[step] + P_HALVES[step]
-        kernel = fourth_send_kernel if step == 0 else functools.partial(later_send_kernel, step)
-        operands = (*keep, *got, *more, *most) if step == 0 else (own, moved)
-        own, sent = call(
-            kernel,
-            [((rows, D), f32), ((rows, D), bf16)],
-            [pltpu.VMEM((2 * rows, D), f32), pltpu.VMEM((2, rows, D), f32)],
-            [VMEM] * len(operands),
-            1_000_000,
-            "later_send",
-            limit=16,
-        )(*operands)
-        moved = lax.ppermute(sent, BOTH, flip_pairs(step, (1, 0)))
+    rows = CHUNK // 4
+    own, *out = call(
+        fourth_send_kernel,
+        [((rows, D), f32)] + [((rows, D), bf16)] * 3,
+        [pltpu.VMEM((CHUNK, D), f32), pltpu.VMEM((4, rows, D), f32)],
+        [VMEM] * 12,
+        1_000_000,
+        "fourth_send",
+        limit=16,
+    )(*keep, *got, *more, *most)
+    moved = [lax.ppermute(out[d - 1], BOTH, xor_pairs(d)) for d in range(1, 4)]
+    own, sent = call(
+        fifth_send_kernel,
+        [((rows // 2, D), f32), ((rows // 2, D), bf16)],
+        [pltpu.VMEM((rows, D), f32), pltpu.VMEM((2, rows // 2, D), f32)],
+        [VMEM] * 4,
+        1_000_000,
+        "fifth_send",
+        limit=8,
+    )(own, *moved)
+    moved = lax.ppermute(sent, BOTH, flip_pairs(2, (1, 0)))
     return call(
         last_sum_kernel,
         [((Q_ROWS, D), f32), ((P_ROWS, D), f32)],
@@ -631,19 +665,11 @@
     x = clip_tokens.reshape(T, D)
     cot = out_cotangent.reshape(T, D)
     mod = modulation.reshape(6, D)
-    cot_pos = to_positions(cot)
-    middle, kept, raw, inv = spatial_forward(x, mod, spatial_weights)
-    middle_pos = to_positions(middle)
-    grad_attn, mine_p, theirs_p = cotangent(cot_pos, mod, temporal_weights)
-    gm_pos, hidden, attn, mine_q, theirs_q = temporal(
-        middle_pos, cot_pos, grad_attn, mod, temporal_weights
-    )
-    gm = to_frames(gm_pos)
-
-    def other(v):
-        return lax.ppermute(v, BOTH, core_pairs())
-
-    operands = (mine_q, other(theirs_q), mine_p, other(theirs_p), hidden, other(hidden), attn, other(attn))
+    both, kept, raw, inv = spatial_forward(x, cot, mod, spatial_weights)
+    both_pos = lax.all_to_all(both, "seq", 0, 0, tiled=True)
+    gm_pos, right, left, theirs = temporal(both_pos, mod, temporal_weights)
+    gm = lax.all_to_all(gm_pos, "seq", 0, 0, tiled=True)
+    operands = (left, lax.ppermute(theirs, BOTH, core_pairs()), right, lax.ppermute(right, BOTH, core_pairs()))
     send = weight_grad(1, *operands)
     keep = weight_grad(0, *operands)
     grad = spatial_attention_back(gm, mod, kept, raw, inv, spatial_weights)

time: 156 us -> 138 us (0.88)
  blocking collectives: 0 us -> 28.4 us
  starting transfers between devices: 43.2 us -> 23.9 us
  local copies, waits for them, and re-layouts: 19.8 us -> 5.47 us
  waiting for transfers between devices: 30.6 us -> 18.2 us
    all_to_all x0 -> x1, blocking collectives: none -> 28.4 us  [on_device(): both_pos = lax.all_to_all(both, 'seq', 0, 0, tiled=True)]
    all_to_all x3 -> x1, starting transfers between devices: 24.5 us -> 5.74 us  [on_device(): gm = lax.all_to_all(gm_pos, 'seq', 0, 0, tiled=True)]
    all_to_all x3 -> x1, waiting for transfers between devices: 11.9 us -> 1.9 us  [on_device(): gm = lax.all_to_all(gm_pos, 'seq', 0, 0, tiled=True)]
    reshape x3 -> x0, local copies, waits for them, and re-layouts: 6.86 us -> none  [the longest x1 2.33 us: to_frames(): sent = tokens.reshape(PLACE, FRAMES, D).transpose(1, 0, 2)]
    unnamed x35 -> x17, local copies, waits for them, and re-layouts: 8.81 us -> 5.47 us
    ppermute x7 -> x6, waiting for transfers between devices: 13.9 us -> 11.5 us  [the longest x3 6.41 us: reduce_rows(): moved = [lax.ppermute(out[d - 1], BOTH, xor_pairs(d)) for d in range(1, 4)]]
    another operation x1 -> x0, local copies, waits for them, and re-layouts: 2.27 us -> none  [to_positions(): tokens.reshape(FRAMES, PLACE, D)]
    pallas_call x2, Pallas kernels: 5.51 us -> 7.61 us  [weight_grad(): call(functools.partial(weight_grad_kernel, flip), [((4, CHUNK, PART), bf1...]
  transfers between devices with their start and end apart: 19 -> 16, of which waited for: 8 -> 8; matrix products, arithmetic and copies ran while one was open for 6% -> 0% of each run, Pallas kernels for 23% -> 18%
where the time goes in v3:
time: 138 us; the launch traced here: 137 us
  Pallas kernels  60.1 us (44%)
  blocking collectives  28.4 us (21%)
  starting transfers between devices  23.9 us (17%)
  waiting for transfers between devices  18.2 us (13%)
  local copies, waits for them, and re-layouts  5.47 us (4%)
    all_to_all x1, blocking collectives, on_device(): both_pos = lax.all_to_all(both, 'seq', 0, 0, tiled=True)  28.4 us
    pallas_call x1, Pallas kernels, temporal(): call(temporal_kernel, [((FRAMES, PLACE, D), bf16), RIGHT, LEFT, LEFT], [W...  20.2 us
    pallas_call x1, Pallas kernels, spatial_forward(): call(spatial_forward_kernel, [((FRAMES, 2 * PLACE, D), bf16), KEPT, KEPT_...  12.9 us
    pallas_call x1, Pallas kernels, spatial_attention_back(): call(spatial_attention_back_kernel, [((3 * HEADS, HEAD, T), bf16)], [W_OU...  9.03 us
    pallas_call x1, Pallas kernels, spatial_norm_back(): call(spatial_norm_back_kernel, [TOKENS], [W_QKV, pltpu.VMEM((3 * D, T), b...  8.33 us
    pallas_call x2, Pallas kernels, weight_grad(): call(functools.partial(weight_grad_kernel, flip), [((4, CHUNK, PART), bf1...  7.61 us
    ppermute x3, waiting for transfers between devices, reduce_rows(): moved = [lax.ppermute(out[d - 1], BOTH, xor_pairs(d)) for d in range(1, 4)]  6.41 us
    ppermute x3, starting transfers between devices, reduce_rows(): moved = [lax.ppermute(out[d - 1], BOTH, xor_pairs(d)) for d in range(1, 4)]  5.99 us
  transfers between devices with their start and end apart: 16, of which 8 were waited for; matrix products, arithmetic and copies ran while one was open for 0% of the time, Pallas kernels for 18%

profile of v3, /device:TPU:0, one launch (start us, length us, event | category | flops | bytes accessed | tf_op | source)
XLA Modules:
  0.0 136.9 jit_solution(9040097481533294319)
XLA Ops:
  0.6 1.4 copy.10
  2.0 12.9 %spatial_forward.1 = (bf16[64,8,1152]{2,1,0:T(8,128)(2,1)}, bf16[280,80,256]{2,1,0:T(8,128)(2,1)}, bf16[88,256,256]{2,1,0:T(8,128)(2,1)}, f32[16,1,256]{2,1,0:T(1,128)}) custom-call(bf16[256,1152]{1,0:T(8,128)(2,1)} %bitcast.12, bf16[256,1152]{1,0:T(8,128)(2,1)} %bitcast.11, f32[6,1152]{1,0:T(8,128)} %bitcast.7, bf16[4608,1152]{1,0:T(8,128)(2,1)} %w_hbm.7), custom_call_target="tpu_custom_call" | custom-call | flops 6000000000 | bytes 12000000 | tf_op jit(solution)/shard_map/spatial_forward/pallas_call | solution.py:523
  14.9 28.4 %all_to_all.10.both_ref = bf16[64,8,1152]{2,1,0:T(8,128)(2,1)} all-to-all(bf16[64,8,1152]{2,1,0:T(8,128)(2,1)} %get-tuple-element.31), channel_id=1, replica_groups=mesh['seq'=64,'rep'=2] {'seq'}, dimensions={0} | all-to-all | bytes 2359296 | tf_op jit(solution)/shard_map/all_to_all | solution.py:669
  43.3 20.2 %temporal_sublayer.1 = (bf16[64,4,1152]{2,1,0:T(4,128)(2,1)}, bf16[512,1152]{1,0:T(8,128)(2,1)}, bf16[8,304,256]{2,1,0:T(8,128)(2,1)}, bf16[8,304,256]{2,1,0:T(8,128)(2,1)}) custom-call(bf16[64,8,1152]{2,1,0:T(8,128)(2,1)} %all_to_all.10.both_ref, f32[6,1152]{1,0:T(8,128)} %bitcast.8, bf16[4608,1152]{1,0:T(8,128)(2,1)} %w_hbm.5), custom_call_target="tpu_custom_call" | custom-call | flops 12000000000 | bytes 12000000 | tf_op jit(solution)/shard_map/temporal_sublayer/pallas_call | solution.py:549
  63.5 0.0 copy-start.5
  63.5 0.1 collective-permute-start
  63.6 0.5 collective-permute-start.1
  64.1 5.7 %all-to-all-start.1 = ((bf16[64,4,1152]{2,1,0:T(4,128)(2,1)}), bf16[64,4,1152]{2,1,0:T(4,128)(2,1)}, u32[]{:S(2)}, u32[]{:S(2)}) async-start(bf16[64,4,1152]{2,1,0:T(4,128)(2,1)} %get-tuple-element.32), calls=%async_computation.1 | async-start | bytes 1179648 | tf_op jit(solution)/shard_map/all_to_all | solution.py:671
  69.8 0.0 collective-permute-done.1.right2_ref
  69.8 0.0 collective-permute-done.left2_ref
  69.8 0.0 copy-start.3
  69.8 0.0 copy-done.5
  69.8 0.0 copy-start.1
  69.8 1.7 %copy-done.1 = bf16[8,304,256]{2,1,0:T(8,128)(2,1)S(1)} copy-done((bf16[8,304,256]{2,1,0:T(8,128)(2,1)S(1)}, bf16[8,304,256]{2,1,0:T(8,128)(2,1)}, u32[]{:S(2)}) %copy-start.1) | copy-done | bytes 1245208
  71.6 4.0 %weight_grad_send.1 = (bf16[4,288,384]{2,1,0:T(8,128)(2,1)}, bf16[4,288,384]{2,1,0:T(8,128)(2,1)}, bf16[4,288,384]{2,1,0:T(8,128)(2,1)S(1)}) custom-call(bf16[8,304,256]{2,1,0:T(8,128)(2,1)S(1)} %copy-done.1, bf16[8,304,256]{2,1,0:T(8,128)(2,1)S(1)} %collective-permute-done.left2_ref, bf16[512,1152]{1,0:T(8,128)(2,1)S(1)} %copy-done.5, ...), custom_call_target="tpu_custom_call" | custom-call | flops 10000000 | bytes 1000 | tf_op jit(solution)/shard_map/weight_grad_send/pallas_call | solution.py:575
  75.6 0.0 copy-done.3
  75.6 1.6 %collective-permute-start.2 = (bf16[4,288,384]{2,1,0:T(8,128)(2,1)}, bf16[4,288,384]{2,1,0:T(8,128)(2,1)S(1)}, u32[]{:S(2)}, u32[]{:S(2)}) collective-permute-start(bf16[4,288,384]{2,1,0:T(8,128)(2,1)} %get-tuple-element.42), channel_id=1, source_target_pairs={{0,64},{2,67},{16,80},{18,83},{32,96},{34,99},{48,112},{50,115},{4... | collective-permute-start | bytes 2654216 | tf_op jit(solution)/shard_map/ppermute | solution.py:623
  77.2 1.5 %collective-permute-start.3 = (bf16[4,288,384]{2,1,0:T(8,128)(2,1)}, bf16[4,288,384]{2,1,0:T(8,128)(2,1)S(1)}, u32[]{:S(2)}, u32[]{:S(2)}) collective-permute-start(bf16[4,288,384]{2,1,0:T(8,128)(2,1)} %get-tuple-element.43), channel_id=1, source_target_pairs={{0,4},{2,14},{16,20},{18,30},{32,36},{34,46},{48,52},{50,62},{4,0}... | collective-permute-start | bytes 2654216 | tf_op jit(solution)/shard_map/ppermute | solution.py:623
  78.7 1.5 %collective-permute-start.4 = (bf16[4,288,384]{2,1,0:T(8,128)(2,1)S(1)}, bf16[4,288,384]{2,1,0:T(8,128)(2,1)S(1)}, u32[]{:S(2)}, u32[]{:S(2)}) collective-permute-start(bf16[4,288,384]{2,1,0:T(8,128)(2,1)S(1)} %get-tuple-element.44), channel_id=1, source_target_pairs={{0,16},{2,50},{16,0},{18,34},{32,48},{34,18},{48,32},{50,2},{4,20}... | collective-permute-start | bytes 2654216 | tf_op jit(solution)/shard_map/ppermute | solution.py:623
  80.2 1.9 %all-to-all-done.1.gm_ref.gm_in = bf16[64,4,1152]{2,1,0:T(4,128)(2,1)} async-done(((bf16[64,4,1152]{2,1,0:T(4,128)(2,1)}), bf16[64,4,1152]{2,1,0:T(4,128)(2,1)}, u32[]{:S(2)}, u32[]{:S(2)}) %all-to-all-start.1) | async-done | bytes 589856 | tf_op jit(solution)/shard_map/all_to_all | solution.py:671
  82.1 0.0 copy-start.2
  82.1 0.0 copy-start.6
  82.1 9.0 %spatial_attention_back.1.grad_ref.refs_6_ = bf16[48,72,256]{2,1,0:T(8,128)(2,1)} custom-call(bf16[64,4,1152]{2,1,0:T(4,128)(2,1)} %all-to-all-done.1.gm_ref.gm_in, f32[6,1152]{1,0:T(8,128)} %bitcast.9, f32[16,1,256]{2,1,0:T(1,128)} %get-tuple-element.33.inv_ref, bf16[280,80,256]{2,1,0:T(8,128)(2,1)} %get-tuple-element.34.kept_hbm, ...), custom_call_target="tpu_custom_call" | custom-call | flops 5000000000 | bytes 12000000 | tf_op jit(solution)/shard_map/spatial_attention_back/pallas_call | solution.py:592
  91.1 0.0 copy-done.2
  91.1 0.0 copy-done.6
  91.2 0.0 copy-start.4
  91.2 1.3 copy-done.4
  92.5 0.0 copy-start
  92.5 3.6 %weight_grad_keep.1 = (bf16[4,288,384]{2,1,0:T(8,128)(2,1)S(1)}, bf16[4,288,384]{2,1,0:T(8,128)(2,1)S(1)}, bf16[4,288,384]{2,1,0:T(8,128)(2,1)S(1)}) custom-call(bf16[8,304,256]{2,1,0:T(8,128)(2,1)S(1)} %copy-done.2, bf16[8,304,256]{2,1,0:T(8,128)(2,1)S(1)} %copy-done.4, bf16[512,1152]{1,0:T(8,128)(2,1)S(1)} %copy-done.6, ...), custom_call_target="tpu_custom_call" | custom-call | flops 10000000 | bytes 1000 | tf_op jit(solution)/shard_map/weight_grad_keep/pallas_call | solution.py:575
  96.1 0.0 collective-permute-done.2.refs_3_
  96.1 0.0 collective-permute-done.3.refs_4_
  96.1 0.0 collective-permute-done.4.refs_5_
  96.1 0.0 copy-done
  96.1 0.3 second_send.1
  96.4 1.0 collective-permute-start.5
  97.4 0.4 collective-permute-start.6
  97.8 1.8 %collective-permute-start.7 = (bf16[2,288,384]{2,1,0:T(8,128)(2,1)S(1)}, bf16[2,288,384]{2,1,0:T(8,128)(2,1)S(1)}, u32[]{:S(2)}, u32[]{:S(2)}) collective-permute-start(bf16[2,288,384]{2,1,0:T(8,128)(2,1)S(1)} %get-tuple-element.47), channel_id=1, source_target_pairs={{0,64},{2,67},{16,80},{18,83},{32,96},{34,99},{48,112},{50,115},{4... | collective-permute-start | bytes 1327112 | tf_op jit(solution)/shard_map/ppermute | solution.py:627
  99.5 8.3 %spatial_norm_back.1.refs_9_ = bf16[256,1152]{1,0:T(8,128)(2,1)} custom-call(bf16[48,72,256]{2,1,0:T(8,128)(2,1)} %spatial_attention_back.1.grad_ref.refs_6_, bf16[64,4,1152]{2,1,0:T(4,128)(2,1)} %all-to-all-done.1.gm_ref.gm_in, bf16[256,1152]{1,0:T(8,128)(2,1)} %bitcast.13, f32[6,1152]{1,0:T(8,128)} %bitcast.10, bf16[4608,1152]{1,0:T(8,128)(2,1)} %w_hbm.7), custom_call_target="tpu_custom_call" | custom-call | flops 5000000000 | bytes 12000000 | tf_op jit(solution)/shard_map/spatial_norm_back/pallas_call | solution.py:611
  107.9 0.0 collective-permute-done.5.refs_6_
  107.9 0.0 collective-permute-done.6.refs_7_
  107.9 0.0 collective-permute-done.7.refs_8_
  107.9 0.0 copy-start.7
  107.9 1.1 copy-done.7
  109.0 0.2 third_send.1
  109.2 1.5 %collective-permute-start.8 = (bf16[288,384]{1,0:T(8,128)(2,1)S(1)}, bf16[288,384]{1,0:T(8,128)(2,1)S(1)}, u32[]{:S(2)}, u32[]{:S(2)}) collective-permute-start(bf16[288,384]{1,0:T(8,128)(2,1)S(1)} %get-tuple-element.48), channel_id=1, source_target_pairs={{0,16},{2,50},{16,0},{18,34},{32,48},{34,18},{48,32},{50,2},{4,20}... | collective-permute-start | bytes 663560 | tf_op jit(solution)/shard_map/ppermute | solution.py:631
  110.7 0.5 collective-permute-start.9
  111.2 1.1 collective-permute-start.10
  112.4 2.9 %collective-permute-done.8.refs_9_ = bf16[288,384]{1,0:T(8,128)(2,1)S(1)} collective-permute-done((bf16[288,384]{1,0:T(8,128)(2,1)S(1)}, bf16[288,384]{1,0:T(8,128)(2,1)S(1)}, u32[]{:S(2)}, u32[]{:S(2)}) %collective-permute-start.8) | collective-permute-done | bytes 221216 | tf_op jit(solution)/shard_map/ppermute | solution.py:631
  115.2 1.4 %collective-permute-done.9.refs_10_ = bf16[288,384]{1,0:T(8,128)(2,1)S(1)} collective-permute-done((bf16[288,384]{1,0:T(8,128)(2,1)S(1)}, bf16[288,384]{1,0:T(8,128)(2,1)S(1)}, u32[]{:S(2)}, u32[]{:S(2)}) %collective-permute-start.9) | collective-permute-done | bytes 221216 | tf_op jit(solution)/shard_map/ppermute | solution.py:631
  116.6 0.5 collective-permute-done.10.refs_11_
  117.2 0.6 fourth_send.1
  117.8 1.8 %collective-permute-start.11 = (bf16[72,1152]{1,0:T(8,128)(2,1)S(1)}, bf16[72,1152]{1,0:T(8,128)(2,1)S(1)}, u32[]{:S(2)}, u32[]{:S(2)}) collective-permute-start(bf16[72,1152]{1,0:T(8,128)(2,1)S(1)} %get-tuple-element.52), channel_id=1, source_target_pairs={{0,12},{2,6},{16,28},{18,22},{32,44},{34,38},{48,60},{50,54},{4,8}... | collective-permute-start | bytes 497672 | tf_op jit(solution)/shard_map/ppermute | solution.py:642
  119.6 1.9 %collective-permute-start.12 = (bf16[72,1152]{1,0:T(8,128)(2,1)S(1)}, bf16[72,1152]{1,0:T(8,128)(2,1)S(1)}, u32[]{:S(2)}, u32[]{:S(2)}) collective-permute-start(bf16[72,1152]{1,0:T(8,128)(2,1)S(1)} %get-tuple-element.53), channel_id=1, source_target_pairs={{0,65},{2,66},{16,81},{18,82},{32,97},{34,98},{48,113},{50,114},{4... | collective-permute-start | bytes 497672 | tf_op jit(solution)/shard_map/ppermute | solution.py:642
  121.5 2.2 %collective-permute-start.13 = (bf16[72,1152]{1,0:T(8,128)(2,1)S(1)}, bf16[72,1152]{1,0:T(8,128)(2,1)S(1)}, u32[]{:S(2)}, u32[]{:S(2)}) collective-permute-start(bf16[72,1152]{1,0:T(8,128)(2,1)S(1)} %get-tuple-element.54), channel_id=1, source_target_pairs={{0,77},{2,70},{16,93},{18,86},{32,109},{34,102},{48,125},{50,118},... | collective-permute-start | bytes 497672 | tf_op jit(solution)/shard_map/ppermute | solution.py:642
  123.8 0.6 collective-permute-done.11.got1_ref
  124.4 1.8 %collective-permute-done.12.got2_ref = bf16[72,1152]{1,0:T(8,128)(2,1)S(1)} collective-permute-done((bf16[72,1152]{1,0:T(8,128)(2,1)S(1)}, bf16[72,1152]{1,0:T(8,128)(2,1)S(1)}, u32[]{:S(2)}, u32[]{:S(2)}) %collective-permute-start.12) | collective-permute-done | bytes 165920 | tf_op jit(solution)/shard_map/ppermute | solution.py:642
  126.2 4.0 %collective-permute-done.13.got3_ref = bf16[72,1152]{1,0:T(8,128)(2,1)S(1)} collective-permute-done((bf16[72,1152]{1,0:T(8,128)(2,1)S(1)}, bf16[72,1152]{1,0:T(8,128)(2,1)S(1)}, u32[]{:S(2)}, u32[]{:S(2)}) %collective-permute-start.13) | collective-permute-done | bytes 165920 | tf_op jit(solution)/shard_map/ppermute | solution.py:642
  130.2 0.2 fifth_send.1
  130.4 0.8 collective-permute-start.14
  131.2 5.1 %collective-permute-done.14.got_ref = bf16[36,1152]{1,0:T(8,128)(2,1)S(1)} collective-permute-done((bf16[36,1152]{1,0:T(8,128)(2,1)S(1)}, bf16[36,1152]{1,0:T(8,128)(2,1)S(1)}, u32[]{:S(2)}, u32[]{:S(2)}) %collective-permute-start.14) | collective-permute-done | bytes 82976 | tf_op jit(solution)/shard_map/ppermute | solution.py:652
  136.2 0.7 last_sum.1
Async XLA Ops:
  63.5 6.4 %copy-start.5 = (bf16[512,1152]{1,0:T(8,128)(2,1)S(1)}, bf16[512,1152]{1,0:T(8,128)(2,1)}, u32[]{:S(2)}) copy-start(bf16[512,1152]{1,0:T(8,128)(2,1)} %get-tuple-element.38.right1_ref) | copy-start | bytes 3538948
  63.5 6.3 %collective-permute-start = (bf16[8,304,256]{2,1,0:T(8,128)(2,1)}, bf16[8,304,256]{2,1,0:T(8,128)(2,1)S(1)}, u32[]{:S(2)}, u32[]{:S(2)}) collective-permute-start(bf16[8,304,256]{2,1,0:T(8,128)(2,1)} %get-tuple-element.37), channel_id=1, source_target_pairs={{0,2},{2,0},{16,18},{18,16},{32,34},{34,32},{48,50},{50,48},{4,6},... | collective-permute-start | bytes 3735560 | tf_op jit(solution)/shard_map/ppermute | solution.py:672
  63.6 6.2 %collective-permute-start.1 = (bf16[512,1152]{1,0:T(8,128)(2,1)}, bf16[512,1152]{1,0:T(8,128)(2,1)}, u32[]{:S(2)}, u32[]{:S(2)}) collective-permute-start(bf16[512,1152]{1,0:T(8,128)(2,1)} %get-tuple-element.38.right1_ref), channel_id=1, source_target_pairs={{0,2},{2,0},{16,18},{18,16},{32,34},{34,32},{48,50},{50,48},{4,6},... | collective-permute-start | bytes 3538952 | tf_op jit(solution)/shard_map/ppermute | solution.py:672
  64.1 18.0 %all-to-all-start.1 = ((bf16[64,4,1152]{2,1,0:T(4,128)(2,1)}), bf16[64,4,1152]{2,1,0:T(4,128)(2,1)}, u32[]{:S(2)}, u32[]{:S(2)}) async-start(bf16[64,4,1152]{2,1,0:T(4,128)(2,1)} %get-tuple-element.32), calls=%async_computation.1 | async-start | bytes 1179648 | tf_op jit(solution)/shard_map/all_to_all | solution.py:671
  69.8 5.8 %copy-start.3 = (bf16[8,304,256]{2,1,0:T(8,128)(2,1)}, bf16[8,304,256]{2,1,0:T(8,128)(2,1)S(1)}, u32[]{:S(2)}) copy-start(bf16[8,304,256]{2,1,0:T(8,128)(2,1)S(1)} %collective-permute-done.left2_ref) | copy-start | bytes 3735556
  69.8 1.7 %copy-start.1 = (bf16[8,304,256]{2,1,0:T(8,128)(2,1)S(1)}, bf16[8,304,256]{2,1,0:T(8,128)(2,1)}, u32[]{:S(2)}) copy-start(bf16[8,304,256]{2,1,0:T(8,128)(2,1)} %get-tuple-element.36.left1_ref) | copy-start | bytes 3735556
  75.6 20.4 %collective-permute-start.2 = (bf16[4,288,384]{2,1,0:T(8,128)(2,1)}, bf16[4,288,384]{2,1,0:T(8,128)(2,1)S(1)}, u32[]{:S(2)}, u32[]{:S(2)}) collective-permute-start(bf16[4,288,384]{2,1,0:T(8,128)(2,1)} %get-tuple-element.42), channel_id=1, source_target_pairs={{0,64},{2,67},{16,80},{18,83},{32,96},{34,99},{48,112},{50,115},{4... | collective-permute-start | bytes 2654216 | tf_op jit(solution)/shard_map/ppermute | solution.py:623
  77.2 18.9 %collective-permute-start.3 = (bf16[4,288,384]{2,1,0:T(8,128)(2,1)}, bf16[4,288,384]{2,1,0:T(8,128)(2,1)S(1)}, u32[]{:S(2)}, u32[]{:S(2)}) collective-permute-start(bf16[4,288,384]{2,1,0:T(8,128)(2,1)} %get-tuple-element.43), channel_id=1, source_target_pairs={{0,4},{2,14},{16,20},{18,30},{32,36},{34,46},{48,52},{50,62},{4,0}... | collective-permute-start | bytes 2654216 | tf_op jit(solution)/shard_map/ppermute | solution.py:623
  78.7 17.4 %collective-permute-start.4 = (bf16[4,288,384]{2,1,0:T(8,128)(2,1)S(1)}, bf16[4,288,384]{2,1,0:T(8,128)(2,1)S(1)}, u32[]{:S(2)}, u32[]{:S(2)}) collective-permute-start(bf16[4,288,384]{2,1,0:T(8,128)(2,1)S(1)} %get-tuple-element.44), channel_id=1, source_target_pairs={{0,16},{2,50},{16,0},{18,34},{32,48},{34,18},{48,32},{50,2},{4,20}... | collective-permute-start | bytes 2654216 | tf_op jit(solution)/shard_map/ppermute | solution.py:623
  82.1 9.0 %copy-start.2 = (bf16[8,304,256]{2,1,0:T(8,128)(2,1)S(1)}, bf16[8,304,256]{2,1,0:T(8,128)(2,1)}, u32[]{:S(2)}) copy-start(bf16[8,304,256]{2,1,0:T(8,128)(2,1)} %get-tuple-element.36.left1_ref) | copy-start | bytes 3735556
  82.1 9.0 %copy-start.6 = (bf16[512,1152]{1,0:T(8,128)(2,1)S(1)}, bf16[512,1152]{1,0:T(8,128)(2,1)}, u32[]{:S(2)}) copy-start(bf16[512,1152]{1,0:T(8,128)(2,1)} %get-tuple-element.38.right1_ref) | copy-start | bytes 3538948
  91.2 1.3 copy-start.4
  92.5 3.6 %copy-start = (bf16[48,72,256]{2,1,0:T(8,128)(2,1)S(1)}, bf16[48,72,256]{2,1,0:T(8,128)(2,1)}, u32[]{:S(2)}) copy-start(bf16[48,72,256]{2,1,0:T(8,128)(2,1)} %spatial_attention_back.1.grad_ref.refs_6_) | copy-start | bytes 5308420
  96.4 11.4 %collective-permute-start.5 = (bf16[2,288,384]{2,1,0:T(8,128)(2,1)S(1)}, bf16[2,288,384]{2,1,0:T(8,128)(2,1)S(1)}, u32[]{:S(2)}, u32[]{:S(2)}) collective-permute-start(bf16[2,288,384]{2,1,0:T(8,128)(2,1)S(1)} %get-tuple-element.45), channel_id=1, source_target_pairs={{0,4},{2,14},{16,20},{18,30},{32,36},{34,46},{48,52},{50,62},{4,0}... | collective-permute-start | bytes 1327112 | tf_op jit(solution)/shard_map/ppermute | solution.py:627
  97.4 10.5 %collective-permute-start.6 = (bf16[2,288,384]{2,1,0:T(8,128)(2,1)S(1)}, bf16[2,288,384]{2,1,0:T(8,128)(2,1)S(1)}, u32[]{:S(2)}, u32[]{:S(2)}) collective-permute-start(bf16[2,288,384]{2,1,0:T(8,128)(2,1)S(1)} %get-tuple-element.46), channel_id=1, source_target_pairs={{0,16},{2,50},{16,0},{18,34},{32,48},{34,18},{48,32},{50,2},{4,20}... | collective-permute-start | bytes 1327112 | tf_op jit(solution)/shard_map/ppermute | solution.py:627
  97.8 10.1 %collective-permute-start.7 = (bf16[2,288,384]{2,1,0:T(8,128)(2,1)S(1)}, bf16[2,288,384]{2,1,0:T(8,128)(2,1)S(1)}, u32[]{:S(2)}, u32[]{:S(2)}) collective-permute-start(bf16[2,288,384]{2,1,0:T(8,128)(2,1)S(1)} %get-tuple-element.47), channel_id=1, source_target_pairs={{0,64},{2,67},{16,80},{18,83},{32,96},{34,99},{48,112},{50,115},{4... | collective-permute-start | bytes 1327112 | tf_op jit(solution)/shard_map/ppermute | solution.py:627
  107.9 1.1 copy-start.7
  109.2 6.0 %collective-permute-start.8 = (bf16[288,384]{1,0:T(8,128)(2,1)S(1)}, bf16[288,384]{1,0:T(8,128)(2,1)S(1)}, u32[]{:S(2)}, u32[]{:S(2)}) collective-permute-start(bf16[288,384]{1,0:T(8,128)(2,1)S(1)} %get-tuple-element.48), channel_id=1, source_target_pairs={{0,16},{2,50},{16,0},{18,34},{32,48},{34,18},{48,32},{50,2},{4,20}... | collective-permute-start | bytes 663560 | tf_op jit(solution)/shard_map/ppermute | solution.py:631
  110.7 5.9 %collective-permute-start.9 = (bf16[288,384]{1,0:T(8,128)(2,1)S(1)}, bf16[288,384]{1,0:T(8,128)(2,1)S(1)}, u32[]{:S(2)}, u32[]{:S(2)}) collective-permute-start(bf16[288,384]{1,0:T(8,128)(2,1)S(1)} %get-tuple-element.49), channel_id=1, source_target_pairs={{0,64},{2,67},{16,80},{18,83},{32,96},{34,99},{48,112},{50,115},{4... | collective-permute-start | bytes 663560 | tf_op jit(solution)/shard_map/ppermute | solution.py:631
  111.2 5.9 %collective-permute-start.10 = (bf16[288,384]{1,0:T(8,128)(2,1)S(1)}, bf16[288,384]{1,0:T(8,128)(2,1)S(1)}, u32[]{:S(2)}, u32[]{:S(2)}) collective-permute-start(bf16[288,384]{1,0:T(8,128)(2,1)S(1)} %get-tuple-element.50), channel_id=1, source_target_pairs={{0,4},{2,14},{16,20},{18,30},{32,36},{34,46},{48,52},{50,62},{4,0}... | collective-permute-start | bytes 663560 | tf_op jit(solution)/shard_map/ppermute | solution.py:631
  117.8 6.6 %collective-permute-start.11 = (bf16[72,1152]{1,0:T(8,128)(2,1)S(1)}, bf16[72,1152]{1,0:T(8,128)(2,1)S(1)}, u32[]{:S(2)}, u32[]{:S(2)}) collective-permute-start(bf16[72,1152]{1,0:T(8,128)(2,1)S(1)} %get-tuple-element.52), channel_id=1, source_target_pairs={{0,12},{2,6},{16,28},{18,22},{32,44},{34,38},{48,60},{50,54},{4,8}... | collective-permute-start | bytes 497672 | tf_op jit(solution)/shard_map/ppermute | solution.py:642
  119.6 6.6 %collective-permute-start.12 = (bf16[72,1152]{1,0:T(8,128)(2,1)S(1)}, bf16[72,1152]{1,0:T(8,128)(2,1)S(1)}, u32[]{:S(2)}, u32[]{:S(2)}) collective-permute-start(bf16[72,1152]{1,0:T(8,128)(2,1)S(1)} %get-tuple-element.53), channel_id=1, source_target_pairs={{0,65},{2,66},{16,81},{18,82},{32,97},{34,98},{48,113},{50,114},{4... | collective-permute-start | bytes 497672 | tf_op jit(solution)/shard_map/ppermute | solution.py:642
  121.5 8.7 %collective-permute-start.13 = (bf16[72,1152]{1,0:T(8,128)(2,1)S(1)}, bf16[72,1152]{1,0:T(8,128)(2,1)S(1)}, u32[]{:S(2)}, u32[]{:S(2)}) collective-permute-start(bf16[72,1152]{1,0:T(8,128)(2,1)S(1)} %get-tuple-element.54), channel_id=1, source_target_pairs={{0,77},{2,70},{16,93},{18,86},{32,109},{34,102},{48,125},{50,118},... | collective-permute-start | bytes 497672 | tf_op jit(solution)/shard_map/ppermute | solution.py:642
  130.4 5.8 %collective-permute-start.14 = (bf16[36,1152]{1,0:T(8,128)(2,1)S(1)}, bf16[36,1152]{1,0:T(8,128)(2,1)S(1)}, u32[]{:S(2)}, u32[]{:S(2)}) collective-permute-start(bf16[36,1152]{1,0:T(8,128)(2,1)S(1)} %get-tuple-element.56), channel_id=1, source_target_pairs={{0,48},{2,18},{16,32},{18,2},{32,16},{34,50},{48,0},{50,34},{4,52}... | collective-permute-start | bytes 248840 | tf_op jit(solution)/shard_map/ppermute | solution.py:652

commit v4 on v3

--- a/solution.py
+++ b/solution.py
@@ -26,6 +26,7 @@
 P_PAD = 80
 KEPT = ((280, 80, 256), jnp.bfloat16)
 KEPT_RAW = ((88, 256, 256), jnp.bfloat16)
+KEPT_SUMS = ((200, 288, 384), jnp.bfloat16)
 GROUP = 4
 V_ROWS = 80
 FRAMES = 64
@@ -91,24 +92,28 @@
 ROWS = 64
 
 
+def row(mod_ref, i):
+    return mod_ref[i]
+
+
 def modulated(src_ref, mod_ref, shift, scale, out_ref):
     for r in range(0, T, ROWS):
         normed, _ = normalize(src_ref[r : r + ROWS, :])
         out_ref[r : r + ROWS, :] = (
-            normed * (1.0 + mod_ref[scale : scale + 1, :]) + mod_ref[shift : shift + 1, :]
+            normed * (1.0 + row(mod_ref, scale)) + row(mod_ref, shift)
         ).astype(bf16)
 
 
 def norm_back_rows(src_ref, direct_ref, grad_ref, mod_ref, scale, out_ref):
     for r in range(0, T, ROWS):
         normed, spread = normalize(src_ref[r : r + ROWS, :])
-        g = grad_ref[r : r + ROWS, :] * (1.0 + mod_ref[scale : scale + 1, :])
+        g = grad_ref[r : r + ROWS, :] * (1.0 + row(mod_ref, scale))
         centered = g - jnp.mean(g, axis=-1, keepdims=True)
         back = spread * (centered - normed * jnp.mean(g * normed, axis=-1, keepdims=True))
         out_ref[r : r + ROWS, :] = (direct_ref[r : r + ROWS, :].astype(f32) + back).astype(bf16)
 
 
-W_ROWS = 576
+W_ROWS = 1152
 W_CHUNKS = 4 * D // W_ROWS
 QKV_CHUNKS = 3 * D // W_ROWS
 
@@ -124,34 +129,22 @@
     ]
 
 
-AHEAD = 3
-
-
-def start_weights(copies):
-    for c in copies[:AHEAD]:
-        c.start()
-
-
-def next_weights(copies, i):
-    copies[i].wait()
-    if i + AHEAD < len(copies):
-        copies[i + AHEAD].start()
-
-
-def qkv_heads(copies, w_ref, hid_ref, qk_ref, v_ref):
-    per = W_ROWS // HEAD
-    for i in range(QKV_CHUNKS):
-        next_weights(copies, i)
-        block = dot(w_ref[i * W_ROWS : (i + 1) * W_ROWS, :], hid_ref[...], NT)
-        for j in range(per):
-            h = i * per + j
+SIDE = HEADS // 2 * HEAD
+
+
+def qkv_heads(side, w_ref, hid_ref, qk_ref, v_ref):
+    for n in range(3):
+        start = n * D + side * SIDE
+        block = dot(w_ref[start : start + SIDE, :], hid_ref[...], NT)
+        for j in range(HEADS // 2):
+            h = side * (HEADS // 2) + j
             rows = block[j * HEAD : (j + 1) * HEAD, :]
-            if h < HEADS:
+            if n == 0:
                 qk_ref[h, :HEAD] = (rows * (FACTOR * LOG2E)).astype(bf16)
-            elif h < 2 * HEADS:
-                qk_ref[h, :HEAD] = rows.astype(bf16)
+            elif n == 1:
+                qk_ref[HEADS + h, :HEAD] = rows.astype(bf16)
             else:
-                v_ref[h - 2 * HEADS, :HEAD] = rows.astype(bf16)
+                v_ref[h, :HEAD] = rows.astype(bf16)
 
 
 def score_grads(q, k, grad_score):
@@ -165,23 +158,20 @@
 
 
 def spatial_forward_kernel(
-    x_ref, cot_ref, mod_ref, w_hbm,
+    x_ref, cot_hbm, mod_ref, w_hbm,
     both_ref, kept_out, raw_out, inv_ref,
-    w_ref, hid_ref, attn_ref, qk_ref, v_ref, o_ref, raw_ref, sems, out_sems,
+    w_ref, cot_ref, hid_ref, attn_ref, qk_ref, v_ref, o_ref, raw_ref, sems, out_sems,
 ):
-    copies = weight_copies(w_hbm, w_ref, sems, range(W_CHUNKS))
-    start_weights(copies)
-    both_ref[:, PLACE:, :] = cot_ref[...].astype(f32).reshape(FRAMES, PLACE, D).astype(bf16)
+    blocks_of = [(n * D + side * SIDE, SIDE) for side in range(2) for n in range(3)] + [(3 * D, D)]
+    copies = [
+        pltpu.make_async_copy(w_hbm.at[pl.ds(r, size), :], w_ref.at[pl.ds(r, size), :], sems.at[i])
+        for i, (r, size) in enumerate(blocks_of)
+    ]
+    copies.append(pltpu.make_async_copy(cot_hbm, cot_ref, sems.at[7]))
+    for c in copies:
+        c.start()
     v_ref[:, HEAD:V_ROWS, :] = jnp.ones((HEADS, V_ROWS - HEAD, T), bf16)
     modulated(x_ref, mod_ref, 0, 1, hid_ref)
-    qkv_heads(copies, w_ref, hid_ref, qk_ref, v_ref)
-    kept = [
-        pltpu.make_async_copy(qk_ref, kept_out.at[pl.ds(0, 2 * HEADS)], out_sems.at[0]),
-        pltpu.make_async_copy(v_ref, kept_out.at[pl.ds(2 * HEADS, HEADS)], out_sems.at[1]),
-    ]
-    for c in kept:
-        c.start()
-
     def raw_copy(i):
         part = pl.ds(i * GROUP, GROUP)
         return pltpu.make_async_copy(raw_ref.at[part], raw_out.at[part], out_sems.at[3 + i])
@@ -203,13 +193,24 @@
             attn_ref[pl.ds(pl.multiple_of(h * HEAD, 8), HEAD), :] = out
         return _
 
-    lax.fori_loop(0, HEADS // GROUP, group, 0)
+    for side in range(2):
+        for c in copies[3 * side : 3 * side + 3]:
+            c.wait()
+        qkv_heads(side, w_ref, hid_ref, qk_ref, v_ref)
+        lax.fori_loop(side * HEADS // GROUP // 2, (side + 1) * HEADS // GROUP // 2, group, 0)
+    kept = [
+        pltpu.make_async_copy(qk_ref, kept_out.at[pl.ds(0, 2 * HEADS)], out_sems.at[0]),
+        pltpu.make_async_copy(v_ref, kept_out.at[pl.ds(2 * HEADS, HEADS)], out_sems.at[1]),
+    ]
+    for c in kept:
+        c.start()
     kept.append(pltpu.make_async_copy(o_ref, kept_out.at[pl.ds(3 * HEADS, HEADS)], out_sems.at[2]))
     kept[-1].start()
-    for i in range(QKV_CHUNKS, W_CHUNKS):
-        next_weights(copies, i)
+    copies[6].wait()
+    copies[7].wait()
+    both_ref[:, PLACE:, :] = cot_ref[...].astype(f32).reshape(FRAMES, PLACE, D).astype(bf16)
     block = dot(w_ref[3 * D :, :], attn_ref[...].astype(bf16)).T
-    middle = x_ref[...].astype(f32) + mod_ref[2:3, :] * block
+    middle = x_ref[...].astype(f32) + row(mod_ref, 2) * block
     both_ref[:, :PLACE, :] = middle.reshape(FRAMES, PLACE, D).astype(bf16)
     for c in kept + [raw_copy(i) for i in range(HEADS // GROUP)]:
         c.wait()
@@ -251,24 +252,27 @@
 
 
 def temporal_kernel(
-    both_ref, mod_ref, w_hbm,
+    both_hbm, mod_ref, w_hbm,
     gm_out, right_ref, mine_ref, theirs_ref,
-    w_ref, m_ref, cot_ref, gm_ref, hid_ref, qk_ref, v_ref, g_ref, attn_ref, grad_ref, gh_ref,
+    w_ref, both_ref, m_ref, cot_ref, gm_ref, hid_ref, qk_ref, v_ref, g_ref, attn_ref, grad_ref, gh_ref,
     tmp_ref, tmp_p_ref, sems,
 ):
-    copies = weight_copies(w_hbm, w_ref, sems, range(W_CHUNKS))
-    start_weights(copies)
+    first = pltpu.make_async_copy(both_hbm, both_ref, sems.at[0])
+    weights = pltpu.make_async_copy(w_hbm, w_ref, sems.at[1])
+    first.start()
+    weights.start()
+    first.wait()
     both = both_ref[...].reshape(2 * T, D)
     m_ref[...] = by_position(both, 0)
     modulated(m_ref, mod_ref, 3, 4, hid_ref)
     right_ref[:T, :] = hid_ref[...]
-    qkv_heads(copies, w_ref, hid_ref, qk_ref, v_ref)
     cot_ref[...] = by_position(both, PLACE)
-    go = (cot_ref[...].astype(f32) * mod_ref[5:6, :]).astype(bf16)
+    go = (cot_ref[...].astype(f32) * row(mod_ref, 5)).astype(bf16)
     grad_ref[:D, :] = go.astype(f32).T
     gather_rows(grad_ref, tmp_p_ref, mine_ref, theirs_ref, P_ROWS, Q_PAD)
-    for i in range(QKV_CHUNKS, W_CHUNKS):
-        next_weights(copies, i)
+    weights.wait()
+    for side in range(2):
+        qkv_heads(side, w_ref, hid_ref, qk_ref, v_ref)
     grad_heads(w_ref[3 * D :, :], go, g_ref)
 
     def group(i, _):
@@ -327,8 +331,17 @@
 
 
 def weight_grad_kernel(
-    flip, left1_ref, left2_ref, right1_ref, right2_ref, out0_ref, out1_ref, out2_ref, ql_ref, pl_ref, h_ref, a_ref
+    flip, left1_ref, left2_ref, right1_ref, right2_ref, *refs
 ):
+    if flip:
+        out0_ref, out1_ref, out2_ref, token_ref, ql_ref, pl_ref, h_ref, a_ref = refs
+        token_ref[...] = jnp.zeros_like(token_ref)
+        moved = []
+    else:
+        gm_in, _, out_hbm, gm_out, ql_ref, pl_ref, h_ref, a_ref, out0_ref, out1_ref, out2_ref, sem, out_sems = refs
+        passed = pltpu.make_async_copy(gm_in, gm_out, sem)
+        passed.start()
+        moved = [passed]
     first, _ = own_bits()
     h_ref[:T, :] = right1_ref[:T, :]
     h_ref[T:, :] = right2_ref[:T, :]
@@ -354,26 +367,38 @@
             out_ref[i] = jnp.concatenate(
                 [q[i * Q_PAD : i * Q_PAD + Q_CHUNK], o[i * P_PAD : i * P_PAD + P_CHUNK]], axis=0
             ).astype(bf16)
+        if not flip:
+            moved.append(pltpu.make_async_copy(out_ref, out_hbm.at[pl.ds(4 * p, 4)], out_sems.at[p]))
+            moved[-1].start()
+    for c in moved:
+        c.wait()
+
+
+HALF = HEADS // 2
 
 
 def spatial_attention_back_kernel(
-    gm_ref, mod_ref, inv_ref, kept_hbm, raw_hbm, w_hbm, grad_ref,
-    w_ref, go_ref, g_ref, kept_ref, raw_ref, sems, in_sems,
+    gm_ref, mod_ref, inv_ref, kept_hbm, raw_hbm, w_hbm, grad_out, token_ref,
+    w_ref, g_ref, kept_ref, raw_ref, grad_ref, sems, in_sems,
 ):
-    copies = weight_copies(w_hbm, w_ref, sems, range(QKV_CHUNKS, W_CHUNKS))
-    kept = [
-        pltpu.make_async_copy(kept_hbm.at[pl.ds(0, 4 * HEADS)], kept_ref, in_sems.at[0]),
-        pltpu.make_async_copy(raw_hbm.at[pl.ds(0, HEADS)], raw_ref, in_sems.at[1]),
-    ]
-    for c in copies + kept:
+    (weights,) = weight_copies(w_hbm, w_ref, sems, range(QKV_CHUNKS, W_CHUNKS))
+    kept = []
+    for side in range(2):
+        copies = []
+        for n in range(4):
+            part = pl.ds(n * HEADS + side * HALF, HALF)
+            copies.append(pltpu.make_async_copy(kept_hbm.at[part], kept_ref.at[part], in_sems.at[side, n]))
+        part = pl.ds(side * HALF, HALF)
+        copies.append(pltpu.make_async_copy(raw_hbm.at[part], raw_ref.at[part], in_sems.at[side, 4]))
+        kept.append(copies)
+    for c in [weights] + kept[0]:
         c.start()
-    gm = gm_ref[...].astype(f32).reshape(T, D)
-    go_ref[...] = (gm * mod_ref[2:3, :]).astype(bf16)
-    for c in copies:
-        c.wait()
-    grad_heads(w_ref[...], go_ref[...], g_ref)
-    for c in kept:
-        c.wait()
+    token_ref[...] = jnp.zeros_like(token_ref)
+    go = (gm_ref[...].astype(f32).reshape(T, D) * row(mod_ref, 2)).astype(bf16)
+    weights.wait()
+    for c in kept[1]:
+        c.start()
+    grad_heads(w_ref[...], go, g_ref)
 
     def group(i, _):
         heads = [i * GROUP + s for s in range(GROUP)]
@@ -389,28 +414,33 @@
             grad_score = (raw.astype(f32) * (gp - inner)).astype(bf16)
             dq, dk = score_grads(kept_ref[h, :HEAD], kept_ref[HEADS + h, :HEAD], grad_score)
             for n, value in enumerate((dq, dk, dot(g, raw, NT))):
-                grad_ref[n * HEADS + h] = value.astype(bf16)
+                grad_ref[pl.ds(pl.multiple_of(n * D + h * HEAD, 8), HEAD), :] = value
         return _
 
-    lax.fori_loop(0, HEADS // GROUP, group, 0)
+    for side in range(2):
+        for c in kept[side]:
+            c.wait()
+        lax.fori_loop(side * HALF // GROUP, (side + 1) * HALF // GROUP, group, 0)
+    grad_out[...] = grad_ref[...].astype(bf16)
 
 
 def spatial_norm_back_kernel(
-    grad_ref, gm_in, x_ref, mod_ref, w_hbm, out_ref, w_ref, cat_ref, gh_ref, gm_ref, sems
+    grad_ref, gm_hbm, x_hbm, mod_ref, w_hbm, out_ref, token_ref, w_ref, gh_ref, gm_in, gm_ref, x_ref, sems, in_sems
 ):
     copies = weight_copies(w_hbm, w_ref, sems, range(QKV_CHUNKS))
-    start_weights(copies)
+    copies.append(pltpu.make_async_copy(gm_hbm, gm_in, in_sems.at[0]))
+    copies.append(pltpu.make_async_copy(x_hbm, x_ref, in_sems.at[1]))
+    for c in copies:
+        c.start()
+    token_ref[...] = jnp.zeros_like(token_ref)
+    flipped = grad_ref[...].T
+    copies[0].wait()
+    copies[1].wait()
+    gh_ref[...] = dot(flipped[:, : 2 * D], w_ref[: 2 * D, :])
+    for c in copies[2:]:
+        c.wait()
     gm_ref[...] = gm_in[...].astype(f32).reshape(T, D).astype(bf16)
-    for h in range(0, 3 * HEADS, 2):
-        pair = jnp.concatenate([grad_ref[h].astype(f32), grad_ref[h + 1].astype(f32)], axis=0)
-        cat_ref[h * HEAD : (h + 2) * HEAD, :] = pair.astype(bf16)
-    flipped = cat_ref[...].T
-    for n in range(3):
-        for i in range(QKV_CHUNKS // 3):
-            next_weights(copies, n * (QKV_CHUNKS // 3) + i)
-        cols = slice(n * D, (n + 1) * D)
-        part = dot(flipped[:, cols], w_ref[cols, :])
-        gh_ref[...] = part if n == 0 else gh_ref[...] + part
+    gh_ref[...] = gh_ref[...] + dot(flipped[:, 2 * D :], w_ref[2 * D :, :])
     norm_back_rows(x_ref, gm_ref, gh_ref, mod_ref, 1, out_ref)
 
 
@@ -419,21 +449,26 @@
     return [(first[(p + 1) % 3], first[(p + 2) % 3]) for p in range(3)]
 
 
-def second_send_kernel(*refs):
-    keep, got, out = refs[0:3], refs[3:6], refs[7:10]
-    for p, (a, _) in enumerate(chunk_bits()):
+def second_sums_kernel(flip, *refs):
+    keep_hbm, got, out, keep, sems = refs[0], refs[1:4], refs[4:7], refs[7:10], refs[10]
+    bits = [a ^ flip for a, _ in chunk_bits()]
+    copies = [
+        pltpu.make_async_copy(keep_hbm.at[pl.ds(4 * p + 2 * a, 2)], keep[p], sems.at[p])
+        for p, a in enumerate(bits)
+    ]
+    for c in copies:
+        c.start()
+    for p, a in enumerate(bits):
+        copies[p].wait()
         for j in range(2):
-            i = 2 * (1 - a) + j
-            out[p][j] = (keep[p][i].astype(f32) + got[p][i].astype(f32)).astype(bf16)
+            out[p][j] = (keep[p][j].astype(f32) + got[p][2 * a + j].astype(f32)).astype(bf16)
 
 
 def third_send_kernel(*refs):
-    keep, got, more, out = refs[0:3], refs[3:6], refs[6:9], refs[10:13]
-    for p, (a, b) in enumerate(chunk_bits()):
-        i = 2 * a + 1 - b
-        out[p][...] = (
-            keep[p][i].astype(f32) + got[p][i].astype(f32) + more[p][1 - b].astype(f32)
-        ).astype(bf16)
+    keep, got, own, out = refs[0:3], refs[3:6], refs[6:9], refs[9:12]
+    for p, (_, b) in enumerate(chunk_bits()):
+        for to, i in ((out, 1 - b), (own, b)):
+            to[p][...] = (keep[p][i].astype(f32) + got[p][i].astype(f32)).astype(bf16)
 
 
 def xor_pairs(flips):
@@ -458,13 +493,10 @@
 
 
 def fourth_send_kernel(*refs):
-    keep, got, more, most = refs[0:3], refs[3:6], refs[6:9], refs[9:12]
-    own_ref, sends, row_ref, part_ref = refs[12], refs[13:16], refs[16], refs[17]
-    for p, (a, b) in enumerate(chunk_bits()):
-        i = 2 * a + b
-        row_ref[:, p * PART : (p + 1) * PART] = (
-            keep[p][i].astype(f32) + got[p][i].astype(f32) + more[p][b].astype(f32)
-        ) + most[p][...].astype(f32)
+    keep, got = refs[0:3], refs[3:6]
+    own_ref, sends, row_ref, part_ref = refs[7], refs[8:11], refs[11], refs[12]
+    for p in range(3):
+        row_ref[:, p * PART : (p + 1) * PART] = keep[p][...].astype(f32) + got[p][...].astype(f32)
     split_rows(row_ref, 4, part_ref)
     _, last = own_bits()
     me = 2 * last[0] + last[1]
@@ -473,7 +505,7 @@
         sends[d - 1][...] = part_ref[me ^ d].astype(bf16)
 
 
-def fifth_send_kernel(own_in, got1_ref, got2_ref, got3_ref, own_ref, send_ref, row_ref, part_ref):
+def fifth_send_kernel(own_in, got1_ref, got2_ref, got3_ref, _, own_ref, send_ref, row_ref, part_ref):
     row_ref[...] = (own_in[...] + got1_ref[...].astype(f32)) + (
         got2_ref[...].astype(f32) + got3_ref[...].astype(f32)
     )
@@ -507,7 +539,7 @@
 
 
 WEIGHT = pltpu.VMEM((4 * D, D), bf16)
-W_QKV = pltpu.VMEM((3 * D, D), bf16)
+TOKEN = ((8, 128), f32)
 W_OUT = pltpu.VMEM((D, D), bf16)
 SEMS = pltpu.SemaphoreType.DMA((W_CHUNKS,))
 QK = ((2 * HEADS, V_ROWS, T), bf16)
@@ -526,15 +558,16 @@
         [
             WEIGHT,
             pltpu.VMEM(*TOKENS),
+            pltpu.VMEM(*TOKENS),
             pltpu.VMEM((D, T), f32),
             pltpu.VMEM(*QK),
             pltpu.VMEM(*V),
             pltpu.VMEM(*V),
             pltpu.VMEM(*RAW),
-            SEMS,
+            pltpu.SemaphoreType.DMA((8,)),
             pltpu.SemaphoreType.DMA((3 + HEADS // GROUP,)),
         ],
-        [VMEM, VMEM, VMEM, ANY],
+        [VMEM, ANY, VMEM, ANY],
         6_000_000_000,
         "spatial_forward",
         [VMEM, ANY, ANY, VMEM],
@@ -551,6 +584,7 @@
         [((FRAMES, PLACE, D), bf16), RIGHT, LEFT, LEFT],
         [
             WEIGHT,
+            pltpu.VMEM((FRAMES, 2 * PLACE, D), bf16),
             pltpu.VMEM(*TOKENS),
             pltpu.VMEM(*TOKENS),
             pltpu.VMEM(*TOKENS),
@@ -563,27 +597,33 @@
             pltpu.VMEM((T, D), f32),
             pltpu.VMEM((2, Q_PAD, T), f32),
             pltpu.VMEM((2, P_PAD, T), f32),
-            SEMS,
+            pltpu.SemaphoreType.DMA((2,)),
         ],
-        [VMEM, VMEM, ANY],
+        [ANY, VMEM, ANY],
         12_000_000_000,
         "temporal_sublayer",
+        limit=40,
     )(both, mod, w)
 
 
 def weight_grad(flip, *operands):
+    part = ((4, CHUNK, PART), bf16)
+    scratch = [
+        pltpu.VMEM((4 * Q_PAD, 2 * T), bf16),
+        pltpu.VMEM((4 * P_PAD, 2 * T), bf16),
+        pltpu.VMEM((2 * T, D), bf16),
+        pltpu.VMEM((2 * T, D), bf16),
+    ]
+    if not flip:
+        scratch += [pltpu.VMEM(*part)] * 3 + [pltpu.SemaphoreType.DMA, pltpu.SemaphoreType.DMA((3,))]
     return call(
         functools.partial(weight_grad_kernel, flip),
-        [((4, CHUNK, PART), bf16)] * 3,
-        [
-            pltpu.VMEM((4 * Q_PAD, 2 * T), bf16),
-            pltpu.VMEM((4 * P_PAD, 2 * T), bf16),
-            pltpu.VMEM((2 * T, D), bf16),
-            pltpu.VMEM((2 * T, D), bf16),
-        ],
-        [VMEM] * 4,
+        [part] * 3 + [TOKEN] if flip else [KEPT_SUMS, ((FRAMES, PLACE, D), bf16)],
+        scratch,
+        [VMEM] * 4 + [ANY] * (2 - 2 * flip),
         10_000_000,
         "weight_grad_send" if flip else "weight_grad_keep",
+        [VMEM] * 4 if flip else [ANY] * 2,
         limit=20,
     )(*operands)
 
@@ -591,64 +631,81 @@
 def spatial_attention_back(gm, mod, kept, raw, inv, w):
     return call(
         spatial_attention_back_kernel,
-        [((3 * HEADS, HEAD, T), bf16)],
+        [((3 * D, T), bf16), TOKEN],
         [
             W_OUT,
-            pltpu.VMEM(*TOKENS),
             pltpu.VMEM(*HEAD_ROWS),
             pltpu.VMEM((4 * HEADS, V_ROWS, T), bf16),
             pltpu.VMEM(*RAW),
+            pltpu.VMEM((3 * D, T), f32),
             SEMS,
-            pltpu.SemaphoreType.DMA((2,)),
+            pltpu.SemaphoreType.DMA((2, 5)),
         ],
         [VMEM] * 3 + [ANY] * 3,
         5_000_000_000,
         "spatial_attention_back",
-    )(gm, mod, inv, kept, raw, w)[0]
+    )(gm, mod, inv, kept, raw, w)
 
 
 def spatial_norm_back(grad, gm, x, mod, w):
     return call(
         spatial_norm_back_kernel,
-        [TOKENS],
-        [W_QKV, pltpu.VMEM((3 * D, T), bf16), pltpu.VMEM((T, D), f32), pltpu.VMEM(*TOKENS), SEMS],
-        [VMEM] * 4 + [ANY],
+        [TOKENS, TOKEN],
+        [
+            pltpu.VMEM((3 * D, D), bf16),
+            pltpu.VMEM((T, D), f32),
+            pltpu.VMEM((FRAMES, PLACE, D), bf16),
+            pltpu.VMEM(*TOKENS),
+            pltpu.VMEM(*TOKENS),
+            SEMS,
+            pltpu.SemaphoreType.DMA((2,)),
+        ],
+        [VMEM, ANY, ANY, VMEM, ANY],
         5_000_000_000,
         "spatial_norm_back",
-    )(grad, gm, x, mod, w)[0]
-
-
-def reduce_rows(send, keep, before_second, before_third):
+    )(grad, gm, x, mod, w)
+
+
+def reduce_rows(send, keep, tokens):
     half, one = ((2, CHUNK, PART), bf16), ((CHUNK, PART), bf16)
+
+    def second_sums(flip):
+        return call(
+            functools.partial(second_sums_kernel, flip),
+            [half] * 3,
+            [pltpu.VMEM(*half)] * 3 + [pltpu.SemaphoreType.DMA((3,))],
+            [ANY] + [VMEM] * 3,
+            1_000_000,
+            "second_sums_send" if flip else "second_sums_own",
+            limit=16,
+        )(keep, *got)
+
     got = [lax.ppermute(send[p], BOTH, flip_pairs(p, (0, 1))) for p in range(3)]
-    out = call(second_send_kernel, [half] * 3, [], [VMEM] * 6 + [ANY], 1_000_000, "second_send", limit=12)(
-        *keep, *got, before_second
-    )
-    more = [lax.ppermute(out[p], BOTH, flip_pairs((p + 1) % 3, (0, 1))) for p in range(3)]
-    out = call(third_send_kernel, [one] * 3, [], [VMEM] * 9 + [ANY], 1_000_000, "third_send", limit=12)(
-        *keep, *got, *more, before_third
-    )
-    most = [lax.ppermute(out[p], BOTH, flip_pairs((p + 2) % 3, (0, 1))) for p in range(3)]
+    out, own = second_sums(1), second_sums(0)
+    got = [lax.ppermute(out[p], BOTH, flip_pairs((p + 1) % 3, (0, 1))) for p in range(3)]
+    outs = call(third_send_kernel, [one] * 6, [], [VMEM] * 6, 1_000_000, "third_send", limit=12)(*own, *got)
+    own, out = outs[:3], outs[3:]
+    got = [lax.ppermute(out[p], BOTH, flip_pairs((p + 2) % 3, (0, 1))) for p in range(3)]
     rows = CHUNK // 4
     own, *out = call(
         fourth_send_kernel,
         [((rows, D), f32)] + [((rows, D), bf16)] * 3,
         [pltpu.VMEM((CHUNK, D), f32), pltpu.VMEM((4, rows, D), f32)],
-        [VMEM] * 12,
+        [VMEM] * 6 + [ANY],
         1_000_000,
         "fourth_send",
         limit=16,
-    )(*keep, *got, *more, *most)
+    )(*own, *got, tokens[0])
     moved = [lax.ppermute(out[d - 1], BOTH, xor_pairs(d)) for d in range(1, 4)]
     own, sent = call(
         fifth_send_kernel,
         [((rows // 2, D), f32), ((rows // 2, D), bf16)],
         [pltpu.VMEM((rows, D), f32), pltpu.VMEM((2, rows // 2, D), f32)],
-        [VMEM] * 4,
+        [VMEM] * 4 + [ANY],
         1_000_000,
         "fifth_send",
         limit=8,
-    )(own, *moved)
+    )(own, *moved, tokens[1])
     moved = lax.ppermute(sent, BOTH, flip_pairs(2, (1, 0)))
     return call(
         last_sum_kernel,
@@ -664,17 +721,18 @@
 def on_device(clip_tokens, modulation, spatial_weights, temporal_weights, out_cotangent):
     x = clip_tokens.reshape(T, D)
     cot = out_cotangent.reshape(T, D)
-    mod = modulation.reshape(6, D)
+    mod = modulation.reshape(6, 1, D)
     both, kept, raw, inv = spatial_forward(x, cot, mod, spatial_weights)
     both_pos = lax.all_to_all(both, "seq", 0, 0, tiled=True)
     gm_pos, right, left, theirs = temporal(both_pos, mod, temporal_weights)
+    operands = (left, lax.ppermute(theirs, BOTH, core_pairs()), right, lax.ppermute(right, BOTH, core_pairs()))
+    *send, token = weight_grad(1, *operands)
+    keep, gm_pos = weight_grad(0, *operands, gm_pos, token)
     gm = lax.all_to_all(gm_pos, "seq", 0, 0, tiled=True)
-    operands = (left, lax.ppermute(theirs, BOTH, core_pairs()), right, lax.ppermute(right, BOTH, core_pairs()))
-    send = weight_grad(1, *operands)
-    keep = weight_grad(0, *operands)
-    grad = spatial_attention_back(gm, mod, kept, raw, inv, spatial_weights)
-    input_grad = spatial_norm_back(grad, gm, x, mod, spatial_weights)
-    qkv_rows, proj_rows = reduce_rows(send, keep, grad, input_grad)
+    grad, token1 = spatial_attention_back(gm, mod, kept, raw, inv, spatial_weights)
+    input_grad, token2 = spatial_norm_back(grad, gm, x, mod, spatial_weights)
+    tokens = (token1, token2)
+    qkv_rows, proj_rows = reduce_rows(send, keep, tokens)
     return input_grad.reshape(clip_tokens.shape), qkv_rows, proj_rows
 
 

time: 138 us -> 126 us (0.913)
  Pallas kernels: 60.1 us -> 53.8 us
  local copies, waits for them, and re-layouts: 5.47 us -> 1.37 us
  waiting for transfers between devices: 18.2 us -> 15 us
  starting transfers between devices: 23.9 us -> 26.4 us
    ppermute x3, waiting for transfers between devices: 0.01 us -> 6.56 us  [reduce_rows(): lax.ppermute(out[p], BOTH, flip_pairs((p + 1) % 3, (0, 1)))]
    ppermute x3, waiting for transfers between devices: 6.41 us -> 0.01 us  [reduce_rows(): moved = [lax.ppermute(out[d - 1], BOTH, xor_pairs(d)) for d in range(1, 4)]]
    pallas_call x1, Pallas kernels: 20.2 us -> 15.4 us  [temporal(): call(temporal_kernel, [((FRAMES, PLACE, D), bf16), RIGHT, LEFT, LEFT], [W...]
    ppermute x3, waiting for transfers between devices: 4.8 us -> 0.01 us  [reduce_rows(): lax.ppermute(out[p], BOTH, flip_pairs((p + 2) % 3, (0, 1)))]
    ppermute x1, waiting for transfers between devices: 0.01 us -> 4.12 us  [on_device(): lax.ppermute(right, BOTH, core_pairs())]
    unnamed x17 -> x6, local copies, waits for them, and re-layouts: 5.47 us -> 1.37 us
    ppermute x1, starting transfers between devices: 0.78 us -> 2.95 us  [reduce_rows(): moved = lax.ppermute(sent, BOTH, flip_pairs(2, (1, 0)))]
    ppermute x1, waiting for transfers between devices: 5.06 us -> 2.89 us  [reduce_rows(): moved = lax.ppermute(sent, BOTH, flip_pairs(2, (1, 0)))]
  transfers between devices with their start and end apart: 16 -> 16, of which waited for: 8 -> 6; matrix products, arithmetic and copies ran while one was open for 0% -> 0% of each run, Pallas kernels for 18% -> 19%
where the time goes in v4:
time: 126 us
  Pallas kernels  53.8 us (43%)
  blocking collectives  28.3 us (22%)
  starting transfers between devices  26.4 us (21%)
  waiting for transfers between devices  15 us (12%)
  local copies, waits for them, and re-layouts  1.37 us (1%)
    all_to_all x1, blocking collectives, on_device(): both_pos = lax.all_to_all(both, 'seq', 0, 0, tiled=True)  28.3 us
    pallas_call x1, Pallas kernels, temporal(): call(temporal_kernel, [((FRAMES, PLACE, D), bf16), RIGHT, LEFT, LEFT], [W...  15.4 us
    pallas_call x1, Pallas kernels, spatial_forward(): call(spatial_forward_kernel, [((FRAMES, 2 * PLACE, D), bf16), KEPT, KEPT_...  11 us
    pallas_call x1, Pallas kernels, spatial_attention_back(): call(spatial_attention_back_kernel, [((3 * D, T), bf16), TOKEN], [W_OUT,...  8.76 us
    pallas_call x1, Pallas kernels, spatial_norm_back(): call(spatial_norm_back_kernel, [TOKENS, TOKEN], [pltpu.VMEM((3 * D, D), b...  8.12 us
    all_to_all x1, starting transfers between devices, on_device(): gm = lax.all_to_all(gm_pos, 'seq', 0, 0, tiled=True)  7.23 us
    ppermute x3, waiting for transfers between devices, reduce_rows(): lax.ppermute(out[p], BOTH, flip_pairs((p + 1) % 3, (0, 1)))  6.56 us
    pallas_call x2, Pallas kernels, weight_grad(): call(functools.partial(weight_grad_kernel, flip), [part] * 3 + [TOKEN] if...  6.16 us
  transfers between devices with their start and end apart: 16, of which 6 were waited for; matrix products, arithmetic and copies ran while one was open for 0% of the time, Pallas kernels for 19%

profile of v4, /device:TPU:0, one launch (start us, length us, event | category | flops | bytes accessed | tf_op | source)
XLA Modules:
  0.0 125.7 jit_solution(12348618495738346692)
XLA Ops:
  0.6 11.0 %spatial_forward.1 = (bf16[64,8,1152]{2,1,0:T(8,128)(2,1)}, bf16[280,80,256]{2,1,0:T(8,128)(2,1)}, bf16[88,256,256]{2,1,0:T(8,128)(2,1)}, f32[16,1,256]{2,1,0:T(1,128)}) custom-call(bf16[256,1152]{1,0:T(8,128)(2,1)} %bitcast.9, bf16[256,1152]{1,0:T(8,128)(2,1)} %bitcast.8, f32[6,1,1152]{2,1,0:T(1,128)} %bitcast.4, bf16[4608,1152]{1,0:T(8,128)(2,1)} %w_hbm.7), custom_call_target="tpu_custom_call" | custom-call | flops 6000000000 | bytes 12000000 | tf_op jit(solution)/shard_map/spatial_forward/pallas_call | solution.py:555
  11.6 0.0 copy-start
  11.6 28.3 %all_to_all.10.both_hbm = bf16[64,8,1152]{2,1,0:T(8,128)(2,1)S(1)} all-to-all(bf16[64,8,1152]{2,1,0:T(8,128)(2,1)} %get-tuple-element.41), channel_id=1, replica_groups=mesh['seq'=64,'rep'=2] {'seq'}, dimensions={0} | all-to-all | bytes 2359296 | tf_op jit(solution)/shard_map/all_to_all | solution.py:726
  39.9 0.0 copy-done
  39.9 15.4 %temporal_sublayer.1 = (bf16[64,4,1152]{2,1,0:T(4,128)(2,1)S(1)}, bf16[512,1152]{1,0:T(8,128)(2,1)S(1)}, bf16[8,304,256]{2,1,0:T(8,128)(2,1)S(1)}, bf16[8,304,256]{2,1,0:T(8,128)(2,1)S(1)}) custom-call(bf16[64,8,1152]{2,1,0:T(8,128)(2,1)S(1)} %all_to_all.10.both_hbm, f32[6,1,1152]{2,1,0:T(1,128)S(1)} %bitcast.7, bf16[4608,1152]{1,0:T(8,128)(2,1)} %w_hbm.5), custom_call_target="tpu_custom_call" | custom-call | flops 12000000000 | bytes 12000000 | tf_op jit(solution)/shard_map/temporal_sublayer/pallas_call | solution.py:582
  55.3 0.1 collective-permute-start
  55.4 0.5 collective-permute-start.1
  55.9 4.1 %collective-permute-done.1.right2_ref = bf16[512,1152]{1,0:T(8,128)(2,1)S(1)} collective-permute-done((bf16[512,1152]{1,0:T(8,128)(2,1)S(1)}, bf16[512,1152]{1,0:T(8,128)(2,1)S(1)}, u32[]{:S(2)}, u32[]{:S(2)}) %collective-permute-start.1) | collective-permute-done | bytes 1179680 | tf_op jit(solution)/shard_map/ppermute | solution.py:728
  60.0 0.0 collective-permute-done.left2_ref
  60.0 2.6 %weight_grad_send.1 = (bf16[4,288,384]{2,1,0:T(8,128)(2,1)}, bf16[4,288,384]{2,1,0:T(8,128)(2,1)}, bf16[4,288,384]{2,1,0:T(8,128)(2,1)S(1)}, f32[8,128]{1,0:T(8,128)S(1)}) custom-call(bf16[8,304,256]{2,1,0:T(8,128)(2,1)S(1)} %get-tuple-element.42.left1_ref, bf16[8,304,256]{2,1,0:T(8,128)(2,1)S(1)} %collective-permute-done.left2_ref, ...), custom_call_target="tpu_custom_call" | custom-call | flops 10000000 | bytes 1000 | tf_op jit(solution)/shard_map/weight_grad_send/pallas_call | solution.py:619
  62.6 2.2 %collective-permute-start.2 = (bf16[4,288,384]{2,1,0:T(8,128)(2,1)}, bf16[4,288,384]{2,1,0:T(8,128)(2,1)S(1)}, u32[]{:S(2)}, u32[]{:S(2)}) collective-permute-start(bf16[4,288,384]{2,1,0:T(8,128)(2,1)} %get-tuple-element.54), channel_id=1, source_target_pairs={{0,64},{2,67},{16,80},{18,83},{32,96},{34,99},{48,112},{50,115},{4... | collective-permute-start | bytes 2654216 | tf_op jit(solution)/shard_map/ppermute | solution.py:683
  64.7 0.6 collective-permute-start.3
  65.3 0.8 collective-permute-start.4
  66.1 3.6 %weight_grad_keep.1 = (bf16[200,288,384]{2,1,0:T(8,128)(2,1)}, bf16[64,4,1152]{2,1,0:T(4,128)(2,1)}) custom-call(bf16[8,304,256]{2,1,0:T(8,128)(2,1)S(1)} %get-tuple-element.42.left1_ref, bf16[8,304,256]{2,1,0:T(8,128)(2,1)S(1)} %collective-permute-done.left2_ref, bf16[512,1152]{1,0:T(8,128)(2,1)S(1)} %get-tuple-element.44.right1_ref, ...), custom_call_target="tpu_custom_call" | custom-call | flops 10000000 | bytes 1000 | tf_op jit(solution)/shard_map/weight_grad_keep/pallas_call | solution.py:619
  69.7 7.2 %all-to-all-start.1 = ((bf16[64,4,1152]{2,1,0:T(4,128)(2,1)}), bf16[64,4,1152]{2,1,0:T(4,128)(2,1)}, u32[]{:S(2)}, u32[]{:S(2)}) async-start(bf16[64,4,1152]{2,1,0:T(4,128)(2,1)} %get-tuple-element.47), calls=%async_computation.1 | async-start | bytes 1179648 | tf_op jit(solution)/shard_map/all_to_all | solution.py:731
  76.9 0.0 collective-permute-done.2.refs_1_
  76.9 1.1 collective-permute-done.3.refs_2_
  78.0 0.4 collective-permute-done.4.refs_3_
  78.4 1.4 %second_sums_send.1 = (bf16[2,288,384]{2,1,0:T(8,128)(2,1)S(1)}, bf16[2,288,384]{2,1,0:T(8,128)(2,1)S(1)}, bf16[2,288,384]{2,1,0:T(8,128)(2,1)S(1)}) custom-call(bf16[200,288,384]{2,1,0:T(8,128)(2,1)} %get-tuple-element.53.refs_0_, bf16[4,288,384]{2,1,0:T(8,128)(2,1)S(1)} %collective-permute-done.2.refs_1_, ...), custom_call_target="tpu_custom_call" | custom-call | flops 1000000 | bytes 1000 | tf_op jit(solution)/shard_map/second_sums_send/pallas_call | solution.py:673
  79.8 1.5 %collective-permute-start.5 = (bf16[2,288,384]{2,1,0:T(8,128)(2,1)S(1)}, bf16[2,288,384]{2,1,0:T(8,128)(2,1)S(1)}, u32[]{:S(2)}, u32[]{:S(2)}) collective-permute-start(bf16[2,288,384]{2,1,0:T(8,128)(2,1)S(1)} %get-tuple-element.60), channel_id=1, source_target_pairs={{0,4},{2,14},{16,20},{18,30},{32,36},{34,46},{48,52},{50,62},{4,0}... | collective-permute-start | bytes 1327112 | tf_op jit(solution)/shard_map/ppermute | solution.py:685
  81.3 0.8 collective-permute-start.6
  82.1 1.0 collective-permute-start.7
  83.1 1.4 %second_sums_own.1 = (bf16[2,288,384]{2,1,0:T(8,128)(2,1)S(1)}, bf16[2,288,384]{2,1,0:T(8,128)(2,1)S(1)}, bf16[2,288,384]{2,1,0:T(8,128)(2,1)S(1)}) custom-call(bf16[200,288,384]{2,1,0:T(8,128)(2,1)} %get-tuple-element.53.refs_0_, bf16[4,288,384]{2,1,0:T(8,128)(2,1)S(1)} %collective-permute-done.2.refs_1_, ...), custom_call_target="tpu_custom_call" | custom-call | flops 1000000 | bytes 1000 | tf_op jit(solution)/shard_map/second_sums_own/pallas_call | solution.py:673
  84.5 5.7 %collective-permute-done.5.refs_3_ = bf16[2,288,384]{2,1,0:T(8,128)(2,1)S(1)} collective-permute-done((bf16[2,288,384]{2,1,0:T(8,128)(2,1)S(1)}, bf16[2,288,384]{2,1,0:T(8,128)(2,1)S(1)}, u32[]{:S(2)}, u32[]{:S(2)}) %collective-permute-start.5) | collective-permute-done | bytes 442400 | tf_op jit(solution)/shard_map/ppermute | solution.py:685
  90.2 0.9 collective-permute-done.6.refs_4_
  91.1 0.0 collective-permute-done.7.refs_5_
  91.1 0.3 third_send.1
  91.4 1.0 collective-permute-start.8
  92.4 1.6 %collective-permute-start.9 = (bf16[288,384]{1,0:T(8,128)(2,1)S(1)}, bf16[288,384]{1,0:T(8,128)(2,1)S(1)}, u32[]{:S(2)}, u32[]{:S(2)}) collective-permute-start(bf16[288,384]{1,0:T(8,128)(2,1)S(1)} %get-tuple-element.67), channel_id=1, source_target_pairs={{0,64},{2,67},{16,80},{18,83},{32,96},{34,99},{48,112},{50,115},{4... | collective-permute-start | bytes 663560 | tf_op jit(solution)/shard_map/ppermute | solution.py:688
  94.0 0.3 collective-permute-start.10
  94.3 0.0 all-to-all-done.1.gm_ref.gm_hbm
  94.3 8.8 %spatial_attention_back.1 = (bf16[3456,256]{1,0:T(8,128)(2,1)}, f32[8,128]{1,0:T(8,128)}) custom-call(bf16[64,4,1152]{2,1,0:T(4,128)(2,1)} %all-to-all-done.1.gm_ref.gm_hbm, f32[6,1,1152]{2,1,0:T(1,128)} %bitcast.5, f32[16,1,256]{2,1,0:T(1,128)} %get-tuple-element.48.inv_ref, bf16[280,80,256]{2,1,0:T(8,128)(2,1)} %get-tuple-element.49.kept_hbm, ...), custom_call_target="tpu_custom_call" | custom-call | flops 5000000000 | bytes 12000000 | tf_op jit(solution)/shard_map/spatial_attention_back/pallas_call | solution.py:632
  103.0 0.0 collective-permute-done.8.refs_3_
  103.0 0.0 collective-permute-done.9.refs_4_
  103.1 0.0 collective-permute-done.10.refs_5_
  103.1 0.0 copy-start.1
  103.1 0.7 copy-done.1
  103.8 0.4 fourth_send.1
  104.1 2.6 %collective-permute-start.11 = (bf16[72,1152]{1,0:T(8,128)(2,1)S(1)}, bf16[72,1152]{1,0:T(8,128)(2,1)S(1)}, u32[]{:S(2)}, u32[]{:S(2)}) collective-permute-start(bf16[72,1152]{1,0:T(8,128)(2,1)S(1)} %get-tuple-element.71), channel_id=1, source_target_pairs={{0,12},{2,6},{16,28},{18,22},{32,44},{34,38},{48,60},{50,54},{4,8}... | collective-permute-start | bytes 497672 | tf_op jit(solution)/shard_map/ppermute | solution.py:699
  106.7 1.2 collective-permute-start.12
  107.8 2.3 %collective-permute-start.13 = (bf16[72,1152]{1,0:T(8,128)(2,1)S(1)}, bf16[72,1152]{1,0:T(8,128)(2,1)S(1)}, u32[]{:S(2)}, u32[]{:S(2)}) collective-permute-start(bf16[72,1152]{1,0:T(8,128)(2,1)S(1)} %get-tuple-element.73), channel_id=1, source_target_pairs={{0,77},{2,70},{16,93},{18,86},{32,109},{34,102},{48,125},{50,118},... | collective-permute-start | bytes 497672 | tf_op jit(solution)/shard_map/ppermute | solution.py:699
  110.1 8.1 %spatial_norm_back.1 = (bf16[256,1152]{1,0:T(8,128)(2,1)}, f32[8,128]{1,0:T(8,128)}) custom-call(bf16[3456,256]{1,0:T(8,128)(2,1)} %get-tuple-element.51.grad_ref, bf16[64,4,1152]{2,1,0:T(4,128)(2,1)} %all-to-all-done.1.gm_ref.gm_hbm, bf16[256,1152]{1,0:T(8,128)(2,1)} %bitcast.10, f32[6,1,1152]{2,1,0:T(1,128)} %bitcast.6, bf16[4608,1152]{1,0:T(8,128)(2,1)} %w_hbm.7), custom_call_target="tpu_custom_call" | custom-call | flops 5000000000 | bytes 12000000 | tf_op jit(solution)/shard_map/spatial_norm_back/pallas_call | solution.py:651
  118.2 0.0 collective-permute-done.11.got1_ref
  118.3 0.0 collective-permute-done.12.got2_ref
  118.3 0.0 collective-permute-done.13.got3_ref
  118.3 0.0 copy-start.2
  118.3 0.7 copy-done.2
  119.0 0.2 fifth_send.1
  119.1 3.0 %collective-permute-start.14 = (bf16[36,1152]{1,0:T(8,128)(2,1)S(1)}, bf16[36,1152]{1,0:T(8,128)(2,1)S(1)}, u32[]{:S(2)}, u32[]{:S(2)}) collective-permute-start(bf16[36,1152]{1,0:T(8,128)(2,1)S(1)} %get-tuple-element.76), channel_id=1, source_target_pairs={{0,48},{2,18},{16,32},{18,2},{32,16},{34,50},{48,0},{50,34},{4,52}... | collective-permute-start | bytes 248840 | tf_op jit(solution)/shard_map/ppermute | solution.py:709
  122.1 2.9 %collective-permute-done.14.got_ref = bf16[36,1152]{1,0:T(8,128)(2,1)S(1)} collective-permute-done((bf16[36,1152]{1,0:T(8,128)(2,1)S(1)}, bf16[36,1152]{1,0:T(8,128)(2,1)S(1)}, u32[]{:S(2)}, u32[]{:S(2)}) %collective-permute-start.14) | collective-permute-done | bytes 82976 | tf_op jit(solution)/shard_map/ppermute | solution.py:709
  125.0 0.7 last_sum.1
Async XLA Ops:
  11.6 28.3 %copy-start = (f32[1,6,1152]{2,0,1:T(1,128)S(1)}, f32[1,6,1152]{2,0,1:T(1,128)}, u32[]{:S(2)}) copy-start(f32[1,6,1152]{2,0,1:T(1,128)} %param.6) | copy-start | bytes 82948
  55.3 4.7 %collective-permute-start = (bf16[8,304,256]{2,1,0:T(8,128)(2,1)S(1)}, bf16[8,304,256]{2,1,0:T(8,128)(2,1)S(1)}, u32[]{:S(2)}, u32[]{:S(2)}) collective-permute-start(bf16[8,304,256]{2,1,0:T(8,128)(2,1)S(1)} %get-tuple-element.43), channel_id=1, source_target_pairs={{0,2},{2,0},{16,18},{18,16},{32,34},{34,32},{48,50},{50,48},{4,6},... | collective-permute-start | bytes 3735560 | tf_op jit(solution)/shard_map/ppermute | solution.py:728
  55.4 4.6 %collective-permute-start.1 = (bf16[512,1152]{1,0:T(8,128)(2,1)S(1)}, bf16[512,1152]{1,0:T(8,128)(2,1)S(1)}, u32[]{:S(2)}, u32[]{:S(2)}) collective-permute-start(bf16[512,1152]{1,0:T(8,128)(2,1)S(1)} %get-tuple-element.44.right1_ref), channel_id=1, source_target_pairs={{0,2},{2,0},{16,18},{18,16},{32,34},{34,32},{48,50},{50,48},{4,6},... | collective-permute-start | bytes 3538952 | tf_op jit(solution)/shard_map/ppermute | solution.py:728
  62.6 14.3 %collective-permute-start.2 = (bf16[4,288,384]{2,1,0:T(8,128)(2,1)}, bf16[4,288,384]{2,1,0:T(8,128)(2,1)S(1)}, u32[]{:S(2)}, u32[]{:S(2)}) collective-permute-start(bf16[4,288,384]{2,1,0:T(8,128)(2,1)} %get-tuple-element.54), channel_id=1, source_target_pairs={{0,64},{2,67},{16,80},{18,83},{32,96},{34,99},{48,112},{50,115},{4... | collective-permute-start | bytes 2654216 | tf_op jit(solution)/shard_map/ppermute | solution.py:683
  64.7 13.3 %collective-permute-start.3 = (bf16[4,288,384]{2,1,0:T(8,128)(2,1)}, bf16[4,288,384]{2,1,0:T(8,128)(2,1)S(1)}, u32[]{:S(2)}, u32[]{:S(2)}) collective-permute-start(bf16[4,288,384]{2,1,0:T(8,128)(2,1)} %get-tuple-element.55), channel_id=1, source_target_pairs={{0,4},{2,14},{16,20},{18,30},{32,36},{34,46},{48,52},{50,62},{4,0}... | collective-permute-start | bytes 2654216 | tf_op jit(solution)/shard_map/ppermute | solution.py:683
  65.3 13.0 %collective-permute-start.4 = (bf16[4,288,384]{2,1,0:T(8,128)(2,1)S(1)}, bf16[4,288,384]{2,1,0:T(8,128)(2,1)S(1)}, u32[]{:S(2)}, u32[]{:S(2)}) collective-permute-start(bf16[4,288,384]{2,1,0:T(8,128)(2,1)S(1)} %get-tuple-element.56), channel_id=1, source_target_pairs={{0,16},{2,50},{16,0},{18,34},{32,48},{34,18},{48,32},{50,2},{4,20}... | collective-permute-start | bytes 2654216 | tf_op jit(solution)/shard_map/ppermute | solution.py:683
  69.7 24.6 %all-to-all-start.1 = ((bf16[64,4,1152]{2,1,0:T(4,128)(2,1)}), bf16[64,4,1152]{2,1,0:T(4,128)(2,1)}, u32[]{:S(2)}, u32[]{:S(2)}) async-start(bf16[64,4,1152]{2,1,0:T(4,128)(2,1)} %get-tuple-element.47), calls=%async_computation.1 | async-start | bytes 1179648 | tf_op jit(solution)/shard_map/all_to_all | solution.py:731
  79.8 10.4 %collective-permute-start.5 = (bf16[2,288,384]{2,1,0:T(8,128)(2,1)S(1)}, bf16[2,288,384]{2,1,0:T(8,128)(2,1)S(1)}, u32[]{:S(2)}, u32[]{:S(2)}) collective-permute-start(bf16[2,288,384]{2,1,0:T(8,128)(2,1)S(1)} %get-tuple-element.60), channel_id=1, source_target_pairs={{0,4},{2,14},{16,20},{18,30},{32,36},{34,46},{48,52},{50,62},{4,0}... | collective-permute-start | bytes 1327112 | tf_op jit(solution)/shard_map/ppermute | solution.py:685
  81.3 9.8 %collective-permute-start.6 = (bf16[2,288,384]{2,1,0:T(8,128)(2,1)S(1)}, bf16[2,288,384]{2,1,0:T(8,128)(2,1)S(1)}, u32[]{:S(2)}, u32[]{:S(2)}) collective-permute-start(bf16[2,288,384]{2,1,0:T(8,128)(2,1)S(1)} %get-tuple-element.61), channel_id=1, source_target_pairs={{0,16},{2,50},{16,0},{18,34},{32,48},{34,18},{48,32},{50,2},{4,20}... | collective-permute-start | bytes 1327112 | tf_op jit(solution)/shard_map/ppermute | solution.py:685
  82.1 9.0 %collective-permute-start.7 = (bf16[2,288,384]{2,1,0:T(8,128)(2,1)S(1)}, bf16[2,288,384]{2,1,0:T(8,128)(2,1)S(1)}, u32[]{:S(2)}, u32[]{:S(2)}) collective-permute-start(bf16[2,288,384]{2,1,0:T(8,128)(2,1)S(1)} %get-tuple-element.62), channel_id=1, source_target_pairs={{0,64},{2,67},{16,80},{18,83},{32,96},{34,99},{48,112},{50,115},{4... | collective-permute-start | bytes 1327112 | tf_op jit(solution)/shard_map/ppermute | solution.py:685
  91.4 11.6 %collective-permute-start.8 = (bf16[288,384]{1,0:T(8,128)(2,1)S(1)}, bf16[288,384]{1,0:T(8,128)(2,1)S(1)}, u32[]{:S(2)}, u32[]{:S(2)}) collective-permute-start(bf16[288,384]{1,0:T(8,128)(2,1)S(1)} %get-tuple-element.66), channel_id=1, source_target_pairs={{0,16},{2,50},{16,0},{18,34},{32,48},{34,18},{48,32},{50,2},{4,20}... | collective-permute-start | bytes 663560 | tf_op jit(solution)/shard_map/ppermute | solution.py:688
  92.4 10.7 %collective-permute-start.9 = (bf16[288,384]{1,0:T(8,128)(2,1)S(1)}, bf16[288,384]{1,0:T(8,128)(2,1)S(1)}, u32[]{:S(2)}, u32[]{:S(2)}) collective-permute-start(bf16[288,384]{1,0:T(8,128)(2,1)S(1)} %get-tuple-element.67), channel_id=1, source_target_pairs={{0,64},{2,67},{16,80},{18,83},{32,96},{34,99},{48,112},{50,115},{4... | collective-permute-start | bytes 663560 | tf_op jit(solution)/shard_map/ppermute | solution.py:688
  94.0 9.1 %collective-permute-start.10 = (bf16[288,384]{1,0:T(8,128)(2,1)S(1)}, bf16[288,384]{1,0:T(8,128)(2,1)S(1)}, u32[]{:S(2)}, u32[]{:S(2)}) collective-permute-start(bf16[288,384]{1,0:T(8,128)(2,1)S(1)} %get-tuple-element.68), channel_id=1, source_target_pairs={{0,4},{2,14},{16,20},{18,30},{32,36},{34,46},{48,52},{50,62},{4,0}... | collective-permute-start | bytes 663560 | tf_op jit(solution)/shard_map/ppermute | solution.py:688
  103.1 0.7 copy-start.1
  104.1 14.1 %collective-permute-start.11 = (bf16[72,1152]{1,0:T(8,128)(2,1)S(1)}, bf16[72,1152]{1,0:T(8,128)(2,1)S(1)}, u32[]{:S(2)}, u32[]{:S(2)}) collective-permute-start(bf16[72,1152]{1,0:T(8,128)(2,1)S(1)} %get-tuple-element.71), channel_id=1, source_target_pairs={{0,12},{2,6},{16,28},{18,22},{32,44},{34,38},{48,60},{50,54},{4,8}... | collective-permute-start | bytes 497672 | tf_op jit(solution)/shard_map/ppermute | solution.py:699
  106.7 11.6 %collective-permute-start.12 = (bf16[72,1152]{1,0:T(8,128)(2,1)S(1)}, bf16[72,1152]{1,0:T(8,128)(2,1)S(1)}, u32[]{:S(2)}, u32[]{:S(2)}) collective-permute-start(bf16[72,1152]{1,0:T(8,128)(2,1)S(1)} %get-tuple-element.72), channel_id=1, source_target_pairs={{0,65},{2,66},{16,81},{18,82},{32,97},{34,98},{48,113},{50,114},{4... | collective-permute-start | bytes 497672 | tf_op jit(solution)/shard_map/ppermute | solution.py:699
  107.8 10.4 %collective-permute-start.13 = (bf16[72,1152]{1,0:T(8,128)(2,1)S(1)}, bf16[72,1152]{1,0:T(8,128)(2,1)S(1)}, u32[]{:S(2)}, u32[]{:S(2)}) collective-permute-start(bf16[72,1152]{1,0:T(8,128)(2,1)S(1)} %get-tuple-element.73), channel_id=1, source_target_pairs={{0,77},{2,70},{16,93},{18,86},{32,109},{34,102},{48,125},{50,118},... | collective-permute-start | bytes 497672 | tf_op jit(solution)/shard_map/ppermute | solution.py:699
  118.3 0.7 copy-start.2
  119.1 5.8 %collective-permute-start.14 = (bf16[36,1152]{1,0:T(8,128)(2,1)S(1)}, bf16[36,1152]{1,0:T(8,128)(2,1)S(1)}, u32[]{:S(2)}, u32[]{:S(2)}) collective-permute-start(bf16[36,1152]{1,0:T(8,128)(2,1)S(1)} %get-tuple-element.76), channel_id=1, source_target_pairs={{0,48},{2,18},{16,32},{18,2},{32,16},{34,50},{48,0},{50,34},{4,52}... | collective-permute-start | bytes 248840 | tf_op jit(solution)/shard_map/ppermute | solution.py:709

commit v5 on v4

--- a/solution.py
+++ b/solution.py
@@ -644,6 +644,7 @@
         [VMEM] * 3 + [ANY] * 3,
         5_000_000_000,
         "spatial_attention_back",
+        limit=51,
     )(gm, mod, inv, kept, raw, w)
 
 
@@ -663,6 +664,7 @@
         [VMEM, ANY, ANY, VMEM, ANY],
         5_000_000_000,
         "spatial_norm_back",
+        limit=51,
     )(grad, gm, x, mod, w)
 
 

time: 126 us -> 123 us (0.976)
  Pallas kernels: 53.8 us -> 50.9 us
    pallas_call x1, Pallas kernels: 8.76 us -> 6.45 us  [spatial_attention_back(): call(spatial_attention_back_kernel, [((3 * D, T), bf16), TOKEN], [W_OUT,...]
    pallas_call x1, Pallas kernels: 8.12 us -> 6.63 us  [spatial_norm_back(): call(spatial_norm_back_kernel, [TOKENS, TOKEN], [pltpu.VMEM((3 * D, D), b...]
  transfers between devices with their start and end apart: 16 -> 16, of which waited for: 6 -> 6; matrix products, arithmetic and copies ran while one was open for 0% -> 0% of each run, Pallas kernels for 19% -> 16%
where the time goes in v5:
time: 123 us; the launch traced here: 122 us
  Pallas kernels  50.9 us (41%)
  blocking collectives  28.3 us (23%)
  starting transfers between devices  26.6 us (22%)
  waiting for transfers between devices  14.8 us (12%)
    all_to_all x1, blocking collectives, on_device(): both_pos = lax.all_to_all(both, 'seq', 0, 0, tiled=True)  28.3 us
    pallas_call x1, Pallas kernels, temporal(): call(temporal_kernel, [((FRAMES, PLACE, D), bf16), RIGHT, LEFT, LEFT], [W...  15.4 us
    pallas_call x1, Pallas kernels, spatial_forward(): call(spatial_forward_kernel, [((FRAMES, 2 * PLACE, D), bf16), KEPT, KEPT_...  11 us
    pallas_call x2, Pallas kernels, weight_grad(): call(functools.partial(weight_grad_kernel, flip), [part] * 3 + [TOKEN] if...  7.14 us
    all_to_all x1, starting transfers between devices, on_device(): gm = lax.all_to_all(gm_pos, 'seq', 0, 0, tiled=True)  6.99 us
    ppermute x3, waiting for transfers between devices, reduce_rows(): lax.ppermute(out[p], BOTH, flip_pairs((p + 1) % 3, (0, 1)))  6.73 us
    pallas_call x1, Pallas kernels, spatial_norm_back(): call(spatial_norm_back_kernel, [TOKENS, TOKEN], [pltpu.VMEM((3 * D, D), b...  6.63 us
    pallas_call x1, Pallas kernels, spatial_attention_back(): call(spatial_attention_back_kernel, [((3 * D, T), bf16), TOKEN], [W_OUT,...  6.45 us
  transfers between devices with their start and end apart: 16, of which 6 were waited for; matrix products, arithmetic and copies ran while one was open for 0% of the time, Pallas kernels for 16%

profile of v5, /device:TPU:0, one launch (start us, length us, event | category | flops | bytes accessed | tf_op | source)
XLA Modules:
  0.0 122.3 jit_solution(8537472220262436918)
XLA Ops:
  0.6 11.0 %spatial_forward.1 = (bf16[64,8,1152]{2,1,0:T(8,128)(2,1)}, bf16[280,80,256]{2,1,0:T(8,128)(2,1)}, bf16[88,256,256]{2,1,0:T(8,128)(2,1)}, f32[16,1,256]{2,1,0:T(1,128)}) custom-call(bf16[256,1152]{1,0:T(8,128)(2,1)} %bitcast.8, bf16[256,1152]{1,0:T(8,128)(2,1)} %bitcast.10, f32[6,1,1152]{2,1,0:T(1,128)} %bitcast.4, bf16[4608,1152]{1,0:T(8,128)(2,1)} %w_hbm.7), custom_call_target="tpu_custom_call" | custom-call | flops 6000000000 | bytes 12000000 | tf_op jit(solution)/shard_map/spatial_forward/pallas_call | solution.py:555
  11.6 0.0 copy-start.1
  11.6 28.3 %all_to_all.10.both_hbm = bf16[64,8,1152]{2,1,0:T(8,128)(2,1)S(1)} all-to-all(bf16[64,8,1152]{2,1,0:T(8,128)(2,1)} %get-tuple-element.41), channel_id=1, replica_groups=mesh['seq'=64,'rep'=2] {'seq'}, dimensions={0} | all-to-all | bytes 2359296 | tf_op jit(solution)/shard_map/all_to_all | solution.py:728
  39.9 0.0 copy-done.1
  39.9 15.4 %temporal_sublayer.1 = (bf16[64,4,1152]{2,1,0:T(4,128)(2,1)S(1)}, bf16[512,1152]{1,0:T(8,128)(2,1)S(1)}, bf16[8,304,256]{2,1,0:T(8,128)(2,1)S(1)}, bf16[8,304,256]{2,1,0:T(8,128)(2,1)S(1)}) custom-call(bf16[64,8,1152]{2,1,0:T(8,128)(2,1)S(1)} %all_to_all.10.both_hbm, f32[6,1,1152]{2,1,0:T(1,128)S(1)} %bitcast.5, bf16[4608,1152]{1,0:T(8,128)(2,1)} %w_hbm.5), custom_call_target="tpu_custom_call" | custom-call | flops 12000000000 | bytes 12000000 | tf_op jit(solution)/shard_map/temporal_sublayer/pallas_call | solution.py:582
  55.3 0.1 collective-permute-start
  55.4 0.5 collective-permute-start.1
  55.9 4.1 %collective-permute-done.1.right2_ref = bf16[512,1152]{1,0:T(8,128)(2,1)S(1)} collective-permute-done((bf16[512,1152]{1,0:T(8,128)(2,1)S(1)}, bf16[512,1152]{1,0:T(8,128)(2,1)S(1)}, u32[]{:S(2)}, u32[]{:S(2)}) %collective-permute-start.1) | collective-permute-done | bytes 1179680 | tf_op jit(solution)/shard_map/ppermute | solution.py:730
  60.0 0.0 collective-permute-done.left2_ref
  60.0 3.5 %weight_grad_send.1 = (bf16[4,288,384]{2,1,0:T(8,128)(2,1)}, bf16[4,288,384]{2,1,0:T(8,128)(2,1)}, bf16[4,288,384]{2,1,0:T(8,128)(2,1)}, f32[8,128]{1,0:T(8,128)S(1)}) custom-call(bf16[8,304,256]{2,1,0:T(8,128)(2,1)S(1)} %get-tuple-element.42.left1_ref, bf16[8,304,256]{2,1,0:T(8,128)(2,1)S(1)} %collective-permute-done.left2_ref, ...), custom_call_target="tpu_custom_call" | custom-call | flops 10000000 | bytes 1000 | tf_op jit(solution)/shard_map/weight_grad_send/pallas_call | solution.py:619
  63.5 2.2 %collective-permute-start.2 = (bf16[4,288,384]{2,1,0:T(8,128)(2,1)}, bf16[4,288,384]{2,1,0:T(8,128)(2,1)S(1)}, u32[]{:S(2)}, u32[]{:S(2)}) collective-permute-start(bf16[4,288,384]{2,1,0:T(8,128)(2,1)} %get-tuple-element.54), channel_id=1, source_target_pairs={{0,64},{2,67},{16,80},{18,83},{32,96},{34,99},{48,112},{50,115},{4... | collective-permute-start | bytes 2654216 | tf_op jit(solution)/shard_map/ppermute | solution.py:685
  65.7 0.6 collective-permute-start.3
  66.3 0.8 collective-permute-start.4
  67.1 3.6 %weight_grad_keep.1 = (bf16[200,288,384]{2,1,0:T(8,128)(2,1)}, bf16[64,4,1152]{2,1,0:T(4,128)(2,1)S(1)}) custom-call(bf16[8,304,256]{2,1,0:T(8,128)(2,1)S(1)} %get-tuple-element.42.left1_ref, bf16[8,304,256]{2,1,0:T(8,128)(2,1)S(1)} %collective-permute-done.left2_ref, bf16[512,1152]{1,0:T(8,128)(2,1)S(1)} %get-tuple-element.44.right1_ref, ...), custom_call_target="tpu_custom_call" | custom-call | flops 10000000 | bytes 1000 | tf_op jit(solution)/shard_map/weight_grad_keep/pallas_call | solution.py:619
  70.7 0.0 copy-start
  70.7 0.8 copy-done
  71.5 7.0 %all-to-all-start.1 = ((bf16[64,4,1152]{2,1,0:T(4,128)(2,1)}), bf16[64,4,1152]{2,1,0:T(4,128)(2,1)S(1)}, u32[]{:S(2)}, u32[]{:S(2)}) async-start(bf16[64,4,1152]{2,1,0:T(4,128)(2,1)} %copy-done), calls=%async_computation.1 | async-start | bytes 1179648 | tf_op jit(solution)/shard_map/all_to_all | solution.py:733
  78.5 0.0 collective-permute-done.2.refs_1_
  78.5 0.4 collective-permute-done.3.refs_2_
  78.9 0.6 collective-permute-done.4.refs_3_
  79.5 1.4 %second_sums_send.1 = (bf16[2,288,384]{2,1,0:T(8,128)(2,1)S(1)}, bf16[2,288,384]{2,1,0:T(8,128)(2,1)S(1)}, bf16[2,288,384]{2,1,0:T(8,128)(2,1)S(1)}) custom-call(bf16[200,288,384]{2,1,0:T(8,128)(2,1)} %get-tuple-element.53.refs_0_, bf16[4,288,384]{2,1,0:T(8,128)(2,1)S(1)} %collective-permute-done.2.refs_1_, ...), custom_call_target="tpu_custom_call" | custom-call | flops 1000000 | bytes 1000 | tf_op jit(solution)/shard_map/second_sums_send/pallas_call | solution.py:675
  81.0 1.5 %collective-permute-start.5 = (bf16[2,288,384]{2,1,0:T(8,128)(2,1)S(1)}, bf16[2,288,384]{2,1,0:T(8,128)(2,1)S(1)}, u32[]{:S(2)}, u32[]{:S(2)}) collective-permute-start(bf16[2,288,384]{2,1,0:T(8,128)(2,1)S(1)} %get-tuple-element.60), channel_id=1, source_target_pairs={{0,4},{2,14},{16,20},{18,30},{32,36},{34,46},{48,52},{50,62},{4,0}... | collective-permute-start | bytes 1327112 | tf_op jit(solution)/shard_map/ppermute | solution.py:687
  82.5 0.8 collective-permute-start.6
  83.3 1.5 %collective-permute-start.7 = (bf16[2,288,384]{2,1,0:T(8,128)(2,1)S(1)}, bf16[2,288,384]{2,1,0:T(8,128)(2,1)S(1)}, u32[]{:S(2)}, u32[]{:S(2)}) collective-permute-start(bf16[2,288,384]{2,1,0:T(8,128)(2,1)S(1)} %get-tuple-element.62), channel_id=1, source_target_pairs={{0,64},{2,67},{16,80},{18,83},{32,96},{34,99},{48,112},{50,115},{4... | collective-permute-start | bytes 1327112 | tf_op jit(solution)/shard_map/ppermute | solution.py:687
  84.7 1.4 %second_sums_own.1 = (bf16[2,288,384]{2,1,0:T(8,128)(2,1)S(1)}, bf16[2,288,384]{2,1,0:T(8,128)(2,1)S(1)}, bf16[2,288,384]{2,1,0:T(8,128)(2,1)S(1)}) custom-call(bf16[200,288,384]{2,1,0:T(8,128)(2,1)} %get-tuple-element.53.refs_0_, bf16[4,288,384]{2,1,0:T(8,128)(2,1)S(1)} %collective-permute-done.2.refs_1_, ...), custom_call_target="tpu_custom_call" | custom-call | flops 1000000 | bytes 1000 | tf_op jit(solution)/shard_map/second_sums_own/pallas_call | solution.py:675
  86.2 5.8 %collective-permute-done.5.refs_3_ = bf16[2,288,384]{2,1,0:T(8,128)(2,1)S(1)} collective-permute-done((bf16[2,288,384]{2,1,0:T(8,128)(2,1)S(1)}, bf16[2,288,384]{2,1,0:T(8,128)(2,1)S(1)}, u32[]{:S(2)}, u32[]{:S(2)}) %collective-permute-start.5) | collective-permute-done | bytes 442400 | tf_op jit(solution)/shard_map/ppermute | solution.py:687
  92.0 0.9 collective-permute-done.6.refs_4_
  92.9 0.0 collective-permute-done.7.refs_5_
  92.9 0.0 copy-start.2
  92.9 0.3 third_send.1
  93.2 1.0 collective-permute-start.8
  94.2 1.5 %collective-permute-start.9 = (bf16[288,384]{1,0:T(8,128)(2,1)S(1)}, bf16[288,384]{1,0:T(8,128)(2,1)S(1)}, u32[]{:S(2)}, u32[]{:S(2)}) collective-permute-start(bf16[288,384]{1,0:T(8,128)(2,1)S(1)} %get-tuple-element.67), channel_id=1, source_target_pairs={{0,64},{2,67},{16,80},{18,83},{32,96},{34,99},{48,112},{50,115},{4... | collective-permute-start | bytes 663560 | tf_op jit(solution)/shard_map/ppermute | solution.py:690
  95.7 0.4 collective-permute-start.10
  96.1 0.0 all-to-all-done.1.gm_ref.gm_hbm
  96.1 0.0 copy-done.2
  96.1 6.4 %spatial_attention_back.1 = (bf16[3456,256]{1,0:T(8,128)(2,1)S(1)}, f32[8,128]{1,0:T(8,128)S(1)}) custom-call(bf16[64,4,1152]{2,1,0:T(4,128)(2,1)S(1)} %all-to-all-done.1.gm_ref.gm_hbm, f32[6,1,1152]{2,1,0:T(1,128)S(1)} %bitcast.6, f32[16,1,256]{2,1,0:T(1,128)S(1)} %copy-done.2, bf16[280,80,256]{2,1,0:T(8,128)(2,1)} %get-tuple-element.49.kept_hbm, ...), custom_call_target="tpu_custom_call" | custom-call | flops 5000000000 | bytes 12000000 | tf_op jit(solution)/shard_map/spatial_attention_back/pallas_call | solution.py:632
  102.5 0.0 copy-start.3
  102.6 0.0 collective-permute-done.8.refs_3_
  102.6 0.0 collective-permute-done.9.refs_4_
  102.6 0.0 collective-permute-done.10.refs_5_
  102.6 0.4 fourth_send.1
  103.0 2.6 %collective-permute-start.11 = (bf16[72,1152]{1,0:T(8,128)(2,1)S(1)}, bf16[72,1152]{1,0:T(8,128)(2,1)S(1)}, u32[]{:S(2)}, u32[]{:S(2)}) collective-permute-start(bf16[72,1152]{1,0:T(8,128)(2,1)S(1)} %get-tuple-element.71), channel_id=1, source_target_pairs={{0,12},{2,6},{16,28},{18,22},{32,44},{34,38},{48,60},{50,54},{4,8}... | collective-permute-start | bytes 497672 | tf_op jit(solution)/shard_map/ppermute | solution.py:701
  105.5 1.1 collective-permute-start.12
  106.7 2.3 %collective-permute-start.13 = (bf16[72,1152]{1,0:T(8,128)(2,1)S(1)}, bf16[72,1152]{1,0:T(8,128)(2,1)S(1)}, u32[]{:S(2)}, u32[]{:S(2)}) collective-permute-start(bf16[72,1152]{1,0:T(8,128)(2,1)S(1)} %get-tuple-element.73), channel_id=1, source_target_pairs={{0,77},{2,70},{16,93},{18,86},{32,109},{34,102},{48,125},{50,118},... | collective-permute-start | bytes 497672 | tf_op jit(solution)/shard_map/ppermute | solution.py:701
  108.9 0.0 copy-done.3
  108.9 6.6 %spatial_norm_back.1 = (bf16[256,1152]{1,0:T(8,128)(2,1)}, f32[8,128]{1,0:T(8,128)S(1)}) custom-call(bf16[3456,256]{1,0:T(8,128)(2,1)S(1)} %get-tuple-element.51.grad_ref, bf16[64,4,1152]{2,1,0:T(4,128)(2,1)S(1)} %all-to-all-done.1.gm_ref.gm_hbm, bf16[256,1152]{1,0:T(8,128)(2,1)S(1)} %bitcast.9, f32[6,1,1152]{2,1,0:T(1,128)S(1)} %bitcast.7, ...), custom_call_target="tpu_custom_call" | custom-call | flops 5000000000 | bytes 12000000 | tf_op jit(solution)/shard_map/spatial_norm_back/pallas_call | solution.py:652
  115.6 0.0 collective-permute-done.11.got1_ref
  115.6 0.0 collective-permute-done.12.got2_ref
  115.6 0.0 collective-permute-done.13.got3_ref
  115.6 0.2 fifth_send.1
  115.8 2.9 %collective-permute-start.14 = (bf16[36,1152]{1,0:T(8,128)(2,1)S(1)}, bf16[36,1152]{1,0:T(8,128)(2,1)S(1)}, u32[]{:S(2)}, u32[]{:S(2)}) collective-permute-start(bf16[36,1152]{1,0:T(8,128)(2,1)S(1)} %get-tuple-element.76), channel_id=1, source_target_pairs={{0,48},{2,18},{16,32},{18,2},{32,16},{34,50},{48,0},{50,34},{4,52}... | collective-permute-start | bytes 248840 | tf_op jit(solution)/shard_map/ppermute | solution.py:711
  118.7 2.9 %collective-permute-done.14.got_ref = bf16[36,1152]{1,0:T(8,128)(2,1)S(1)} collective-permute-done((bf16[36,1152]{1,0:T(8,128)(2,1)S(1)}, bf16[36,1152]{1,0:T(8,128)(2,1)S(1)}, u32[]{:S(2)}, u32[]{:S(2)}) %collective-permute-start.14) | collective-permute-done | bytes 82976 | tf_op jit(solution)/shard_map/ppermute | solution.py:711
  121.6 0.7 last_sum.1
Async XLA Ops:
  11.6 28.3 %copy-start.1 = (f32[1,6,1152]{2,0,1:T(1,128)S(1)}, f32[1,6,1152]{2,0,1:T(1,128)}, u32[]{:S(2)}) copy-start(f32[1,6,1152]{2,0,1:T(1,128)} %param.6) | copy-start | bytes 82948
  55.3 4.7 %collective-permute-start = (bf16[8,304,256]{2,1,0:T(8,128)(2,1)S(1)}, bf16[8,304,256]{2,1,0:T(8,128)(2,1)S(1)}, u32[]{:S(2)}, u32[]{:S(2)}) collective-permute-start(bf16[8,304,256]{2,1,0:T(8,128)(2,1)S(1)} %get-tuple-element.43), channel_id=1, source_target_pairs={{0,2},{2,0},{16,18},{18,16},{32,34},{34,32},{48,50},{50,48},{4,6},... | collective-permute-start | bytes 3735560 | tf_op jit(solution)/shard_map/ppermute | solution.py:730
  55.4 4.6 %collective-permute-start.1 = (bf16[512,1152]{1,0:T(8,128)(2,1)S(1)}, bf16[512,1152]{1,0:T(8,128)(2,1)S(1)}, u32[]{:S(2)}, u32[]{:S(2)}) collective-permute-start(bf16[512,1152]{1,0:T(8,128)(2,1)S(1)} %get-tuple-element.44.right1_ref), channel_id=1, source_target_pairs={{0,2},{2,0},{16,18},{18,16},{32,34},{34,32},{48,50},{50,48},{4,6},... | collective-permute-start | bytes 3538952 | tf_op jit(solution)/shard_map/ppermute | solution.py:730
  63.5 15.0 %collective-permute-start.2 = (bf16[4,288,384]{2,1,0:T(8,128)(2,1)}, bf16[4,288,384]{2,1,0:T(8,128)(2,1)S(1)}, u32[]{:S(2)}, u32[]{:S(2)}) collective-permute-start(bf16[4,288,384]{2,1,0:T(8,128)(2,1)} %get-tuple-element.54), channel_id=1, source_target_pairs={{0,64},{2,67},{16,80},{18,83},{32,96},{34,99},{48,112},{50,115},{4... | collective-permute-start | bytes 2654216 | tf_op jit(solution)/shard_map/ppermute | solution.py:685
  65.7 13.3 %collective-permute-start.3 = (bf16[4,288,384]{2,1,0:T(8,128)(2,1)}, bf16[4,288,384]{2,1,0:T(8,128)(2,1)S(1)}, u32[]{:S(2)}, u32[]{:S(2)}) collective-permute-start(bf16[4,288,384]{2,1,0:T(8,128)(2,1)} %get-tuple-element.55), channel_id=1, source_target_pairs={{0,4},{2,14},{16,20},{18,30},{32,36},{34,46},{48,52},{50,62},{4,0}... | collective-permute-start | bytes 2654216 | tf_op jit(solution)/shard_map/ppermute | solution.py:685
  66.3 13.3 %collective-permute-start.4 = (bf16[4,288,384]{2,1,0:T(8,128)(2,1)}, bf16[4,288,384]{2,1,0:T(8,128)(2,1)S(1)}, u32[]{:S(2)}, u32[]{:S(2)}) collective-permute-start(bf16[4,288,384]{2,1,0:T(8,128)(2,1)} %get-tuple-element.56), channel_id=1, source_target_pairs={{0,16},{2,50},{16,0},{18,34},{32,48},{34,18},{48,32},{50,2},{4,20}... | collective-permute-start | bytes 2654216 | tf_op jit(solution)/shard_map/ppermute | solution.py:685
  70.7 0.8 copy-start
  71.5 24.6 %all-to-all-start.1 = ((bf16[64,4,1152]{2,1,0:T(4,128)(2,1)}), bf16[64,4,1152]{2,1,0:T(4,128)(2,1)S(1)}, u32[]{:S(2)}, u32[]{:S(2)}) async-start(bf16[64,4,1152]{2,1,0:T(4,128)(2,1)} %copy-done), calls=%async_computation.1 | async-start | bytes 1179648 | tf_op jit(solution)/shard_map/all_to_all | solution.py:733
  81.0 11.0 %collective-permute-start.5 = (bf16[2,288,384]{2,1,0:T(8,128)(2,1)S(1)}, bf16[2,288,384]{2,1,0:T(8,128)(2,1)S(1)}, u32[]{:S(2)}, u32[]{:S(2)}) collective-permute-start(bf16[2,288,384]{2,1,0:T(8,128)(2,1)S(1)} %get-tuple-element.60), channel_id=1, source_target_pairs={{0,4},{2,14},{16,20},{18,30},{32,36},{34,46},{48,52},{50,62},{4,0}... | collective-permute-start | bytes 1327112 | tf_op jit(solution)/shard_map/ppermute | solution.py:687
  82.5 10.4 %collective-permute-start.6 = (bf16[2,288,384]{2,1,0:T(8,128)(2,1)S(1)}, bf16[2,288,384]{2,1,0:T(8,128)(2,1)S(1)}, u32[]{:S(2)}, u32[]{:S(2)}) collective-permute-start(bf16[2,288,384]{2,1,0:T(8,128)(2,1)S(1)} %get-tuple-element.61), channel_id=1, source_target_pairs={{0,16},{2,50},{16,0},{18,34},{32,48},{34,18},{48,32},{50,2},{4,20}... | collective-permute-start | bytes 1327112 | tf_op jit(solution)/shard_map/ppermute | solution.py:687
  83.3 9.6 %collective-permute-start.7 = (bf16[2,288,384]{2,1,0:T(8,128)(2,1)S(1)}, bf16[2,288,384]{2,1,0:T(8,128)(2,1)S(1)}, u32[]{:S(2)}, u32[]{:S(2)}) collective-permute-start(bf16[2,288,384]{2,1,0:T(8,128)(2,1)S(1)} %get-tuple-element.62), channel_id=1, source_target_pairs={{0,64},{2,67},{16,80},{18,83},{32,96},{34,99},{48,112},{50,115},{4... | collective-permute-start | bytes 1327112 | tf_op jit(solution)/shard_map/ppermute | solution.py:687
  92.9 3.2 %copy-start.2 = (f32[16,1,256]{2,1,0:T(1,128)S(1)}, f32[16,1,256]{2,1,0:T(1,128)}, u32[]{:S(2)}) copy-start(f32[16,1,256]{2,1,0:T(1,128)} %get-tuple-element.48.inv_ref) | copy-start | bytes 49156
  93.2 9.3 %collective-permute-start.8 = (bf16[288,384]{1,0:T(8,128)(2,1)S(1)}, bf16[288,384]{1,0:T(8,128)(2,1)S(1)}, u32[]{:S(2)}, u32[]{:S(2)}) collective-permute-start(bf16[288,384]{1,0:T(8,128)(2,1)S(1)} %get-tuple-element.66), channel_id=1, source_target_pairs={{0,16},{2,50},{16,0},{18,34},{32,48},{34,18},{48,32},{50,2},{4,20}... | collective-permute-start | bytes 663560 | tf_op jit(solution)/shard_map/ppermute | solution.py:690
  94.2 8.4 %collective-permute-start.9 = (bf16[288,384]{1,0:T(8,128)(2,1)S(1)}, bf16[288,384]{1,0:T(8,128)(2,1)S(1)}, u32[]{:S(2)}, u32[]{:S(2)}) collective-permute-start(bf16[288,384]{1,0:T(8,128)(2,1)S(1)} %get-tuple-element.67), channel_id=1, source_target_pairs={{0,64},{2,67},{16,80},{18,83},{32,96},{34,99},{48,112},{50,115},{4... | collective-permute-start | bytes 663560 | tf_op jit(solution)/shard_map/ppermute | solution.py:690
  95.7 6.9 %collective-permute-start.10 = (bf16[288,384]{1,0:T(8,128)(2,1)S(1)}, bf16[288,384]{1,0:T(8,128)(2,1)S(1)}, u32[]{:S(2)}, u32[]{:S(2)}) collective-permute-start(bf16[288,384]{1,0:T(8,128)(2,1)S(1)} %get-tuple-element.68), channel_id=1, source_target_pairs={{0,4},{2,14},{16,20},{18,30},{32,36},{34,46},{48,52},{50,62},{4,0}... | collective-permute-start | bytes 663560 | tf_op jit(solution)/shard_map/ppermute | solution.py:690
  102.5 6.4 %copy-start.3 = (bf16[1,1,256,1152]{3,2,1,0:T(8,128)(2,1)S(1)}, bf16[1,1,256,1152]{3,2,1,0:T(8,128)(2,1)}, u32[]{:S(2)}) copy-start(bf16[1,1,256,1152]{3,2,1,0:T(8,128)(2,1)} %param.5) | copy-start | bytes 1769476
  103.0 12.6 %collective-permute-start.11 = (bf16[72,1152]{1,0:T(8,128)(2,1)S(1)}, bf16[72,1152]{1,0:T(8,128)(2,1)S(1)}, u32[]{:S(2)}, u32[]{:S(2)}) collective-permute-start(bf16[72,1152]{1,0:T(8,128)(2,1)S(1)} %get-tuple-element.71), channel_id=1, source_target_pairs={{0,12},{2,6},{16,28},{18,22},{32,44},{34,38},{48,60},{50,54},{4,8}... | collective-permute-start | bytes 497672 | tf_op jit(solution)/shard_map/ppermute | solution.py:701
  105.5 10.1 %collective-permute-start.12 = (bf16[72,1152]{1,0:T(8,128)(2,1)S(1)}, bf16[72,1152]{1,0:T(8,128)(2,1)S(1)}, u32[]{:S(2)}, u32[]{:S(2)}) collective-permute-start(bf16[72,1152]{1,0:T(8,128)(2,1)S(1)} %get-tuple-element.72), channel_id=1, source_target_pairs={{0,65},{2,66},{16,81},{18,82},{32,97},{34,98},{48,113},{50,114},{4... | collective-permute-start | bytes 497672 | tf_op jit(solution)/shard_map/ppermute | solution.py:701
  106.7 8.9 %collective-permute-start.13 = (bf16[72,1152]{1,0:T(8,128)(2,1)S(1)}, bf16[72,1152]{1,0:T(8,128)(2,1)S(1)}, u32[]{:S(2)}, u32[]{:S(2)}) collective-permute-start(bf16[72,1152]{1,0:T(8,128)(2,1)S(1)} %get-tuple-element.73), channel_id=1, source_target_pairs={{0,77},{2,70},{16,93},{18,86},{32,109},{34,102},{48,125},{50,118},... | collective-permute-start | bytes 497672 | tf_op jit(solution)/shard_map/ppermute | solution.py:701
  115.8 5.8 %collective-permute-start.14 = (bf16[36,1152]{1,0:T(8,128)(2,1)S(1)}, bf16[36,1152]{1,0:T(8,128)(2,1)S(1)}, u32[]{:S(2)}, u32[]{:S(2)}) collective-permute-start(bf16[36,1152]{1,0:T(8,128)(2,1)S(1)} %get-tuple-element.76), channel_id=1, source_target_pairs={{0,48},{2,18},{16,32},{18,2},{32,16},{34,50},{48,0},{50,34},{4,52}... | collective-permute-start | bytes 248840 | tf_op jit(solution)/shard_map/ppermute | solution.py:711
